TPU v7x, 128 devices: a whole 4x4x4 slice. The times are simulated.
128 devices in a mesh: row: 8 (over y_hi, z), col: 16 (over y_lo, x, core).
Axes of the slice: x: 4, y: 4 (y_hi: 2, y_lo: 2; y = y_hi * 2 + y_lo), z: 4, core: 2. Of those that a mesh axis runs over, the one named last changes fastest.
Arguments:
- tensor: bfloat16 [8, 4096, 2048], P('row', 'col'), may hold values from -6 to 6
- density: bfloat16 [2048, 16384], P('row', 'col'), may hold values from -0.125 to 0.125
- tensor_mask: int32 [32, 16], replicated, may hold values 0 or 1
- density_mask: int32 [16, 128], replicated, may hold values 0 or 1
- block_sizes: int32 [128], replicated, may hold values from 64 to 128
Outputs:
- contracted: bfloat16 [8, 4096, 16384], P('row', None, 'col')
All inputs are finite; a program needn't handle non-finite values.
Results may differ from a plain program's by a relative error of at most 0.001.
Values may be sent and summed in bfloat16 or wider, within the bound.
No kernel may reach another device: no remote copies, remote signals or barrier semaphores. Data moves between devices by JAX's collectives and lax.ppermute only.
A program may use at most 256 MiB of HBM per device.

v0:
```python
import jax
import jax.numpy as jnp
from jax import lax
from jax.sharding import PartitionSpec as P

BLK = 128


def passed_along(value, axis, by):
    count = lax.axis_size(axis)
    return lax.ppermute(value, axis, [(i, (i + by) % count) for i in range(count)])


def expand_keep(block_mask, row_live, col_live):
    wide = jnp.repeat(jnp.repeat(block_mask == 1, BLK, 0), BLK, 1)
    return wide & row_live[:, None] & col_live[None, :]


def remap_panels(tensor_kept, row_count, col_count, row_at):
    aux_dev, mu_dev, nu_all = tensor_kept.shape
    panel_width = nu_all // row_count
    panels = tensor_kept.reshape(aux_dev, mu_dev, row_count, panel_width)
    turned = jnp.roll(panels, -row_at, axis=2)
    copies = jnp.concatenate([turned] * (col_count // row_count), axis=2)
    moved = lax.all_to_all(copies, "col", split_axis=2, concat_axis=1, tiled=True)
    return moved.reshape(aux_dev * mu_dev * col_count, panel_width)


def local(tensor, density, tensor_mask, density_mask, block_sizes):
    row_count = lax.axis_size("row")
    col_count = lax.axis_size("col")
    row_at = lax.axis_index("row")
    col_at = lax.axis_index("col")
    aux_dev, mu_dev, nu_all = tensor.shape
    nu_dev, sig_dev = density.shape
    within = jnp.arange(BLK, dtype=jnp.int32)
    slot_live = (within[None, :] < block_sizes[:, None]).reshape(-1)
    mu_live = lax.dynamic_slice_in_dim(slot_live, col_at * mu_dev, mu_dev)
    tensor_rows_mask = lax.dynamic_slice_in_dim(
        tensor_mask, col_at * (mu_dev // BLK), mu_dev // BLK, 0
    )
    tensor_keep = expand_keep(tensor_rows_mask, mu_live, slot_live[:nu_all])
    tensor_kept = jnp.where(tensor_keep[None], tensor, jnp.zeros((), tensor.dtype))
    nu_live = lax.dynamic_slice_in_dim(slot_live, row_at * nu_dev, nu_dev)
    sig_live = lax.dynamic_slice_in_dim(slot_live, col_at * sig_dev, sig_dev)
    density_block = lax.dynamic_slice(
        density_mask,
        (row_at * (nu_dev // BLK), col_at * (sig_dev // BLK)),
        (nu_dev // BLK, sig_dev // BLK),
    )
    density_keep = expand_keep(density_block, nu_live, sig_live)
    density_part = jnp.where(density_keep, density, jnp.zeros((), density.dtype))
    total_rows = aux_dev * mu_dev * col_count
    tensor_panel = remap_panels(tensor_kept, row_count, col_count, row_at)
    col_offset = col_at % row_count
    for bit_no in range((row_count - 1).bit_length()):
        shifted = passed_along(density_part, "row", -(1 << bit_no))
        density_part = jnp.where(col_offset >> bit_no & 1 == 1, shifted, density_part)
    total_sum = jnp.zeros((total_rows, sig_dev), jnp.float32)
    for step_no in range(row_count):
        total_sum = total_sum + jnp.dot(
            tensor_panel, density_part, preferred_element_type=jnp.float32
        )
        if step_no < row_count - 1:
            tensor_panel = passed_along(tensor_panel, "col", -1)
            density_part = passed_along(density_part, "row", -1)
    result = total_sum.reshape(aux_dev, mu_dev * col_count, sig_dev)
    return result.astype(jnp.bfloat16)


def solution(mesh):
    placed = (P("row", "col", None), P("row", "col"), P(), P(), P())
    return jax.shard_map(
        local, mesh=mesh, in_specs=placed, out_specs=P("row", None, "col"), check_vma=False
    )
```

profile of v0, /device:TPU:31, one launch (start us, length us, event | category | flops | bytes accessed | tf_op | source)
XLA Modules:
  0.0 414.0 jit_solution(3823719398691112908)
XLA Ops:
  4.3 30.4 %all_to_all.15 = bf16[1,256,16,256]{1,3,0,2:T(8,128)(2,1)} all-to-all(bf16[1,256,16,256]{1,3,0,2:T(8,128)(2,1)S(1)} %maximum_bitcast_fusion), channel_id=1, replica_groups=mesh['row'=8,'col'=16] {'col'}, dimensions={2} | all-to-all | bytes 4194304 | tf_op jit(solution)/shard_map/all_to_all | solution.py:25
  34.7 2.9 copy.14
  38.1 27.1 %collective-permute-done.3 = bf16[4096,256]{1,0:T(8,128)(2,1)S(1)} collective-permute-done((bf16[4096,256]{1,0:T(8,128)(2,1)S(1)}, bf16[4096,256]{1,0:T(8,128)(2,1)S(1)}, u32[]{:S(2)}, u32[]{:S(2)}) %collective-permute-start.3) | collective-permute-done | bytes 2097184 | tf_op jit(solution)/shard_map/ppermute | solution.py:11
  66.6 27.7 %collective-permute-done.5 = bf16[4096,256]{1,0:T(8,128)(2,1)} collective-permute-done((bf16[4096,256]{1,0:T(8,128)(2,1)S(1)}, bf16[4096,256]{1,0:T(8,128)(2,1)}, u32[]{:S(2)}, u32[]{:S(2)}) %collective-permute-start.5) | collective-permute-done | bytes 2097184 | tf_op jit(solution)/shard_map/ppermute | solution.py:11
  95.7 4.5 %collective-permute-start = (bf16[256,1024]{1,0:T(8,128)(2,1)S(1)}, bf16[256,1024]{1,0:T(8,128)(2,1)}, u32[]{:S(2)}, u32[]{:S(2)}) collective-permute-start(bf16[256,1024]{1,0:T(8,128)(2,1)S(1)} %fusion.5), channel_id=1, source_target_pairs={{0,112},{16,0},{32,16},{48,32},{64,48},{80,64},{96,80},{112,96},{1... | collective-permute-start | bytes 1572872 | tf_op jit(solution)/shard_map/ppermute | solution.py:11
  100.2 31.5 %collective-permute-done = bf16[256,1024]{1,0:T(8,128)(2,1)} collective-permute-done((bf16[256,1024]{1,0:T(8,128)(2,1)S(1)}, bf16[256,1024]{1,0:T(8,128)(2,1)}, u32[]{:S(2)}, u32[]{:S(2)}) %collective-permute-start) | collective-permute-done | bytes 524320 | tf_op jit(solution)/shard_map/ppermute | solution.py:11
  132.9 32.6 %collective-permute-done.1 = bf16[256,1024]{1,0:T(8,128)(2,1)} collective-permute-done((bf16[256,1024]{1,0:T(8,128)(2,1)S(1)}, bf16[256,1024]{1,0:T(8,128)(2,1)}, u32[]{:S(2)}, u32[]{:S(2)}) %collective-permute-start.1) | collective-permute-done | bytes 524320 | tf_op jit(solution)/shard_map/ppermute | solution.py:11
  166.6 2.9 collective-permute-start.2
  169.5 12.2 %collective-permute-done.2 = bf16[256,1024]{1,0:T(8,128)(2,1)S(1)} collective-permute-done((bf16[256,1024]{1,0:T(8,128)(2,1)S(1)}, bf16[256,1024]{1,0:T(8,128)(2,1)S(1)}, u32[]{:S(2)}, u32[]{:S(2)}) %collective-permute-start.2) | collective-permute-done | bytes 524320 | tf_op jit(solution)/shard_map/ppermute | solution.py:11
  181.8 12.2 %collective-permute-start.4 = (bf16[256,1024]{1,0:T(8,128)(2,1)S(1)}, bf16[256,1024]{1,0:T(8,128)(2,1)S(1)}, u32[]{:S(2)}, u32[]{:S(2)}) collective-permute-start(bf16[256,1024]{1,0:T(8,128)(2,1)S(1)} %broadcast_select_fusion.2), channel_id=1, source_target_pairs={{0,112},{16,0},{32,16},{48,32},{64,48},{80,64},{96,80},{112,96},{1... | collective-permute-start | bytes 1572872 | tf_op jit(solution)/shard_map/ppermute | solution.py:11
  194.0 10.4 %collective-permute-done.4 = bf16[256,1024]{1,0:T(8,128)(2,1)S(1)} collective-permute-done((bf16[256,1024]{1,0:T(8,128)(2,1)S(1)}, bf16[256,1024]{1,0:T(8,128)(2,1)S(1)}, u32[]{:S(2)}, u32[]{:S(2)}) %collective-permute-start.4) | collective-permute-done | bytes 524320 | tf_op jit(solution)/shard_map/ppermute | solution.py:11
  204.4 5.8 %collective-permute-start.6 = (bf16[256,1024]{1,0:T(8,128)(2,1)S(1)}, bf16[256,1024]{1,0:T(8,128)(2,1)S(1)}, u32[]{:S(2)}, u32[]{:S(2)}) collective-permute-start(bf16[256,1024]{1,0:T(8,128)(2,1)S(1)} %collective-permute-done.4), channel_id=1, source_target_pairs={{0,112},{16,0},{32,16},{48,32},{64,48},{80,64},{96,80},{112,96},{1... | collective-permute-start | bytes 1572872 | tf_op jit(solution)/shard_map/ppermute | solution.py:11
  210.2 2.0 collective-permute-start.11
  212.2 30.0 %collective-permute-done.6 = bf16[256,1024]{1,0:T(8,128)(2,1)S(1)} collective-permute-done((bf16[256,1024]{1,0:T(8,128)(2,1)S(1)}, bf16[256,1024]{1,0:T(8,128)(2,1)S(1)}, u32[]{:S(2)}, u32[]{:S(2)}) %collective-permute-start.6) | collective-permute-done | bytes 524320 | tf_op jit(solution)/shard_map/ppermute | solution.py:11
  242.2 5.8 %collective-permute-start.8 = (bf16[256,1024]{1,0:T(8,128)(2,1)S(1)}, bf16[256,1024]{1,0:T(8,128)(2,1)S(1)}, u32[]{:S(2)}, u32[]{:S(2)}) collective-permute-start(bf16[256,1024]{1,0:T(8,128)(2,1)S(1)} %collective-permute-done.6), channel_id=1, source_target_pairs={{0,112},{16,0},{32,16},{48,32},{64,48},{80,64},{96,80},{112,96},{1... | collective-permute-start | bytes 1572872 | tf_op jit(solution)/shard_map/ppermute | solution.py:11
  248.0 8.6 %collective-permute-done.8 = bf16[256,1024]{1,0:T(8,128)(2,1)S(1)} collective-permute-done((bf16[256,1024]{1,0:T(8,128)(2,1)S(1)}, bf16[256,1024]{1,0:T(8,128)(2,1)S(1)}, u32[]{:S(2)}, u32[]{:S(2)}) %collective-permute-start.8) | collective-permute-done | bytes 524320 | tf_op jit(solution)/shard_map/ppermute | solution.py:11
  256.6 5.8 %collective-permute-start.10 = (bf16[256,1024]{1,0:T(8,128)(2,1)S(1)}, bf16[256,1024]{1,0:T(8,128)(2,1)S(1)}, u32[]{:S(2)}, u32[]{:S(2)}) collective-permute-start(bf16[256,1024]{1,0:T(8,128)(2,1)S(1)} %collective-permute-done.8), channel_id=1, source_target_pairs={{0,112},{16,0},{32,16},{48,32},{64,48},{80,64},{96,80},{112,96},{1... | collective-permute-start | bytes 1572872 | tf_op jit(solution)/shard_map/ppermute | solution.py:11
  262.4 7.7 %collective-permute-done.10 = bf16[256,1024]{1,0:T(8,128)(2,1)S(1)} collective-permute-done((bf16[256,1024]{1,0:T(8,128)(2,1)S(1)}, bf16[256,1024]{1,0:T(8,128)(2,1)S(1)}, u32[]{:S(2)}, u32[]{:S(2)}) %collective-permute-start.10) | collective-permute-done | bytes 524320 | tf_op jit(solution)/shard_map/ppermute | solution.py:11
  270.1 5.8 %collective-permute-start.12 = (bf16[256,1024]{1,0:T(8,128)(2,1)S(1)}, bf16[256,1024]{1,0:T(8,128)(2,1)S(1)}, u32[]{:S(2)}, u32[]{:S(2)}) collective-permute-start(bf16[256,1024]{1,0:T(8,128)(2,1)S(1)} %collective-permute-done.10), channel_id=1, source_target_pairs={{0,112},{16,0},{32,16},{48,32},{64,48},{80,64},{96,80},{112,96},{1... | collective-permute-start | bytes 1572872 | tf_op jit(solution)/shard_map/ppermute | solution.py:11
  275.9 8.1 %fusion.8 = f32[4096,1024]{1,0:T(8,128)} fusion(bf16[4096,256]{1,0:T(8,128)(2,1)S(1)} %bitcast.51, bf16[256,1024]{1,0:T(8,128)(2,1)S(1)} %broadcast_select_fusion.2), kind=kOutput, calls=%fused_computation.22 | convolution fusion | flops 2147483648 | bytes 19398656 | tf_op jit(solution)/shard_map/dot_general | solution.py:61
  284.0 4.5 %collective-permute-start.14 = (bf16[256,1024]{1,0:T(8,128)(2,1)S(1)}, bf16[256,1024]{1,0:T(8,128)(2,1)S(1)}, u32[]{:S(2)}, u32[]{:S(2)}) collective-permute-start(bf16[256,1024]{1,0:T(8,128)(2,1)S(1)} %collective-permute-done.12), channel_id=1, source_target_pairs={{0,112},{16,0},{32,16},{48,32},{64,48},{80,64},{96,80},{112,96},{1... | collective-permute-start | bytes 1572872 | tf_op jit(solution)/shard_map/ppermute | solution.py:11
  288.5 5.7 %collective-permute-start.13 = (bf16[4096,256]{1,0:T(8,128)(2,1)S(1)}, bf16[4096,256]{1,0:T(8,128)(2,1)S(1)}, u32[]{:S(2)}, u32[]{:S(2)}) collective-permute-start(bf16[4096,256]{1,0:T(8,128)(2,1)S(1)} %collective-permute-done.11), channel_id=1, source_target_pairs={{0,15},{1,0},{2,1},{3,2},{4,3},{5,4},{6,5},{7,6},{8,7},{9,8},{10,9... | collective-permute-start | bytes 6291464 | tf_op jit(solution)/shard_map/ppermute | solution.py:11
  294.2 8.1 %fusion.9 = f32[4096,1024]{1,0:T(8,128)} fusion(bf16[4096,256]{1,0:T(8,128)(2,1)S(1)} %copy-done.1, bf16[256,1024]{1,0:T(8,128)(2,1)S(1)} %collective-permute-done.4), kind=kOutput, calls=%fused_computation.23 | convolution fusion | flops 2147483648 | bytes 19398656 | tf_op jit(solution)/shard_map/dot_general | solution.py:61
  302.2 18.0 %collective-permute-done.14 = bf16[256,1024]{1,0:T(8,128)(2,1)S(1)} collective-permute-done((bf16[256,1024]{1,0:T(8,128)(2,1)S(1)}, bf16[256,1024]{1,0:T(8,128)(2,1)S(1)}, u32[]{:S(2)}, u32[]{:S(2)}) %collective-permute-start.14) | collective-permute-done | bytes 524320 | tf_op jit(solution)/shard_map/ppermute | solution.py:11
  320.2 5.8 %collective-permute-start.16 = (bf16[256,1024]{1,0:T(8,128)(2,1)S(1)}, bf16[256,1024]{1,0:T(8,128)(2,1)S(1)}, u32[]{:S(2)}, u32[]{:S(2)}) collective-permute-start(bf16[256,1024]{1,0:T(8,128)(2,1)S(1)} %collective-permute-done.14), channel_id=1, source_target_pairs={{0,112},{16,0},{32,16},{48,32},{64,48},{80,64},{96,80},{112,96},{1... | collective-permute-start | bytes 1572872 | tf_op jit(solution)/shard_map/ppermute | solution.py:11
  326.0 9.7 %fusion.10 = f32[4096,1024]{1,0:T(8,128)} fusion(bf16[4096,256]{1,0:T(8,128)(2,1)} %collective-permute-done.5, bf16[256,1024]{1,0:T(8,128)(2,1)S(1)} %collective-permute-done.6), kind=kOutput, calls=%fused_computation.24 | convolution fusion | flops 2147483648 | bytes 19398656 | tf_op jit(solution)/shard_map/dot_general | solution.py:61
  335.7 9.7 %fusion.11 = f32[4096,1024]{1,0:T(8,128)} fusion(bf16[4096,256]{1,0:T(8,128)(2,1)} %collective-permute-done.7, bf16[256,1024]{1,0:T(8,128)(2,1)S(1)} %collective-permute-done.8), kind=kOutput, calls=%fused_computation.25 | convolution fusion | flops 2147483648 | bytes 19398656 | tf_op jit(solution)/shard_map/dot_general | solution.py:61
  345.4 3.1 collective-permute-start.15
  348.5 9.7 %fusion.12 = f32[4096,1024]{1,0:T(8,128)} fusion(bf16[4096,256]{1,0:T(8,128)(2,1)} %collective-permute-done.9, bf16[256,1024]{1,0:T(8,128)(2,1)S(1)} %collective-permute-done.10), kind=kOutput, calls=%fused_computation.26 | convolution fusion | flops 2147483648 | bytes 19398656 | tf_op jit(solution)/shard_map/dot_general | solution.py:61
  358.2 8.1 %fusion.13 = f32[4096,1024]{1,0:T(8,128)} fusion(bf16[4096,256]{1,0:T(8,128)(2,1)S(1)} %collective-permute-done.11, bf16[256,1024]{1,0:T(8,128)(2,1)S(1)} %collective-permute-done.12), kind=kOutput, calls=%fused_computation.27 | convolution fusion | flops 2147483648 | bytes 19398656 | tf_op jit(solution)/shard_map/dot_general | solution.py:61
  366.3 8.2 %fusion.14 = f32[4096,1024]{1,0:T(8,128)} fusion(bf16[4096,256]{1,0:T(8,128)(2,1)S(1)} %collective-permute-done.13, bf16[256,1024]{1,0:T(8,128)(2,1)S(1)} %collective-permute-done.14), kind=kOutput, calls=%fused_computation.28 | convolution fusion | flops 2147483648 | bytes 19398656 | tf_op jit(solution)/shard_map/dot_general | solution.py:61
  374.5 39.5 %fusion = bf16[1,4096,1024]{2,1,0:T(8,128)(2,1)} fusion(bf16[4096,256]{1,0:T(8,128)(2,1)S(1)} %collective-permute-done.15, bf16[256,1024]{1,0:T(8,128)(2,1)S(1)} %collective-permute-done.16, f32[4096,1024]{1,0:T(8,128)} %fusion.14, f32[4096,1024]{1,0:T(8,128)} %fusion.13, f32[4096,1024]{1,0:T(8,128)} %fusion.12, f32[4096,1024]{1,0:T(8,128)} %fusion.11, ...), kind=kOutput, calls=%fused_computation.1 | convolution fusion | flops 2181038080 | bytes 128450560 | tf_op jit(solution)/shard_map/dot_general | solution.py:61
  (36 shorter events, 9.9 us)
Async XLA Ops:
  34.7 60.7 %copy-start.2 = (bf16[256,1024]{1,0:T(8,128)(2,1)S(1)}, bf16[256,1024]{1,0:T(8,128)(2,1)}, u32[]{:S(2)}) copy-start(bf16[256,1024]{1,0:T(8,128)(2,1)} %param.6) | copy-start | bytes 1572868
  37.6 27.6 %collective-permute-start.3 = (bf16[4096,256]{1,0:T(8,128)(2,1)S(1)}, bf16[4096,256]{1,0:T(8,128)(2,1)S(1)}, u32[]{:S(2)}, u32[]{:S(2)}) collective-permute-start(bf16[4096,256]{1,0:T(8,128)(2,1)S(1)} %bitcast.50), channel_id=1, source_target_pairs={{0,15},{1,0},{2,1},{3,2},{4,3},{5,4},{6,5},{7,6},{8,7},{9,8},{10,9... | collective-permute-start | bytes 6291464 | tf_op jit(solution)/shard_map/ppermute | solution.py:11
  65.2 1.3 copy-start
  66.6 27.7 %collective-permute-start.5 = (bf16[4096,256]{1,0:T(8,128)(2,1)S(1)}, bf16[4096,256]{1,0:T(8,128)(2,1)}, u32[]{:S(2)}, u32[]{:S(2)}) collective-permute-start(bf16[4096,256]{1,0:T(8,128)(2,1)S(1)} %collective-permute-done.3), channel_id=1, source_target_pairs={{0,15},{1,0},{2,1},{3,2},{4,3},{5,4},{6,5},{7,6},{8,7},{9,8},{10,9... | collective-permute-start | bytes 6291464 | tf_op jit(solution)/shard_map/ppermute | solution.py:11
  94.2 38.6 %collective-permute-start.7 = (bf16[4096,256]{1,0:T(8,128)(2,1)}, bf16[4096,256]{1,0:T(8,128)(2,1)}, u32[]{:S(2)}, u32[]{:S(2)}) collective-permute-start(bf16[4096,256]{1,0:T(8,128)(2,1)} %collective-permute-done.5), channel_id=1, source_target_pairs={{0,15},{1,0},{2,1},{3,2},{4,3},{5,4},{6,5},{7,6},{8,7},{9,8},{10,9... | collective-permute-start | bytes 6291464 | tf_op jit(solution)/shard_map/ppermute | solution.py:11
  95.7 36.0 %collective-permute-start = (bf16[256,1024]{1,0:T(8,128)(2,1)S(1)}, bf16[256,1024]{1,0:T(8,128)(2,1)}, u32[]{:S(2)}, u32[]{:S(2)}) collective-permute-start(bf16[256,1024]{1,0:T(8,128)(2,1)S(1)} %fusion.5), channel_id=1, source_target_pairs={{0,112},{16,0},{32,16},{48,32},{64,48},{80,64},{96,80},{112,96},{1... | collective-permute-start | bytes 1572872 | tf_op jit(solution)/shard_map/ppermute | solution.py:11
  132.8 32.8 %collective-permute-start.1 = (bf16[256,1024]{1,0:T(8,128)(2,1)S(1)}, bf16[256,1024]{1,0:T(8,128)(2,1)}, u32[]{:S(2)}, u32[]{:S(2)}) collective-permute-start(bf16[256,1024]{1,0:T(8,128)(2,1)S(1)} %broadcast_select_fusion), channel_id=1, source_target_pairs={{0,96},{16,112},{32,0},{48,16},{64,32},{80,48},{96,64},{112,80},{1... | collective-permute-start | bytes 1572872 | tf_op jit(solution)/shard_map/ppermute | solution.py:11
  132.9 77.4 %collective-permute-start.9 = (bf16[4096,256]{1,0:T(8,128)(2,1)}, bf16[4096,256]{1,0:T(8,128)(2,1)}, u32[]{:S(2)}, u32[]{:S(2)}) collective-permute-start(bf16[4096,256]{1,0:T(8,128)(2,1)} %collective-permute-done.7), channel_id=1, source_target_pairs={{0,15},{1,0},{2,1},{3,2},{4,3},{5,4},{6,5},{7,6},{8,7},{9,8},{10,9... | collective-permute-start | bytes 6291464 | tf_op jit(solution)/shard_map/ppermute | solution.py:11
  166.6 15.1 %collective-permute-start.2 = (bf16[256,1024]{1,0:T(8,128)(2,1)S(1)}, bf16[256,1024]{1,0:T(8,128)(2,1)S(1)}, u32[]{:S(2)}, u32[]{:S(2)}) collective-permute-start(bf16[256,1024]{1,0:T(8,128)(2,1)S(1)} %broadcast_select_fusion.1), channel_id=1, source_target_pairs={{0,64},{16,80},{32,96},{48,112},{64,0},{80,16},{96,32},{112,48},{1... | collective-permute-start | bytes 1572872 | tf_op jit(solution)/shard_map/ppermute | solution.py:11
  181.8 112.4 %copy-start.1 = (bf16[4096,256]{1,0:T(8,128)(2,1)S(1)}, bf16[4096,256]{1,0:T(8,128)(2,1)}, u32[]{:S(2)}) copy-start(bf16[4096,256]{1,0:T(8,128)(2,1)} %copy-done) | copy-start | bytes 6291460
  181.8 22.6 %collective-permute-start.4 = (bf16[256,1024]{1,0:T(8,128)(2,1)S(1)}, bf16[256,1024]{1,0:T(8,128)(2,1)S(1)}, u32[]{:S(2)}, u32[]{:S(2)}) collective-permute-start(bf16[256,1024]{1,0:T(8,128)(2,1)S(1)} %broadcast_select_fusion.2), channel_id=1, source_target_pairs={{0,112},{16,0},{32,16},{48,32},{64,48},{80,64},{96,80},{112,96},{1... | collective-permute-start | bytes 1572872 | tf_op jit(solution)/shard_map/ppermute | solution.py:11
  204.4 37.8 %collective-permute-start.6 = (bf16[256,1024]{1,0:T(8,128)(2,1)S(1)}, bf16[256,1024]{1,0:T(8,128)(2,1)S(1)}, u32[]{:S(2)}, u32[]{:S(2)}) collective-permute-start(bf16[256,1024]{1,0:T(8,128)(2,1)S(1)} %collective-permute-done.4), channel_id=1, source_target_pairs={{0,112},{16,0},{32,16},{48,32},{64,48},{80,64},{96,80},{112,96},{1... | collective-permute-start | bytes 1572872 | tf_op jit(solution)/shard_map/ppermute | solution.py:11
  210.2 78.2 %collective-permute-start.11 = (bf16[4096,256]{1,0:T(8,128)(2,1)}, bf16[4096,256]{1,0:T(8,128)(2,1)S(1)}, u32[]{:S(2)}, u32[]{:S(2)}) collective-permute-start(bf16[4096,256]{1,0:T(8,128)(2,1)} %collective-permute-done.9), channel_id=1, source_target_pairs={{0,15},{1,0},{2,1},{3,2},{4,3},{5,4},{6,5},{7,6},{8,7},{9,8},{10,9... | collective-permute-start | bytes 6291464 | tf_op jit(solution)/shard_map/ppermute | solution.py:11
  242.2 14.4 %collective-permute-start.8 = (bf16[256,1024]{1,0:T(8,128)(2,1)S(1)}, bf16[256,1024]{1,0:T(8,128)(2,1)S(1)}, u32[]{:S(2)}, u32[]{:S(2)}) collective-permute-start(bf16[256,1024]{1,0:T(8,128)(2,1)S(1)} %collective-permute-done.6), channel_id=1, source_target_pairs={{0,112},{16,0},{32,16},{48,32},{64,48},{80,64},{96,80},{112,96},{1... | collective-permute-start | bytes 1572872 | tf_op jit(solution)/shard_map/ppermute | solution.py:11
  256.6 13.5 %collective-permute-start.10 = (bf16[256,1024]{1,0:T(8,128)(2,1)S(1)}, bf16[256,1024]{1,0:T(8,128)(2,1)S(1)}, u32[]{:S(2)}, u32[]{:S(2)}) collective-permute-start(bf16[256,1024]{1,0:T(8,128)(2,1)S(1)} %collective-permute-done.8), channel_id=1, source_target_pairs={{0,112},{16,0},{32,16},{48,32},{64,48},{80,64},{96,80},{112,96},{1... | collective-permute-start | bytes 1572872 | tf_op jit(solution)/shard_map/ppermute | solution.py:11
  270.1 13.9 %collective-permute-start.12 = (bf16[256,1024]{1,0:T(8,128)(2,1)S(1)}, bf16[256,1024]{1,0:T(8,128)(2,1)S(1)}, u32[]{:S(2)}, u32[]{:S(2)}) collective-permute-start(bf16[256,1024]{1,0:T(8,128)(2,1)S(1)} %collective-permute-done.10), channel_id=1, source_target_pairs={{0,112},{16,0},{32,16},{48,32},{64,48},{80,64},{96,80},{112,96},{1... | collective-permute-start | bytes 1572872 | tf_op jit(solution)/shard_map/ppermute | solution.py:11
  284.0 36.2 %collective-permute-start.14 = (bf16[256,1024]{1,0:T(8,128)(2,1)S(1)}, bf16[256,1024]{1,0:T(8,128)(2,1)S(1)}, u32[]{:S(2)}, u32[]{:S(2)}) collective-permute-start(bf16[256,1024]{1,0:T(8,128)(2,1)S(1)} %collective-permute-done.12), channel_id=1, source_target_pairs={{0,112},{16,0},{32,16},{48,32},{64,48},{80,64},{96,80},{112,96},{1... | collective-permute-start | bytes 1572872 | tf_op jit(solution)/shard_map/ppermute | solution.py:11
  288.5 56.9 %collective-permute-start.13 = (bf16[4096,256]{1,0:T(8,128)(2,1)S(1)}, bf16[4096,256]{1,0:T(8,128)(2,1)S(1)}, u32[]{:S(2)}, u32[]{:S(2)}) collective-permute-start(bf16[4096,256]{1,0:T(8,128)(2,1)S(1)} %collective-permute-done.11), channel_id=1, source_target_pairs={{0,15},{1,0},{2,1},{3,2},{4,3},{5,4},{6,5},{7,6},{8,7},{9,8},{10,9... | collective-permute-start | bytes 6291464 | tf_op jit(solution)/shard_map/ppermute | solution.py:11
  320.2 54.2 %collective-permute-start.16 = (bf16[256,1024]{1,0:T(8,128)(2,1)S(1)}, bf16[256,1024]{1,0:T(8,128)(2,1)S(1)}, u32[]{:S(2)}, u32[]{:S(2)}) collective-permute-start(bf16[256,1024]{1,0:T(8,128)(2,1)S(1)} %collective-permute-done.14), channel_id=1, source_target_pairs={{0,112},{16,0},{32,16},{48,32},{64,48},{80,64},{96,80},{112,96},{1... | collective-permute-start | bytes 1572872 | tf_op jit(solution)/shard_map/ppermute | solution.py:11
  345.4 29.1 %collective-permute-start.15 = (bf16[4096,256]{1,0:T(8,128)(2,1)S(1)}, bf16[4096,256]{1,0:T(8,128)(2,1)S(1)}, u32[]{:S(2)}, u32[]{:S(2)}) collective-permute-start(bf16[4096,256]{1,0:T(8,128)(2,1)S(1)} %collective-permute-done.13), channel_id=1, source_target_pairs={{0,15},{1,0},{2,1},{3,2},{4,3},{5,4},{6,5},{7,6},{8,7},{9,8},{10,9... | collective-permute-start | bytes 6291464 | tf_op jit(solution)/shard_map/ppermute | solution.py:11
where the time goes:
time: 414 us
  waiting for transfers between devices  206 us (50%)
  matrix products  101 us (24%)
  starting transfers between devices  64.6 us (16%)
  blocking collectives  30.4 us (7%)
  local copies, waits for them, and re-layouts  6.25 us (2%)
  other arithmetic  5.91 us (1%)
    ppermute x17, waiting for transfers between devices, passed_along(): lax.ppermute(value, axis, [(i, (i + by) % count) for i in range(count)])  206 us
    dot_general x8, matrix products, local(): jnp.dot(tensor_panel, density_part, preferred_element_type=jnp.float32)  101 us
    ppermute x17, starting transfers between devices, passed_along(): lax.ppermute(value, axis, [(i, (i + by) % count) for i in range(count)])  64.6 us
    all_to_all x1, blocking collectives, remap_panels(): lax.all_to_all(copies, 'col', split_axis=2, concat_axis=1, tiled=True)  30.4 us
  transfers between devices with their start and end apart: 17, of which 10 were waited for; matrix products, arithmetic and copies ran while one was open for 16% of the time, Pallas kernels for 0%

commit v1 on v0

v1 whole, which is shorter than its diff:
```python
import functools

import jax
import jax.numpy as jnp
from jax import lax
from jax.experimental import pallas as pl
from jax.experimental.pallas import tpu as pltpu
from jax.sharding import Mesh, PartitionSpec as P

BLK = 128
ROW = ("yh", "z")
COL = ("yl", "x", "c")
MIB = 1024 * 1024
VMEM = pl.BlockSpec(memory_space=pltpu.VMEM)
SMEM = pl.BlockSpec(memory_space=pltpu.SMEM)
ANY = pl.BlockSpec(memory_space=pl.ANY)
HBM = pl.BlockSpec(memory_space=pltpu.HBM)
ROUND = pl.CostEstimate(flops=3 * 10**10, bytes_accessed=0, transcendentals=0)


def after(value, *earlier):
    return lax.optimization_barrier((value, *earlier))[0]


def passed(value, axis):
    n = lax.axis_size(axis)
    pairs = [(i * 2 + c, ((i + 1 - 2 * c) % n) * 2 + c) for i in range(n) for c in range(2)]
    return lax.ppermute(value, (axis, "c"), pairs)


def swapped(value, axis):
    return lax.ppermute(value, axis, [(0, 1), (1, 0)])


def offset_of(sizes_ref, count):
    return lax.fori_loop(0, count, lambda i, s: s + sizes_ref[i], jnp.int32(0))


def at_row():
    return lax.axis_index("yh") * lax.axis_size("z") + lax.axis_index("z")


def at_col():
    nx, nc = lax.axis_size("x"), lax.axis_size("c")
    return (lax.axis_index("yl") * nx + lax.axis_index("x")) * nc + lax.axis_index("c")


def wrapped(value, n):
    return lax.rem(value + n, n)


def chunk_place(dy, d, dc):
    nx = lax.axis_size("x")
    c = wrapped(lax.axis_index("c") + dc, 2)
    x = wrapped(lax.axis_index("x") - (1 - 2 * c) * d, nx)
    return (wrapped(lax.axis_index("yl") + dy, 2) * nx + x) * 2 + c


def panel_place(dy, d):
    nz = lax.axis_size("z")
    z = wrapped(lax.axis_index("z") - (1 - 2 * lax.axis_index("c")) * d, nz)
    return wrapped(lax.axis_index("yh") + dy, 2) * nz + z


def start_body(sizes_hbm, t_mask_hbm, d_mask_hbm, tensor_hbm, density_hbm, own_ref, rho_ref,
               sizes_ref, t_mask_ref, d_mask_ref, tensor_ref, density_ref, sem):
    copies = [
        pltpu.make_async_copy(src, dst, sem.at[i])
        for i, (src, dst) in enumerate([
            (sizes_hbm, sizes_ref), (t_mask_hbm, t_mask_ref), (d_mask_hbm, d_mask_ref),
            (density_hbm, density_ref), (tensor_hbm.at[0], tensor_ref),
        ])
    ]
    for copy in copies:
        copy.start()
    row_at, col_at = at_row(), at_col()
    wide = own_ref.shape[1]
    slot = lax.broadcasted_iota(jnp.int32, (BLK, 2 * BLK), 0)
    target = lax.broadcasted_iota(jnp.int32, (BLK, 2 * BLK), 1)
    row = lax.broadcasted_iota(jnp.int32, (BLK, BLK), 0)
    col = lax.broadcasted_iota(jnp.int32, (BLK, BLK), 1)
    own_ref[...] = jnp.zeros_like(own_ref)
    for copy in copies[:4]:
        copy.wait()
    rows, cols = rho_ref.shape
    for i in range(rows // BLK):
        nu = row_at * (rows // BLK) + i
        for j in range(cols // BLK):
            sig = col_at * (cols // BLK) + j
            live = jnp.where(d_mask_ref[nu, sig] == 1, sizes_ref[nu], 0)
            at = (pl.ds(i * BLK, BLK), pl.ds(j * BLK, BLK))
            part = density_ref[at].astype(jnp.float32)
            keep = (row < live) & (col < sizes_ref[sig])
            rho_ref[at] = jnp.where(keep, part, 0.0).astype(rho_ref.dtype)
    copies[4].wait()
    blocks = own_ref.shape[0] // BLK
    offset = jnp.int32(0)
    for n in range(tensor_ref.shape[1] // BLK):
        size = sizes_ref[n]
        start = jnp.minimum(offset // BLK * BLK, wide - 2 * BLK)
        start = pl.multiple_of(start, BLK)
        pick = (target == slot + (offset - start)) & (slot < size)
        pick = pick.astype(jnp.float32).astype(jnp.bfloat16)
        for m in range(blocks):
            mu = col_at * blocks + m
            live = jnp.where(t_mask_ref[n, mu] == 1, sizes_ref[mu], 0)
            at = pl.ds(m * BLK, BLK)
            part = tensor_ref[at, n * BLK : (n + 1) * BLK].astype(jnp.float32)
            part = jnp.where(row < live, part, 0.0).astype(jnp.bfloat16)
            moved = jnp.dot(part, pick, preferred_element_type=jnp.float32)
            own_ref[at, pl.ds(start, 2 * BLK)] += moved.astype(jnp.bfloat16)
        offset = offset + size


def start(sizes, t_mask, d_mask, tensor, density, wide):
    _, rows, nu = tensor.shape
    return pl.pallas_call(
        start_body,
        in_specs=[HBM] * 5,
        out_specs=[VMEM] * 2,
        out_shape=[
            jax.ShapeDtypeStruct((rows, wide), tensor.dtype),
            jax.ShapeDtypeStruct(density.shape, density.dtype),
        ],
        scratch_shapes=[
            pltpu.SMEM(sizes.shape, jnp.int32),
            pltpu.SMEM(t_mask.shape[::-1], jnp.int32),
            pltpu.SMEM(d_mask.shape, jnp.int32),
            pltpu.VMEM((rows, nu), tensor.dtype),
            pltpu.VMEM(density.shape, density.dtype),
            pltpu.SemaphoreType.DMA((5,)),
        ],
        compiler_params=pltpu.CompilerParams(vmem_limit_bytes=60 * MIB),
        cost_estimate=ROUND,
    )(sizes, t_mask.T, d_mask, tensor, density)


def gather_body(origins, first, sizes_hbm, *refs):
    panels = len(origins)
    out_ref, sizes_ref, sem = refs[panels + (0 if first else 1) :]
    copy = pltpu.make_async_copy(sizes_hbm, sizes_ref, sem)
    copy.start()
    rows = refs[0].shape[0]
    wide = out_ref.shape[0]
    window = rows + 16
    target = lax.broadcasted_iota(jnp.int32, (window, rows), 0)
    slot = lax.broadcasted_iota(jnp.int32, (window, rows), 1)
    if first:
        out_ref[...] = jnp.zeros_like(out_ref)
    per = rows // BLK
    copy.wait()
    for k, origin in enumerate(origins):
        at = panel_place(*origin) * per
        offset = offset_of(sizes_ref, at)
        start = pl.multiple_of(jnp.minimum(offset // 16 * 16, wide - window), 16)
        base = offset - start
        pick = jnp.zeros((window, rows), jnp.bool_)
        for b in range(per):
            size = sizes_ref[at + b]
            inside = (slot >= b * BLK) & (slot < b * BLK + size)
            pick = pick | (inside & (target == slot - b * BLK + base))
            base = base + size
        pick = pick.astype(jnp.float32).astype(jnp.bfloat16)
        moved = jnp.dot(pick, refs[k][...], preferred_element_type=jnp.float32)
        out_ref[pl.ds(start, window), :] += moved.astype(out_ref.dtype)


def gather(sizes, panels, wide, out):
    cols = panels[0][1].shape[1]
    first = out is None
    return pl.pallas_call(
        functools.partial(gather_body, [o for o, _ in panels], first),
        in_specs=[HBM] + [VMEM] * (len(panels) + (0 if first else 1)),
        out_specs=VMEM,
        out_shape=jax.ShapeDtypeStruct((wide, cols), jnp.bfloat16),
        scratch_shapes=[pltpu.SMEM(sizes.shape, jnp.int32), pltpu.SemaphoreType.DMA],
        input_output_aliases={} if first else {1 + len(panels): 0},
        compiler_params=pltpu.CompilerParams(vmem_limit_bytes=8 * MIB),
        cost_estimate=ROUND,
    )(sizes, *[p for _, p in panels], *([] if first else [out]))


def product_body(origins, split, first, rho_ref, *refs):
    count = len(origins)
    a_refs = refs[: sum(split)]
    out_ref, o_buf, o_sem = refs[sum(split) + (0 if first else 1) :]
    tall = o_buf.shape[1]

    def out_copy(i):
        start = pl.multiple_of(chunk_place(*origins[i]) * tall, tall)
        return pltpu.make_async_copy(
            o_buf.at[i % 2], out_ref.at[pl.ds(start, tall)], o_sem.at[i % 2]
        )

    k = 0
    for i, parts in enumerate(split):
        if i >= 2:
            out_copy(i - 2).wait()
        rows = [a_refs[k + part][...] for part in range(parts)]
        k += parts
        rows = rows[0] if parts == 1 else jnp.concatenate(rows, axis=0)
        o_buf[i % 2] = jnp.dot(
            rows, rho_ref[...], preferred_element_type=jnp.float32
        ).astype(o_buf.dtype)
        out_copy(i).start()
    for i in range(max(count - 2, 0), count):
        out_copy(i).wait()


def product(rho, chunks, out, shape):
    split = [len(parts) for _, parts in chunks]
    flat = [p for _, parts in chunks for p in parts]
    tall, wide = sum(p.shape[0] for p in chunks[0][1]), rho.shape[0]
    count, first = len(chunks), out is None
    return pl.pallas_call(
        functools.partial(product_body, [o for o, _ in chunks], split, first),
        in_specs=[VMEM] * (1 + len(flat)) + ([] if first else [ANY]),
        out_specs=ANY,
        scratch_shapes=[
            pltpu.VMEM((2, tall, shape[1]), jnp.bfloat16),
            pltpu.SemaphoreType.DMA((2,)),
        ],
        out_shape=jax.ShapeDtypeStruct(shape, jnp.bfloat16),
        input_output_aliases={} if first else {1 + len(flat): 0},
        compiler_params=pltpu.CompilerParams(vmem_limit_bytes=8 * MIB),
        cost_estimate=pl.CostEstimate(
            flops=2 * count * tall * wide * shape[1],
            bytes_accessed=2 * count * tall * shape[1],
            transcendentals=0,
        ),
    )(rho, *flat, *([] if first else [out]))


def contract(wide, out, tensor, density, tensor_mask, density_mask, block_sizes):
    nz, nx = lax.axis_size("z"), lax.axis_size("x")
    own, rho = start(block_sizes, tensor_mask, density_mask, tensor, density, wide)
    r1, c_own = passed(own, "x"), swapped(own, "c")
    t0, s1 = swapped(rho, "yh"), passed(rho, "z")

    def add(panels, out, *earlier):
        return gather(after(block_sizes, *earlier), panels, wide, out)

    rho_all = add([((0, 0), rho)], None, own)
    s2 = passed(after(s1, rho_all), "z")
    t1, y0 = passed(after(t0, rho_all), "z"), swapped(after(own, t0, rho_all), "yl")
    r2, c_r1 = passed(after(r1, rho_all), "x"), swapped(after(r1, c_own), "c")
    rho_all = add([((0, 1), s1), ((1, 0), t0)], rho_all, r1)
    s3, t2, r3 = passed(after(s2, rho_all), "z"), passed(after(t1, rho_all), "z"), passed(after(r2, rho_all), "x")
    c_r2 = swapped(after(r2, c_r1), "c")
    rho_all = add([((0, 2), s2), ((1, 1), t1)], rho_all, r2, c_r1)
    t3 = passed(after(t2, rho_all), "z")
    q1, q2 = passed(after(y0, r3, rho_all), "x"), swapped(after(r2, y0, rho_all), "yl")
    c_y0, c_r3 = swapped(after(y0, c_r2), "c"), swapped(after(r3, s3), "c")
    rho_all = add([((0, 3), s3), ((1, 2), t2)], rho_all, r3, y0, c_r2)
    rho_all = add([((1, 3), t3)], rho_all)
    shape = (own.shape[0] * 2 * nx * 2, density.shape[1])
    out = product(rho_all, [
        ((0, 0, 0), (own,)), ((0, 1, 0), (r1,)), ((0, 2, 0), (r2,)), ((1, 0, 0), (y0,)),
        ((0, 3, 0), (r3,)), ((0, 0, 1), (c_own,)), ((0, 1, 1), (c_r1,)), ((0, 2, 1), (c_r2,)),
    ], out, shape)
    q1 = after(q1, out)
    q3 = passed(after(q2, q1), "x")
    c_q1 = swapped(after(q1, c_r3), "c")
    c_q2 = swapped(after(q2, c_y0), "c")
    out = product(rho_all, [
        ((1, 0, 1), (c_y0,)), ((0, 3, 1), (c_r3,)), ((1, 1, 0), (q1,)), ((1, 1, 1), (c_q1,)),
        ((1, 2, 0), (q2,)), ((1, 2, 1), (c_q2,)),
    ], out, shape)
    q3 = after(q3, out)
    c_q3 = swapped(q3, "c")
    out = product(rho_all, [((1, 3, 0), (q3,))], out, shape)
    out = product(rho_all, [((1, 3, 1), (c_q3,))], out, shape)
    return out, q1


def local(*args):
    nu, sizes = args[0].shape[2], args[4]
    narrow = nu * 13 // 16
    out, late = contract(narrow, None, *args)
    more = jnp.sum(after(sizes, late)[: nu // BLK]) > narrow

    def again(carry):
        return jnp.bool_(False), contract(nu, carry[1], *args)[0]

    return lax.while_loop(lambda carry: carry[0], again, (more, out))[1][None]


def solution(mesh):
    rows, cols = mesh.devices.shape
    nz, nx, nc = rows // 2, cols // 4, 2
    fine = Mesh(mesh.devices.reshape(2, nz, 2, nx, nc), ("yh", "z", "yl", "x", "c"))
    placed = (P(ROW, COL, None), P(ROW, COL), P(), P(), P())
    return jax.shard_map(
        local, mesh=fine, in_specs=placed, out_specs=P(ROW, None, COL), check_vma=False
    )
```

time: 414 us -> 92 us (0.22)
  the two profiles are of different devices: /device:TPU:31 before, /device:TPU:1 now
where the time goes in v1:
time: 92 us; the launch traced here: 91.7 us
  starting transfers between devices  39.3 us (43%)
  Pallas kernels  31.4 us (34%)
  waiting for transfers between devices  16.6 us (18%)
  local copies, waits for them, and re-layouts  2.4 us (3%)
  between operations  1.06 us (1%)
    ppermute x11, starting transfers between devices, passed(): return lax.ppermute(value, (axis, 'c'), pairs)  28.1 us
    pallas_call x4, Pallas kernels, product(): pl.pallas_call(functools.partial(product_body, [o for o, _ in chunks], sp...  22.4 us
    ppermute x11, waiting for transfers between devices, passed(): return lax.ppermute(value, (axis, 'c'), pairs)  12.1 us
    ppermute x11, starting transfers between devices, swapped(): return lax.ppermute(value, axis, [(0, 1), (1, 0)])  11.3 us
    pallas_call x5, Pallas kernels, gather(): pl.pallas_call(functools.partial(gather_body, [o for o, _ in panels], fir...  5.93 us
    ppermute x11, waiting for transfers between devices, swapped(): return lax.ppermute(value, axis, [(0, 1), (1, 0)])  4.52 us
    pallas_call x1, Pallas kernels, start(): pl.pallas_call(start_body, in_specs=[HBM] * 5, out_specs=[VMEM] * 2, out_...  3.11 us
    unnamed x14, local copies, waits for them, and re-layouts  2.4 us
  transfers between devices with their start and end apart: 22, of which 10 were waited for; matrix products, arithmetic and copies ran while one was open for 1% of the time, Pallas kernels for 27%

profile of v1, /device:TPU:1, one launch (start us, length us, event | category | flops | bytes accessed | tf_op | source)
XLA Modules:
  0.0 91.7 jit_solution(702738478379222077)
XLA Ops:
  0.0 3.1 %shard_map.55 = (bf16[256,1664]{1,0:T(8,128)(2,1)}, bf16[256,1024]{1,0:T(8,128)(2,1)}) custom-call(s32[128]{0:T(128)} %sizes_hbm.6, s32[16,32]{1,0:T(8,128)} %bitcast.5, s32[16,128]{1,0:T(8,128)} %d_mask_hbm.1, bf16[1,256,2048]{2,1,0:T(8,128)(2,1)} %tensor_hbm.1, bf16[256,1024]{1,0:T(8,128)(2,1)} %density_hbm.1), custom_call_target="tpu_custom_call" | custom-call | flops 30000001024 | tf_op jit(solution)/shard_map/pallas_call | solution.py:117
  3.1 3.8 %collective-permute-start.22 = (bf16[256,1024]{1,0:T(8,128)(2,1)}, bf16[256,1024]{1,0:T(8,128)(2,1)S(1)}, u32[]{:S(2)}, u32[]{:S(2)}) collective-permute-start(bf16[256,1024]{1,0:T(8,128)(2,1)} %get-tuple-element.93.refs_0_), channel_id=1, source_target_pairs={{0,64},{64,0},{1,65},{65,1},{2,66},{66,2},{3,67},{67,3},{4,68},{68... | collective-permute-start | bytes 1572872 | tf_op jit(solution)/shard_map/ppermute | solution.py:32
  6.9 3.8 %collective-permute-start.26 = (bf16[256,1024]{1,0:T(8,128)(2,1)}, bf16[256,1024]{1,0:T(8,128)(2,1)S(1)}, u32[]{:S(2)}, u32[]{:S(2)}) collective-permute-start(bf16[256,1024]{1,0:T(8,128)(2,1)} %get-tuple-element.93.refs_0_), channel_id=1, source_target_pairs={{0,16},{1,49},{16,32},{17,1},{32,48},{33,17},{48,0},{49,33},{2,18}... | collective-permute-start | bytes 1572872 | tf_op jit(solution)/shard_map/ppermute | solution.py:28
  10.7 2.5 %collective-permute-start.24 = (bf16[256,1664]{1,0:T(8,128)(2,1)}, bf16[256,1664]{1,0:T(8,128)(2,1)S(1)}, u32[]{:S(2)}, u32[]{:S(2)}) collective-permute-start(bf16[256,1664]{1,0:T(8,128)(2,1)} %get-tuple-element.95.refs_0_), channel_id=1, source_target_pairs={{0,2},{1,7},{2,4},{3,1},{4,6},{5,3},{6,0},{7,5},{8,10},{9,15},{10,... | collective-permute-start | bytes 2555912 | tf_op jit(solution)/shard_map/ppermute | solution.py:28
  13.2 1.0 %copy-done.4 = bf16[256,1024]{1,0:T(8,128)(2,1)S(1)} copy-done((bf16[256,1024]{1,0:T(8,128)(2,1)S(1)}, bf16[256,1024]{1,0:T(8,128)(2,1)}, u32[]{:S(2)}) %copy-start.4) | copy-done | bytes 524312
  14.2 0.9 shard_map.56.refs_2_
  15.1 3.4 %collective-permute-done.22.refs_1_ = bf16[256,1024]{1,0:T(8,128)(2,1)S(1)} collective-permute-done((bf16[256,1024]{1,0:T(8,128)(2,1)}, bf16[256,1024]{1,0:T(8,128)(2,1)S(1)}, u32[]{:S(2)}, u32[]{:S(2)}) %collective-permute-start.22) | collective-permute-done | bytes 524320 | tf_op jit(solution)/shard_map/ppermute | solution.py:32
  18.5 3.8 %collective-permute-start.30 = (bf16[256,1024]{1,0:T(8,128)(2,1)S(1)}, bf16[256,1024]{1,0:T(8,128)(2,1)S(1)}, u32[]{:S(2)}, u32[]{:S(2)}) collective-permute-start(bf16[256,1024]{1,0:T(8,128)(2,1)S(1)} %collective-permute-done.26.refs_0_), channel_id=1, source_target_pairs={{0,16},{1,49},{16,32},{17,1},{32,48},{33,17},{48,0},{49,33},{2,18}... | collective-permute-start | bytes 1572872 | tf_op jit(solution)/shard_map/ppermute | solution.py:28
  22.4 0.7 collective-permute-done.24.refs_1_
  23.1 3.0 %collective-permute-start.25 = (bf16[256,1664]{1,0:T(8,128)(2,1)S(1)}, bf16[256,1664]{1,0:T(8,128)(2,1)S(1)}, u32[]{:S(2)}, u32[]{:S(2)}) collective-permute-start(bf16[256,1664]{1,0:T(8,128)(2,1)S(1)} %collective-permute-done.24.refs_1_), channel_id=1, source_target_pairs={{0,2},{1,7},{2,4},{3,1},{4,6},{5,3},{6,0},{7,5},{8,10},{9,15},{10,... | collective-permute-start | bytes 2555912 | tf_op jit(solution)/shard_map/ppermute | solution.py:28
  26.1 1.2 %shard_map.57.refs_2_ = bf16[1664,1024]{1,0:T(8,128)(2,1)S(1)} custom-call(s32[128]{0:T(128)S(1)} %copy-done.14, bf16[256,1024]{1,0:T(8,128)(2,1)S(1)} %collective-permute-done.26.refs_0_, bf16[256,1024]{1,0:T(8,128)(2,1)S(1)} %collective-permute-done.22.refs_1_, bf16[1664,1024]{1,0:T(8,128)(2,1)S(1)} %shard_map.56.refs_2_), custom_call_target="tpu_custom_call", output_to_operand_aliasing={{}: (3, {})} | custom-call | flops 30000001024 | tf_op jit(solution)/shard_map/pallas_call | solution.py:171
  28.4 5.6 %collective-permute-done.31.refs_1_ = bf16[256,1024]{1,0:T(8,128)(2,1)S(1)} collective-permute-done((bf16[256,1024]{1,0:T(8,128)(2,1)S(1)}, bf16[256,1024]{1,0:T(8,128)(2,1)S(1)}, u32[]{:S(2)}, u32[]{:S(2)}) %collective-permute-start.31) | collective-permute-done | bytes 524320 | tf_op jit(solution)/shard_map/ppermute | solution.py:28
  34.0 3.4 %collective-permute-start.33 = (bf16[256,1024]{1,0:T(8,128)(2,1)S(1)}, bf16[256,1024]{1,0:T(8,128)(2,1)S(1)}, u32[]{:S(2)}, u32[]{:S(2)}) collective-permute-start(bf16[256,1024]{1,0:T(8,128)(2,1)S(1)} %collective-permute-done.31.refs_1_), channel_id=1, source_target_pairs={{0,16},{1,49},{16,32},{17,1},{32,48},{33,17},{48,0},{49,33},{2,18}... | collective-permute-start | bytes 1572872 | tf_op jit(solution)/shard_map/ppermute | solution.py:28
  37.5 2.2 %collective-permute-start.27 = (bf16[256,1664]{1,0:T(8,128)(2,1)S(1)}, bf16[256,1664]{1,0:T(8,128)(2,1)S(1)}, u32[]{:S(2)}, u32[]{:S(2)}) collective-permute-start(bf16[256,1664]{1,0:T(8,128)(2,1)S(1)} %collective-permute-done.25.refs_2_), channel_id=1, source_target_pairs={{0,2},{1,7},{2,4},{3,1},{4,6},{5,3},{6,0},{7,5},{8,10},{9,15},{10,... | collective-permute-start | bytes 2555912 | tf_op jit(solution)/shard_map/ppermute | solution.py:28
  40.2 1.3 %shard_map.58.refs_2_ = bf16[1664,1024]{1,0:T(8,128)(2,1)S(1)} custom-call(s32[128]{0:T(128)S(1)} %copy-done.14, bf16[256,1024]{1,0:T(8,128)(2,1)S(1)} %collective-permute-done.30.refs_0_, bf16[256,1024]{1,0:T(8,128)(2,1)S(1)} %collective-permute-done.31.refs_1_, bf16[1664,1024]{1,0:T(8,128)(2,1)S(1)} %shard_map.57.refs_2_), custom_call_target="tpu_custom_call", output_to_operand_aliasing={{}: (3, {})} | custom-call | flops 30000001024 | tf_op jit(solution)/shard_map/pallas_call | solution.py:171
  41.5 2.1 %collective-permute-done.33.refs_1_ = bf16[256,1024]{1,0:T(8,128)(2,1)S(1)} collective-permute-done((bf16[256,1024]{1,0:T(8,128)(2,1)S(1)}, bf16[256,1024]{1,0:T(8,128)(2,1)S(1)}, u32[]{:S(2)}, u32[]{:S(2)}) %collective-permute-start.33) | collective-permute-done | bytes 524320 | tf_op jit(solution)/shard_map/ppermute | solution.py:28
  43.6 3.4 %collective-permute-start.34 = (bf16[256,1024]{1,0:T(8,128)(2,1)S(1)}, bf16[256,1024]{1,0:T(8,128)(2,1)S(1)}, u32[]{:S(2)}, u32[]{:S(2)}) collective-permute-start(bf16[256,1024]{1,0:T(8,128)(2,1)S(1)} %collective-permute-done.33.refs_1_), channel_id=1, source_target_pairs={{0,16},{1,49},{16,32},{17,1},{32,48},{33,17},{48,0},{49,33},{2,18}... | collective-permute-start | bytes 1572872 | tf_op jit(solution)/shard_map/ppermute | solution.py:28
  47.5 0.8 collective-permute-start.37
  48.3 1.0 %collective-permute-done.27.refs_4_ = bf16[256,1664]{1,0:T(8,128)(2,1)S(1)} collective-permute-done((bf16[256,1664]{1,0:T(8,128)(2,1)S(1)}, bf16[256,1664]{1,0:T(8,128)(2,1)S(1)}, u32[]{:S(2)}, u32[]{:S(2)}) %collective-permute-start.27) | collective-permute-done | bytes 852000 | tf_op jit(solution)/shard_map/ppermute | solution.py:28
  49.3 3.4 %collective-permute-start.32 = (bf16[256,1664]{1,0:T(8,128)(2,1)S(1)}, bf16[256,1664]{1,0:T(8,128)(2,1)S(1)}, u32[]{:S(2)}, u32[]{:S(2)}) collective-permute-start(bf16[256,1664]{1,0:T(8,128)(2,1)S(1)} %collective-permute-done.23.refs_3_), channel_id=1, source_target_pairs={{0,2},{1,7},{2,4},{3,1},{4,6},{5,3},{6,0},{7,5},{8,10},{9,15},{10,... | collective-permute-start | bytes 2555912 | tf_op jit(solution)/shard_map/ppermute | solution.py:28
  52.9 1.3 %shard_map.59.refs_1_ = bf16[1664,1024]{1,0:T(8,128)(2,1)S(1)} custom-call(s32[128]{0:T(128)S(1)} %copy-done.14, bf16[256,1024]{1,0:T(8,128)(2,1)S(1)} %collective-permute-done.36.refs_0_, bf16[256,1024]{1,0:T(8,128)(2,1)S(1)} %collective-permute-done.33.refs_1_, bf16[1664,1024]{1,0:T(8,128)(2,1)S(1)} %shard_map.58.refs_2_), custom_call_target="tpu_custom_call", output_to_operand_aliasing={{}: (3, {})} | custom-call | flops 30000001024 | tf_op jit(solution)/shard_map/pallas_call | solution.py:171
  54.8 1.2 %shard_map.60.rho_ref = bf16[1664,1024]{1,0:T(8,128)(2,1)S(1)} custom-call(s32[128]{0:T(128)S(1)} %copy-done.14, bf16[256,1024]{1,0:T(8,128)(2,1)S(1)} %collective-permute-done.34.refs_0_, bf16[1664,1024]{1,0:T(8,128)(2,1)S(1)} %shard_map.59.refs_1_), custom_call_target="tpu_custom_call", output_to_operand_aliasing={{}: (2, {})} | custom-call | flops 30000001024 | tf_op jit(solution)/shard_map/pallas_call | solution.py:171
  56.1 9.2 %shard_map.61.refs_6_ = bf16[4096,1024]{1,0:T(8,128)(2,1)S(1)} custom-call(bf16[1664,1024]{1,0:T(8,128)(2,1)S(1)} %shard_map.60.rho_ref, bf16[256,1664]{1,0:T(8,128)(2,1)S(1)} %copy-done.3, bf16[256,1664]{1,0:T(8,128)(2,1)S(1)} %collective-permute-done.24.refs_1_, bf16[256,1664]{1,0:T(8,128)(2,1)S(1)} %collective-permute-done.25.refs_2_, ...), custom_call_target="tpu_custom_call" | custom-call | flops 6979321856 | bytes 4194304 | tf_op jit(solution)/shard_map/pallas_call | solution.py:215
  65.3 3.8 %collective-permute-start.41 = (bf16[256,1664]{1,0:T(8,128)(2,1)S(1)}, bf16[256,1664]{1,0:T(8,128)(2,1)S(1)}, u32[]{:S(2)}, u32[]{:S(2)}) collective-permute-start(bf16[256,1664]{1,0:T(8,128)(2,1)S(1)} %collective-permute-done.32.refs_2_), channel_id=1, source_target_pairs={{0,1},{1,0},{2,3},{3,2},{4,5},{5,4},{6,7},{7,6},{8,9},{9,8},{10,11... | collective-permute-start | bytes 2555912 | tf_op jit(solution)/shard_map/ppermute | solution.py:32
  69.2 2.5 %collective-permute-start.38 = (bf16[256,1664]{1,0:T(8,128)(2,1)S(1)}, bf16[256,1664]{1,0:T(8,128)(2,1)}, u32[]{:S(2)}, u32[]{:S(2)}) collective-permute-start(bf16[256,1664]{1,0:T(8,128)(2,1)S(1)} %collective-permute-done.37.refs_4_), channel_id=1, source_target_pairs={{0,2},{1,7},{2,4},{3,1},{4,6},{5,3},{6,0},{7,5},{8,10},{9,15},{10,... | collective-permute-start | bytes 2555912 | tf_op jit(solution)/shard_map/ppermute | solution.py:28
  72.3 6.9 %shard_map.62.refs_1_ = bf16[4096,1024]{1,0:T(8,128)(2,1)S(1)} custom-call(bf16[1664,1024]{1,0:T(8,128)(2,1)S(1)} %shard_map.60.rho_ref, bf16[256,1664]{1,0:T(8,128)(2,1)S(1)} %collective-permute-done.39.refs_0_, bf16[256,1664]{1,0:T(8,128)(2,1)S(1)} %collective-permute-done.40.refs_1_, ...), custom_call_target="tpu_custom_call", output_to_operand_aliasing={{}: (7, {})} | custom-call | flops 5234491392 | bytes 3145728 | tf_op jit(solution)/shard_map/pallas_call | solution.py:215
  79.3 2.1 %collective-permute-done.38.refs_0_ = bf16[256,1664]{1,0:T(8,128)(2,1)} collective-permute-done((bf16[256,1664]{1,0:T(8,128)(2,1)S(1)}, bf16[256,1664]{1,0:T(8,128)(2,1)}, u32[]{:S(2)}, u32[]{:S(2)}) %collective-permute-start.38) | collective-permute-done | bytes 852000 | tf_op jit(solution)/shard_map/ppermute | solution.py:28
  81.3 1.3 %copy-done.6 = bf16[4096,1024]{1,0:T(8,128)(2,1)} copy-done((bf16[4096,1024]{1,0:T(8,128)(2,1)}, bf16[4096,1024]{1,0:T(8,128)(2,1)S(1)}, u32[]{:S(2)}) %copy-start.6) | copy-done | bytes 8388632
  82.7 1.0 %collective-permute-start.43 = (bf16[256,1664]{1,0:T(8,128)(2,1)}, bf16[256,1664]{1,0:T(8,128)(2,1)}, u32[]{:S(2)}, u32[]{:S(2)}) collective-permute-start(bf16[256,1664]{1,0:T(8,128)(2,1)} %collective-permute-done.38.refs_0_), channel_id=1, source_target_pairs={{0,1},{1,0},{2,3},{3,2},{4,5},{5,4},{6,7},{7,6},{8,9},{9,8},{10,11... | collective-permute-start | bytes 2555912 | tf_op jit(solution)/shard_map/ppermute | solution.py:32
  83.6 0.7 slice_reduce_fusion
  85.0 3.1 %shard_map.63.refs_1_ = bf16[4096,1024]{1,0:T(8,128)(2,1)} custom-call(bf16[1664,1024]{1,0:T(8,128)(2,1)S(1)} %shard_map.60.rho_ref, bf16[256,1664]{1,0:T(8,128)(2,1)} %collective-permute-done.38.refs_0_, bf16[4096,1024]{1,0:T(8,128)(2,1)} %copy-done.6), custom_call_target="tpu_custom_call", output_to_operand_aliasing={{}: (2, {})} | custom-call | flops 872415232 | bytes 524288 | tf_op jit(solution)/shard_map/pallas_call | solution.py:215
  88.1 3.1 %shard_map.64 = bf16[4096,1024]{1,0:T(8,128)(2,1)} custom-call(bf16[1664,1024]{1,0:T(8,128)(2,1)S(1)} %shard_map.60.rho_ref, bf16[256,1664]{1,0:T(8,128)(2,1)} %collective-permute-done.43.refs_0_, bf16[4096,1024]{1,0:T(8,128)(2,1)} %shard_map.63.refs_1_), custom_call_target="tpu_custom_call", output_to_operand_aliasing={{}: (2, {})} | custom-call | flops 872415232 | bytes 524288 | tf_op jit(solution)/shard_map/pallas_call | solution.py:215
  (38 shorter events, 4.0 us)
Async XLA Ops:
  0.0 13.2 %copy-start.14 = (s32[128]{0:T(128)S(1)}, s32[128]{0:T(128)}, u32[]{:S(2)}) copy-start(s32[128]{0:T(128)} %sizes_hbm.6) | copy-start | bytes 1540
  3.1 15.4 %collective-permute-start.22 = (bf16[256,1024]{1,0:T(8,128)(2,1)}, bf16[256,1024]{1,0:T(8,128)(2,1)S(1)}, u32[]{:S(2)}, u32[]{:S(2)}) collective-permute-start(bf16[256,1024]{1,0:T(8,128)(2,1)} %get-tuple-element.93.refs_0_), channel_id=1, source_target_pairs={{0,64},{64,0},{1,65},{65,1},{2,66},{66,2},{3,67},{67,3},{4,68},{68... | collective-permute-start | bytes 1572872 | tf_op jit(solution)/shard_map/ppermute | solution.py:32
  6.9 11.6 %collective-permute-start.26 = (bf16[256,1024]{1,0:T(8,128)(2,1)}, bf16[256,1024]{1,0:T(8,128)(2,1)S(1)}, u32[]{:S(2)}, u32[]{:S(2)}) collective-permute-start(bf16[256,1024]{1,0:T(8,128)(2,1)} %get-tuple-element.93.refs_0_), channel_id=1, source_target_pairs={{0,16},{1,49},{16,32},{17,1},{32,48},{33,17},{48,0},{49,33},{2,18}... | collective-permute-start | bytes 1572872 | tf_op jit(solution)/shard_map/ppermute | solution.py:28
  10.7 12.4 %collective-permute-start.24 = (bf16[256,1664]{1,0:T(8,128)(2,1)}, bf16[256,1664]{1,0:T(8,128)(2,1)S(1)}, u32[]{:S(2)}, u32[]{:S(2)}) collective-permute-start(bf16[256,1664]{1,0:T(8,128)(2,1)} %get-tuple-element.95.refs_0_), channel_id=1, source_target_pairs={{0,2},{1,7},{2,4},{3,1},{4,6},{5,3},{6,0},{7,5},{8,10},{9,15},{10,... | collective-permute-start | bytes 2555912 | tf_op jit(solution)/shard_map/ppermute | solution.py:28
  13.2 13.0 %collective-permute-start.28 = (bf16[256,1664]{1,0:T(8,128)(2,1)}, bf16[256,1664]{1,0:T(8,128)(2,1)S(1)}, u32[]{:S(2)}, u32[]{:S(2)}) collective-permute-start(bf16[256,1664]{1,0:T(8,128)(2,1)} %get-tuple-element.95.refs_0_), channel_id=1, source_target_pairs={{0,1},{1,0},{2,3},{3,2},{4,5},{5,4},{6,7},{7,6},{8,9},{9,8},{10,11... | collective-permute-start | bytes 2555912 | tf_op jit(solution)/shard_map/ppermute | solution.py:32
  13.2 1.0 %copy-start.4 = (bf16[256,1024]{1,0:T(8,128)(2,1)S(1)}, bf16[256,1024]{1,0:T(8,128)(2,1)}, u32[]{:S(2)}) copy-start(bf16[256,1024]{1,0:T(8,128)(2,1)} %get-tuple-element.93.refs_0_) | copy-start | bytes 1572868
  15.1 12.3 %copy-start.3 = (bf16[256,1664]{1,0:T(8,128)(2,1)S(1)}, bf16[256,1664]{1,0:T(8,128)(2,1)}, u32[]{:S(2)}) copy-start(bf16[256,1664]{1,0:T(8,128)(2,1)} %get-tuple-element.95.refs_0_) | copy-start | bytes 2555908
  18.5 9.9 %collective-permute-start.30 = (bf16[256,1024]{1,0:T(8,128)(2,1)S(1)}, bf16[256,1024]{1,0:T(8,128)(2,1)S(1)}, u32[]{:S(2)}, u32[]{:S(2)}) collective-permute-start(bf16[256,1024]{1,0:T(8,128)(2,1)S(1)} %collective-permute-done.26.refs_0_), channel_id=1, source_target_pairs={{0,16},{1,49},{16,32},{17,1},{32,48},{33,17},{48,0},{49,33},{2,18}... | collective-permute-start | bytes 1572872 | tf_op jit(solution)/shard_map/ppermute | solution.py:28
  22.3 11.7 %collective-permute-start.31 = (bf16[256,1024]{1,0:T(8,128)(2,1)S(1)}, bf16[256,1024]{1,0:T(8,128)(2,1)S(1)}, u32[]{:S(2)}, u32[]{:S(2)}) collective-permute-start(bf16[256,1024]{1,0:T(8,128)(2,1)S(1)} %collective-permute-done.22.refs_1_), channel_id=1, source_target_pairs={{0,16},{1,49},{16,32},{17,1},{32,48},{33,17},{48,0},{49,33},{2,18}... | collective-permute-start | bytes 1572872 | tf_op jit(solution)/shard_map/ppermute | solution.py:28
  23.1 14.4 %collective-permute-start.25 = (bf16[256,1664]{1,0:T(8,128)(2,1)S(1)}, bf16[256,1664]{1,0:T(8,128)(2,1)S(1)}, u32[]{:S(2)}, u32[]{:S(2)}) collective-permute-start(bf16[256,1664]{1,0:T(8,128)(2,1)S(1)} %collective-permute-done.24.refs_1_), channel_id=1, source_target_pairs={{0,2},{1,7},{2,4},{3,1},{4,6},{5,3},{6,0},{7,5},{8,10},{9,15},{10,... | collective-permute-start | bytes 2555912 | tf_op jit(solution)/shard_map/ppermute | solution.py:28
  26.1 13.5 %collective-permute-start.29 = (bf16[256,1664]{1,0:T(8,128)(2,1)S(1)}, bf16[256,1664]{1,0:T(8,128)(2,1)S(1)}, u32[]{:S(2)}, u32[]{:S(2)}) collective-permute-start(bf16[256,1664]{1,0:T(8,128)(2,1)S(1)} %collective-permute-done.24.refs_1_), channel_id=1, source_target_pairs={{0,1},{1,0},{2,3},{3,2},{4,5},{5,4},{6,7},{7,6},{8,9},{9,8},{10,11... | collective-permute-start | bytes 2555912 | tf_op jit(solution)/shard_map/ppermute | solution.py:32
  27.4 20.1 %collective-permute-start.23 = (bf16[256,1664]{1,0:T(8,128)(2,1)S(1)}, bf16[256,1664]{1,0:T(8,128)(2,1)S(1)}, u32[]{:S(2)}, u32[]{:S(2)}) collective-permute-start(bf16[256,1664]{1,0:T(8,128)(2,1)S(1)} %copy-done.3), channel_id=1, source_target_pairs={{0,8},{8,0},{1,9},{9,1},{2,10},{10,2},{3,11},{11,3},{4,12},{12,4},... | collective-permute-start | bytes 2555912 | tf_op jit(solution)/shard_map/ppermute | solution.py:32
  34.0 9.5 %collective-permute-start.33 = (bf16[256,1024]{1,0:T(8,128)(2,1)S(1)}, bf16[256,1024]{1,0:T(8,128)(2,1)S(1)}, u32[]{:S(2)}, u32[]{:S(2)}) collective-permute-start(bf16[256,1024]{1,0:T(8,128)(2,1)S(1)} %collective-permute-done.31.refs_1_), channel_id=1, source_target_pairs={{0,16},{1,49},{16,32},{17,1},{32,48},{33,17},{48,0},{49,33},{2,18}... | collective-permute-start | bytes 1572872 | tf_op jit(solution)/shard_map/ppermute | solution.py:28
  37.4 15.5 %collective-permute-start.36 = (bf16[256,1024]{1,0:T(8,128)(2,1)S(1)}, bf16[256,1024]{1,0:T(8,128)(2,1)S(1)}, u32[]{:S(2)}, u32[]{:S(2)}) collective-permute-start(bf16[256,1024]{1,0:T(8,128)(2,1)S(1)} %collective-permute-done.30.refs_0_), channel_id=1, source_target_pairs={{0,16},{1,49},{16,32},{17,1},{32,48},{33,17},{48,0},{49,33},{2,18}... | collective-permute-start | bytes 1572872 | tf_op jit(solution)/shard_map/ppermute | solution.py:28
  37.5 11.8 %collective-permute-start.27 = (bf16[256,1664]{1,0:T(8,128)(2,1)S(1)}, bf16[256,1664]{1,0:T(8,128)(2,1)S(1)}, u32[]{:S(2)}, u32[]{:S(2)}) collective-permute-start(bf16[256,1664]{1,0:T(8,128)(2,1)S(1)} %collective-permute-done.25.refs_2_), channel_id=1, source_target_pairs={{0,2},{1,7},{2,4},{3,1},{4,6},{5,3},{6,0},{7,5},{8,10},{9,15},{10,... | collective-permute-start | bytes 2555912 | tf_op jit(solution)/shard_map/ppermute | solution.py:28
  39.7 13.0 %collective-permute-start.35 = (bf16[256,1664]{1,0:T(8,128)(2,1)S(1)}, bf16[256,1664]{1,0:T(8,128)(2,1)S(1)}, u32[]{:S(2)}, u32[]{:S(2)}) collective-permute-start(bf16[256,1664]{1,0:T(8,128)(2,1)S(1)} %collective-permute-done.25.refs_2_), channel_id=1, source_target_pairs={{0,1},{1,0},{2,3},{3,2},{4,5},{5,4},{6,7},{7,6},{8,9},{9,8},{10,11... | collective-permute-start | bytes 2555912 | tf_op jit(solution)/shard_map/ppermute | solution.py:32
  43.6 11.2 %collective-permute-start.34 = (bf16[256,1024]{1,0:T(8,128)(2,1)S(1)}, bf16[256,1024]{1,0:T(8,128)(2,1)S(1)}, u32[]{:S(2)}, u32[]{:S(2)}) collective-permute-start(bf16[256,1024]{1,0:T(8,128)(2,1)S(1)} %collective-permute-done.33.refs_1_), channel_id=1, source_target_pairs={{0,16},{1,49},{16,32},{17,1},{32,48},{33,17},{48,0},{49,33},{2,18}... | collective-permute-start | bytes 1572872 | tf_op jit(solution)/shard_map/ppermute | solution.py:28
  47.5 21.6 %collective-permute-start.37 = (bf16[256,1664]{1,0:T(8,128)(2,1)S(1)}, bf16[256,1664]{1,0:T(8,128)(2,1)S(1)}, u32[]{:S(2)}, u32[]{:S(2)}) collective-permute-start(bf16[256,1664]{1,0:T(8,128)(2,1)S(1)} %collective-permute-done.25.refs_2_), channel_id=1, source_target_pairs={{0,8},{8,0},{1,9},{9,1},{2,10},{10,2},{3,11},{11,3},{4,12},{12,4},... | collective-permute-start | bytes 2555912 | tf_op jit(solution)/shard_map/ppermute | solution.py:32
  49.3 16.0 %collective-permute-start.32 = (bf16[256,1664]{1,0:T(8,128)(2,1)S(1)}, bf16[256,1664]{1,0:T(8,128)(2,1)S(1)}, u32[]{:S(2)}, u32[]{:S(2)}) collective-permute-start(bf16[256,1664]{1,0:T(8,128)(2,1)S(1)} %collective-permute-done.23.refs_3_), channel_id=1, source_target_pairs={{0,2},{1,7},{2,4},{3,1},{4,6},{5,3},{6,0},{7,5},{8,10},{9,15},{10,... | collective-permute-start | bytes 2555912 | tf_op jit(solution)/shard_map/ppermute | solution.py:28
  52.7 16.4 %collective-permute-start.39 = (bf16[256,1664]{1,0:T(8,128)(2,1)S(1)}, bf16[256,1664]{1,0:T(8,128)(2,1)S(1)}, u32[]{:S(2)}, u32[]{:S(2)}) collective-permute-start(bf16[256,1664]{1,0:T(8,128)(2,1)S(1)} %collective-permute-done.23.refs_3_), channel_id=1, source_target_pairs={{0,1},{1,0},{2,3},{3,2},{4,5},{5,4},{6,7},{7,6},{8,9},{9,8},{10,11... | collective-permute-start | bytes 2555912 | tf_op jit(solution)/shard_map/ppermute | solution.py:32
  54.2 11.1 %collective-permute-start.40 = (bf16[256,1664]{1,0:T(8,128)(2,1)S(1)}, bf16[256,1664]{1,0:T(8,128)(2,1)S(1)}, u32[]{:S(2)}, u32[]{:S(2)}) collective-permute-start(bf16[256,1664]{1,0:T(8,128)(2,1)S(1)} %collective-permute-done.27.refs_4_), channel_id=1, source_target_pairs={{0,1},{1,0},{2,3},{3,2},{4,5},{5,4},{6,7},{7,6},{8,9},{9,8},{10,11... | collective-permute-start | bytes 2555912 | tf_op jit(solution)/shard_map/ppermute | solution.py:32
  65.3 6.4 %collective-permute-start.41 = (bf16[256,1664]{1,0:T(8,128)(2,1)S(1)}, bf16[256,1664]{1,0:T(8,128)(2,1)S(1)}, u32[]{:S(2)}, u32[]{:S(2)}) collective-permute-start(bf16[256,1664]{1,0:T(8,128)(2,1)S(1)} %collective-permute-done.32.refs_2_), channel_id=1, source_target_pairs={{0,1},{1,0},{2,3},{3,2},{4,5},{5,4},{6,7},{7,6},{8,9},{9,8},{10,11... | collective-permute-start | bytes 2555912 | tf_op jit(solution)/shard_map/ppermute | solution.py:32
  69.1 3.2 %collective-permute-start.42 = (bf16[256,1664]{1,0:T(8,128)(2,1)S(1)}, bf16[256,1664]{1,0:T(8,128)(2,1)S(1)}, u32[]{:S(2)}, u32[]{:S(2)}) collective-permute-start(bf16[256,1664]{1,0:T(8,128)(2,1)S(1)} %collective-permute-done.37.refs_4_), channel_id=1, source_target_pairs={{0,1},{1,0},{2,3},{3,2},{4,5},{5,4},{6,7},{7,6},{8,9},{9,8},{10,11... | collective-permute-start | bytes 2555912 | tf_op jit(solution)/shard_map/ppermute | solution.py:32
  69.2 12.1 %collective-permute-start.38 = (bf16[256,1664]{1,0:T(8,128)(2,1)S(1)}, bf16[256,1664]{1,0:T(8,128)(2,1)}, u32[]{:S(2)}, u32[]{:S(2)}) collective-permute-start(bf16[256,1664]{1,0:T(8,128)(2,1)S(1)} %collective-permute-done.37.refs_4_), channel_id=1, source_target_pairs={{0,2},{1,7},{2,4},{3,1},{4,6},{5,3},{6,0},{7,5},{8,10},{9,15},{10,... | collective-permute-start | bytes 2555912 | tf_op jit(solution)/shard_map/ppermute | solution.py:28
  79.3 3.4 %copy-start.6 = (bf16[4096,1024]{1,0:T(8,128)(2,1)}, bf16[4096,1024]{1,0:T(8,128)(2,1)S(1)}, u32[]{:S(2)}) copy-start(bf16[4096,1024]{1,0:T(8,128)(2,1)S(1)} %shard_map.62.refs_1_) | copy-start | bytes 25165828
  82.7 5.5 %collective-permute-start.43 = (bf16[256,1664]{1,0:T(8,128)(2,1)}, bf16[256,1664]{1,0:T(8,128)(2,1)}, u32[]{:S(2)}, u32[]{:S(2)}) collective-permute-start(bf16[256,1664]{1,0:T(8,128)(2,1)} %collective-permute-done.38.refs_0_), channel_id=1, source_target_pairs={{0,1},{1,0},{2,3},{3,2},{4,5},{5,4},{6,7},{7,6},{8,9},{9,8},{10,11... | collective-permute-start | bytes 2555912 | tf_op jit(solution)/shard_map/ppermute | solution.py:32
  88.1 3.2 %copy-start.8 = (bf16[256,1024]{1,0:T(8,128)(2,1)S(1)}, bf16[256,1024]{1,0:T(8,128)(2,1)}, u32[]{:S(2)}) copy-start(bf16[256,1024]{1,0:T(8,128)(2,1)} %density_hbm.1) | copy-start | bytes 1572868
  88.1 3.2 %copy-start.10 = (s32[32,16]{0,1:T(8,128)S(1)}, s32[32,16]{0,1:T(8,128)}, u32[]{:S(2)}) copy-start(s32[32,16]{0,1:T(8,128)} %param.9) | copy-start | bytes 6148
  88.1 3.2 %copy-start.12 = (s32[16,128]{1,0:T(8,128)S(1)}, s32[16,128]{1,0:T(8,128)}, u32[]{:S(2)}) copy-start(s32[16,128]{1,0:T(8,128)} %d_mask_hbm.1) | copy-start | bytes 24580

commit v2 on v1

--- a/solution.py
+++ b/solution.py
@@ -15,7 +15,7 @@
 SMEM = pl.BlockSpec(memory_space=pltpu.SMEM)
 ANY = pl.BlockSpec(memory_space=pl.ANY)
 HBM = pl.BlockSpec(memory_space=pltpu.HBM)
-ROUND = pl.CostEstimate(flops=3 * 10**10, bytes_accessed=0, transcendentals=0)
+ROUND = pl.CostEstimate(flops=5 * 10**9, bytes_accessed=0, transcendentals=0)
 
 
 def after(value, *earlier):
@@ -49,11 +49,10 @@
     return lax.rem(value + n, n)
 
 
-def chunk_place(dy, d, dc):
-    nx = lax.axis_size("x")
-    c = wrapped(lax.axis_index("c") + dc, 2)
-    x = wrapped(lax.axis_index("x") - (1 - 2 * c) * d, nx)
-    return (wrapped(lax.axis_index("yl") + dy, 2) * nx + x) * 2 + c
+def chunk_place(dy, dx, dc):
+    nx, c = lax.axis_size("x"), lax.axis_index("c")
+    x = wrapped(lax.axis_index("x") - (1 - 2 * c) * dx, nx)
+    return (wrapped(lax.axis_index("yl") + dy, 2) * nx + x) * 2 + wrapped(c + dc, 2)
 
 
 def panel_place(dy, d):
@@ -63,7 +62,7 @@
 
 
 def start_body(sizes_hbm, t_mask_hbm, d_mask_hbm, tensor_hbm, density_hbm, own_ref, rho_ref,
-               sizes_ref, t_mask_ref, d_mask_ref, tensor_ref, density_ref, sem):
+               live_ref, sizes_ref, t_mask_ref, d_mask_ref, tensor_ref, density_ref, sem):
     copies = [
         pltpu.make_async_copy(src, dst, sem.at[i])
         for i, (src, dst) in enumerate([
@@ -110,6 +109,7 @@
             moved = jnp.dot(part, pick, preferred_element_type=jnp.float32)
             own_ref[at, pl.ds(start, 2 * BLK)] += moved.astype(jnp.bfloat16)
         offset = offset + size
+    live_ref[...] = jnp.full_like(live_ref, offset)
 
 
 def start(sizes, t_mask, d_mask, tensor, density, wide):
@@ -117,10 +117,11 @@
     return pl.pallas_call(
         start_body,
         in_specs=[HBM] * 5,
-        out_specs=[VMEM] * 2,
+        out_specs=[VMEM] * 3,
         out_shape=[
             jax.ShapeDtypeStruct((rows, wide), tensor.dtype),
             jax.ShapeDtypeStruct(density.shape, density.dtype),
+            jax.ShapeDtypeStruct((8, BLK), jnp.int32),
         ],
         scratch_shapes=[
             pltpu.SMEM(sizes.shape, jnp.int32),
@@ -130,7 +131,7 @@
             pltpu.VMEM(density.shape, density.dtype),
             pltpu.SemaphoreType.DMA((5,)),
         ],
-        compiler_params=pltpu.CompilerParams(vmem_limit_bytes=60 * MIB),
+        compiler_params=pltpu.CompilerParams(vmem_limit_bytes=48 * MIB),
         cost_estimate=ROUND,
     )(sizes, t_mask.T, d_mask, tensor, density)
 
@@ -180,10 +181,10 @@
     )(sizes, *[p for _, p in panels], *([] if first else [out]))
 
 
-def product_body(origins, split, first, rho_ref, *refs):
+def product_body(origins, split, first, live_ref, rho_ref, *refs):
     count = len(origins)
     a_refs = refs[: sum(split)]
-    out_ref, o_buf, o_sem = refs[sum(split) + (0 if first else 1) :]
+    out_ref, token_ref, o_buf, o_sem = refs[sum(split) + (0 if first else 1) :]
     tall = o_buf.shape[1]
 
     def out_copy(i):
@@ -205,79 +206,83 @@
         out_copy(i).start()
     for i in range(max(count - 2, 0), count):
         out_copy(i).wait()
-
-
-def product(rho, chunks, out, shape):
+    token_ref[...] = live_ref[...]
+
+
+def product(live, rho, chunks, out, shape):
     split = [len(parts) for _, parts in chunks]
     flat = [p for _, parts in chunks for p in parts]
     tall, wide = sum(p.shape[0] for p in chunks[0][1]), rho.shape[0]
     count, first = len(chunks), out is None
     return pl.pallas_call(
         functools.partial(product_body, [o for o, _ in chunks], split, first),
-        in_specs=[VMEM] * (1 + len(flat)) + ([] if first else [ANY]),
-        out_specs=ANY,
+        in_specs=[VMEM] * (2 + len(flat)) + ([] if first else [ANY]),
+        out_specs=[ANY, VMEM],
         scratch_shapes=[
             pltpu.VMEM((2, tall, shape[1]), jnp.bfloat16),
             pltpu.SemaphoreType.DMA((2,)),
         ],
-        out_shape=jax.ShapeDtypeStruct(shape, jnp.bfloat16),
-        input_output_aliases={} if first else {1 + len(flat): 0},
+        out_shape=[
+            jax.ShapeDtypeStruct(shape, jnp.bfloat16),
+            jax.ShapeDtypeStruct(live.shape, live.dtype),
+        ],
+        input_output_aliases={} if first else {2 + len(flat): 0},
         compiler_params=pltpu.CompilerParams(vmem_limit_bytes=8 * MIB),
         cost_estimate=pl.CostEstimate(
             flops=2 * count * tall * wide * shape[1],
             bytes_accessed=2 * count * tall * shape[1],
             transcendentals=0,
         ),
-    )(rho, *flat, *([] if first else [out]))
+    )(live, rho, *flat, *([] if first else [out]))
 
 
 def contract(wide, out, tensor, density, tensor_mask, density_mask, block_sizes):
     nz, nx = lax.axis_size("z"), lax.axis_size("x")
-    own, rho = start(block_sizes, tensor_mask, density_mask, tensor, density, wide)
-    r1, c_own = passed(own, "x"), swapped(own, "c")
-    t0, s1 = swapped(rho, "yh"), passed(rho, "z")
+    own, rho, live = start(block_sizes, tensor_mask, density_mask, tensor, density, wide)
 
     def add(panels, out, *earlier):
         return gather(after(block_sizes, *earlier), panels, wide, out)
 
-    rho_all = add([((0, 0), rho)], None, own)
-    s2 = passed(after(s1, rho_all), "z")
-    t1, y0 = passed(after(t0, rho_all), "z"), swapped(after(own, t0, rho_all), "yl")
-    r2, c_r1 = passed(after(r1, rho_all), "x"), swapped(after(r1, c_own), "c")
-    rho_all = add([((0, 1), s1), ((1, 0), t0)], rho_all, r1)
-    s3, t2, r3 = passed(after(s2, rho_all), "z"), passed(after(t1, rho_all), "z"), passed(after(r2, rho_all), "x")
-    c_r2 = swapped(after(r2, c_r1), "c")
-    rho_all = add([((0, 2), s2), ((1, 1), t1)], rho_all, r2, c_r1)
-    t3 = passed(after(t2, rho_all), "z")
-    q1, q2 = passed(after(y0, r3, rho_all), "x"), swapped(after(r2, y0, rho_all), "yl")
-    c_y0, c_r3 = swapped(after(y0, c_r2), "c"), swapped(after(r3, s3), "c")
-    rho_all = add([((0, 3), s3), ((1, 2), t2)], rho_all, r3, y0, c_r2)
-    rho_all = add([((1, 3), t3)], rho_all)
-    shape = (own.shape[0] * 2 * nx * 2, density.shape[1])
-    out = product(rho_all, [
-        ((0, 0, 0), (own,)), ((0, 1, 0), (r1,)), ((0, 2, 0), (r2,)), ((1, 0, 0), (y0,)),
-        ((0, 3, 0), (r3,)), ((0, 0, 1), (c_own,)), ((0, 1, 1), (c_r1,)), ((0, 2, 1), (c_r2,)),
+    a1, c_own = passed(own, "x"), swapped(own, "c")
+    s1, t0 = passed(rho, "z"), swapped(rho, "yh")
+    y0 = swapped(own, "yl")
+    g = add([((0, 0), rho)], None, own)
+    b1, a2 = passed(after(c_own, g), "x"), passed(after(a1, g), "x")
+    s2, t1 = passed(after(s1, g), "z"), passed(after(t0, g), "z")
+    g = add([((0, 1), s1), ((1, 0), t0)], g, c_own, a1)
+    s3, t2 = passed(after(s2, g), "z"), passed(after(t1, g), "z")
+    c_a1 = swapped(after(a1, b1, g), "c")
+    g = add([((0, 2), s2), ((1, 1), t1)], g, b1)
+    qa, q2 = passed(after(y0, g), "x"), swapped(after(a2, y0, g), "yl")
+    c_y0 = swapped(after(y0, s3, g), "c")
+    c_b1 = swapped(after(b1, c_a1, g), "c")
+    t3 = passed(after(t2, g), "z")
+    g = add([((0, 3), s3), ((1, 2), t2)], g, y0, a2, c_a1)
+    qb = passed(after(c_y0, g), "x")
+    c_a2 = swapped(after(a2, c_b1, g), "c")
+    c_qa = swapped(after(qa, c_y0, g), "c")
+    g = add([((1, 3), t3)], g, c_b1, c_y0, qa)
+    shape = (own.shape[0] * 4 * nx, density.shape[1])
+    out, live = product(live, g, [
+        ((0, 0, 0), (own,)), ((0, 0, 1), (c_own,)), ((0, 1, 0), (a1,)), ((0, 1, 1), (b1,)),
+        ((1, 0, 0), (y0,)), ((1, 0, 1), (c_y0,)), ((0, 2, 0), (a2,)), ((0, -1, 1), (c_a1,)),
     ], out, shape)
-    q1 = after(q1, out)
-    q3 = passed(after(q2, q1), "x")
-    c_q1 = swapped(after(q1, c_r3), "c")
-    c_q2 = swapped(after(q2, c_y0), "c")
-    out = product(rho_all, [
-        ((1, 0, 1), (c_y0,)), ((0, 3, 1), (c_r3,)), ((1, 1, 0), (q1,)), ((1, 1, 1), (c_q1,)),
-        ((1, 2, 0), (q2,)), ((1, 2, 1), (c_q2,)),
+    c_q2 = swapped(after(q2, live), "c")
+    c_qb = swapped(after(qb, live), "c")
+    out, live = product(live, g, [
+        ((0, -1, 0), (c_b1,)), ((0, 2, 1), (c_a2,)), ((1, 1, 0), (qa,)), ((1, -1, 1), (c_qa,)),
     ], out, shape)
-    q3 = after(q3, out)
-    c_q3 = swapped(q3, "c")
-    out = product(rho_all, [((1, 3, 0), (q3,))], out, shape)
-    out = product(rho_all, [((1, 3, 1), (c_q3,))], out, shape)
-    return out, q1
+    out, live = product(live, g, [
+        ((1, 2, 0), (q2,)), ((1, 2, 1), (c_q2,)), ((1, 1, 1), (qb,)), ((1, -1, 0), (c_qb,)),
+    ], out, shape)
+    return out, live
 
 
 def local(*args):
-    nu, sizes = args[0].shape[2], args[4]
-    narrow = nu * 13 // 16
-    out, late = contract(narrow, None, *args)
-    more = jnp.sum(after(sizes, late)[: nu // BLK]) > narrow
+    nu = args[0].shape[2]
+    narrow = nu * 7 // 8
+    out, live = contract(narrow, None, *args)
+    more = live[0, 0] > narrow
 
     def again(carry):
         return jnp.bool_(False), contract(nu, carry[1], *args)[0]

time: 92 us -> 85.4 us (0.928)
  Pallas kernels: 31.4 us -> 28.4 us
  local copies, waits for them, and re-layouts: 2.4 us -> 0.54 us
  starting transfers between devices: 39.3 us -> 37.7 us
    ppermute x11, starting transfers between devices: 28.1 us -> 25.6 us  [passed(): return lax.ppermute(value, (axis, 'c'), pairs)]
    unnamed x14 -> x10, local copies, waits for them, and re-layouts: 2.4 us -> 0.03 us
    ppermute x11, waiting for transfers between devices: 4.52 us -> 6.81 us  [swapped(): return lax.ppermute(value, axis, [(0, 1), (1, 0)])]
    pallas_call x4 -> x3, Pallas kernels: 22.4 us -> 20.3 us  [product(): pl.pallas_call(functools.partial(product_body, [o for o, _ in chunks], sp...]
    ppermute x11, waiting for transfers between devices: 12.1 us -> 10.6 us  [passed(): return lax.ppermute(value, (axis, 'c'), pairs)]
    ppermute x11, starting transfers between devices: 11.3 us -> 12.2 us  [swapped(): return lax.ppermute(value, axis, [(0, 1), (1, 0)])]
  transfers between devices with their start and end apart: 22 -> 22, of which waited for: 10 -> 7; matrix products, arithmetic and copies ran while one was open for 1% -> 0% of each run, Pallas kernels for 27% -> 25%
where the time goes in v2:
time: 85.4 us; the launch traced here: 85.2 us
  starting transfers between devices  37.7 us (44%)
  Pallas kernels  28.4 us (33%)
  waiting for transfers between devices  17.4 us (20%)
  between operations  0.95 us (1%)
    ppermute x11, starting transfers between devices, passed(): return lax.ppermute(value, (axis, 'c'), pairs)  25.6 us
    pallas_call x3, Pallas kernels, product(): pl.pallas_call(functools.partial(product_body, [o for o, _ in chunks], sp...  20.3 us
    ppermute x11, starting transfers between devices, swapped(): return lax.ppermute(value, axis, [(0, 1), (1, 0)])  12.2 us
    ppermute x11, waiting for transfers between devices, passed(): return lax.ppermute(value, (axis, 'c'), pairs)  10.6 us
    ppermute x11, waiting for transfers between devices, swapped(): return lax.ppermute(value, axis, [(0, 1), (1, 0)])  6.81 us
    pallas_call x5, Pallas kernels, gather(): pl.pallas_call(functools.partial(gather_body, [o for o, _ in panels], fir...  5.93 us
    pallas_call x1, Pallas kernels, start(): pl.pallas_call(start_body, in_specs=[HBM] * 5, out_specs=[VMEM] * 3, out_...  2.2 us
  transfers between devices with their start and end apart: 22, of which 7 were waited for; matrix products, arithmetic and copies ran while one was open for 0% of the time, Pallas kernels for 25%

profile of v2, /device:TPU:1, one launch (start us, length us, event | category | flops | bytes accessed | tf_op | source)
XLA Modules:
  0.0 85.2 jit_solution(17075224109075965329)
XLA Ops:
  0.0 2.2 %shard_map.55 = (bf16[256,1792]{1,0:T(8,128)(2,1)S(1)}, bf16[256,1024]{1,0:T(8,128)(2,1)S(1)}, s32[8,128]{1,0:T(8,128)S(1)}) custom-call(s32[128]{0:T(128)} %sizes_hbm.6, s32[16,32]{1,0:T(8,128)} %bitcast.4, s32[16,128]{1,0:T(8,128)} %d_mask_hbm.1, bf16[1,256,2048]{2,1,0:T(8,128)(2,1)} %tensor_hbm.1, bf16[256,1024]{1,0:T(8,128)(2,1)} %density_hbm.1), custom_call_target="tpu_custom_call" | custom-call | flops 5000000000 | tf_op jit(solution)/shard_map/pallas_call | solution.py:117
  2.2 1.5 %collective-permute-start.22 = (bf16[256,1792]{1,0:T(8,128)(2,1)S(1)}, bf16[256,1792]{1,0:T(8,128)(2,1)S(1)}, u32[]{:S(2)}, u32[]{:S(2)}) collective-permute-start(bf16[256,1792]{1,0:T(8,128)(2,1)S(1)} %get-tuple-element.103.refs_0_), channel_id=1, source_target_pairs={{0,1},{1,0},{2,3},{3,2},{4,5},{5,4},{6,7},{7,6},{8,9},{9,8},{10,11... | collective-permute-start | bytes 2752520 | tf_op jit(solution)/shard_map/ppermute | solution.py:32
  3.7 2.6 %collective-permute-start.24 = (bf16[256,1792]{1,0:T(8,128)(2,1)S(1)}, bf16[256,1792]{1,0:T(8,128)(2,1)S(1)}, u32[]{:S(2)}, u32[]{:S(2)}) collective-permute-start(bf16[256,1792]{1,0:T(8,128)(2,1)S(1)} %get-tuple-element.103.refs_0_), channel_id=1, source_target_pairs={{0,2},{1,7},{2,4},{3,1},{4,6},{5,3},{6,0},{7,5},{8,10},{9,15},{10,... | collective-permute-start | bytes 2752520 | tf_op jit(solution)/shard_map/ppermute | solution.py:28
  6.3 2.9 %collective-permute-start.26 = (bf16[256,1024]{1,0:T(8,128)(2,1)S(1)}, bf16[256,1024]{1,0:T(8,128)(2,1)S(1)}, u32[]{:S(2)}, u32[]{:S(2)}) collective-permute-start(bf16[256,1024]{1,0:T(8,128)(2,1)S(1)} %get-tuple-element.105.refs_0_), channel_id=1, source_target_pairs={{0,64},{64,0},{1,65},{65,1},{2,66},{66,2},{3,67},{67,3},{4,68},{68... | collective-permute-start | bytes 1572872 | tf_op jit(solution)/shard_map/ppermute | solution.py:32
  9.2 3.8 %collective-permute-start.25 = (bf16[256,1024]{1,0:T(8,128)(2,1)S(1)}, bf16[256,1024]{1,0:T(8,128)(2,1)S(1)}, u32[]{:S(2)}, u32[]{:S(2)}) collective-permute-start(bf16[256,1024]{1,0:T(8,128)(2,1)S(1)} %get-tuple-element.105.refs_0_), channel_id=1, source_target_pairs={{0,16},{1,49},{16,32},{17,1},{32,48},{33,17},{48,0},{49,33},{2,18}... | collective-permute-start | bytes 1572872 | tf_op jit(solution)/shard_map/ppermute | solution.py:28
  13.0 0.9 %shard_map.56.refs_2_ = bf16[1792,1024]{1,0:T(8,128)(2,1)S(1)} custom-call(s32[128]{0:T(128)S(1)} %copy-done.8, bf16[256,1024]{1,0:T(8,128)(2,1)S(1)} %get-tuple-element.105.refs_0_), custom_call_target="tpu_custom_call" | custom-call | flops 5000000000 | tf_op jit(solution)/shard_map/pallas_call | solution.py:172
  13.9 0.6 collective-permute-start.23
  14.9 6.5 %collective-permute-done.26.refs_1_ = bf16[256,1024]{1,0:T(8,128)(2,1)S(1)} collective-permute-done((bf16[256,1024]{1,0:T(8,128)(2,1)S(1)}, bf16[256,1024]{1,0:T(8,128)(2,1)S(1)}, u32[]{:S(2)}, u32[]{:S(2)}) %collective-permute-start.26) | collective-permute-done | bytes 524320 | tf_op jit(solution)/shard_map/ppermute | solution.py:32
  21.4 3.8 %collective-permute-start.28 = (bf16[256,1024]{1,0:T(8,128)(2,1)S(1)}, bf16[256,1024]{1,0:T(8,128)(2,1)S(1)}, u32[]{:S(2)}, u32[]{:S(2)}) collective-permute-start(bf16[256,1024]{1,0:T(8,128)(2,1)S(1)} %collective-permute-done.25.refs_0_), channel_id=1, source_target_pairs={{0,16},{1,49},{16,32},{17,1},{32,48},{33,17},{48,0},{49,33},{2,18}... | collective-permute-start | bytes 1572872 | tf_op jit(solution)/shard_map/ppermute | solution.py:28
  25.2 1.2 %shard_map.57.refs_2_ = bf16[1792,1024]{1,0:T(8,128)(2,1)S(1)} custom-call(s32[128]{0:T(128)S(1)} %copy-done.8, bf16[256,1024]{1,0:T(8,128)(2,1)S(1)} %collective-permute-done.25.refs_0_, bf16[256,1024]{1,0:T(8,128)(2,1)S(1)} %collective-permute-done.26.refs_1_, bf16[1792,1024]{1,0:T(8,128)(2,1)S(1)} %shard_map.56.refs_2_), custom_call_target="tpu_custom_call", output_to_operand_aliasing={{}: (3, {})} | custom-call | flops 5000000000 | tf_op jit(solution)/shard_map/pallas_call | solution.py:172
  26.5 1.7 %collective-permute-start.27 = (bf16[256,1792]{1,0:T(8,128)(2,1)S(1)}, bf16[256,1792]{1,0:T(8,128)(2,1)S(1)}, u32[]{:S(2)}, u32[]{:S(2)}) collective-permute-start(bf16[256,1792]{1,0:T(8,128)(2,1)S(1)} %collective-permute-done.24.refs_2_), channel_id=1, source_target_pairs={{0,1},{1,0},{2,3},{3,2},{4,5},{5,4},{6,7},{7,6},{8,9},{9,8},{10,11... | collective-permute-start | bytes 2752520 | tf_op jit(solution)/shard_map/ppermute | solution.py:32
  28.2 3.0 %collective-permute-done.28.refs_0_ = bf16[256,1024]{1,0:T(8,128)(2,1)S(1)} collective-permute-done((bf16[256,1024]{1,0:T(8,128)(2,1)S(1)}, bf16[256,1024]{1,0:T(8,128)(2,1)S(1)}, u32[]{:S(2)}, u32[]{:S(2)}) %collective-permute-start.28) | collective-permute-done | bytes 524320 | tf_op jit(solution)/shard_map/ppermute | solution.py:28
  31.2 3.1 %collective-permute-start.32 = (bf16[256,1024]{1,0:T(8,128)(2,1)S(1)}, bf16[256,1024]{1,0:T(8,128)(2,1)S(1)}, u32[]{:S(2)}, u32[]{:S(2)}) collective-permute-start(bf16[256,1024]{1,0:T(8,128)(2,1)S(1)} %collective-permute-done.28.refs_0_), channel_id=1, source_target_pairs={{0,16},{1,49},{16,32},{17,1},{32,48},{33,17},{48,0},{49,33},{2,18}... | collective-permute-start | bytes 1572872 | tf_op jit(solution)/shard_map/ppermute | solution.py:28
  34.4 0.5 collective-permute-start.37
  34.9 2.0 %collective-permute-done.29.refs_1_ = bf16[256,1024]{1,0:T(8,128)(2,1)S(1)} collective-permute-done((bf16[256,1024]{1,0:T(8,128)(2,1)S(1)}, bf16[256,1024]{1,0:T(8,128)(2,1)S(1)}, u32[]{:S(2)}, u32[]{:S(2)}) %collective-permute-start.29) | collective-permute-done | bytes 524320 | tf_op jit(solution)/shard_map/ppermute | solution.py:28
  36.9 3.4 %collective-permute-start.35 = (bf16[256,1024]{1,0:T(8,128)(2,1)S(1)}, bf16[256,1024]{1,0:T(8,128)(2,1)S(1)}, u32[]{:S(2)}, u32[]{:S(2)}) collective-permute-start(bf16[256,1024]{1,0:T(8,128)(2,1)S(1)} %collective-permute-done.29.refs_1_), channel_id=1, source_target_pairs={{0,16},{1,49},{16,32},{17,1},{32,48},{33,17},{48,0},{49,33},{2,18}... | collective-permute-start | bytes 1572872 | tf_op jit(solution)/shard_map/ppermute | solution.py:28
  40.3 1.3 %shard_map.58.refs_2_ = bf16[1792,1024]{1,0:T(8,128)(2,1)S(1)} custom-call(s32[128]{0:T(128)S(1)} %copy-done.8, bf16[256,1024]{1,0:T(8,128)(2,1)S(1)} %collective-permute-done.28.refs_0_, bf16[256,1024]{1,0:T(8,128)(2,1)S(1)} %collective-permute-done.29.refs_1_, bf16[1792,1024]{1,0:T(8,128)(2,1)S(1)} %shard_map.57.refs_2_), custom_call_target="tpu_custom_call", output_to_operand_aliasing={{}: (3, {})} | custom-call | flops 5000000000 | tf_op jit(solution)/shard_map/pallas_call | solution.py:172
  41.5 0.9 %collective-permute-done.32.refs_0_ = bf16[256,1024]{1,0:T(8,128)(2,1)S(1)} collective-permute-done((bf16[256,1024]{1,0:T(8,128)(2,1)S(1)}, bf16[256,1024]{1,0:T(8,128)(2,1)S(1)}, u32[]{:S(2)}, u32[]{:S(2)}) %collective-permute-start.32) | collective-permute-done | bytes 524320 | tf_op jit(solution)/shard_map/ppermute | solution.py:28
  42.5 1.3 %collective-permute-start.33 = (bf16[256,1792]{1,0:T(8,128)(2,1)S(1)}, bf16[256,1792]{1,0:T(8,128)(2,1)S(1)}, u32[]{:S(2)}, u32[]{:S(2)}) collective-permute-start(bf16[256,1792]{1,0:T(8,128)(2,1)S(1)} %collective-permute-done.31.refs_4_), channel_id=1, source_target_pairs={{0,1},{1,0},{2,3},{3,2},{4,5},{5,4},{6,7},{7,6},{8,9},{9,8},{10,11... | collective-permute-start | bytes 2752520 | tf_op jit(solution)/shard_map/ppermute | solution.py:32
  43.7 1.8 %collective-permute-start.34 = (bf16[256,1792]{1,0:T(8,128)(2,1)S(1)}, bf16[256,1792]{1,0:T(8,128)(2,1)S(1)}, u32[]{:S(2)}, u32[]{:S(2)}) collective-permute-start(bf16[256,1792]{1,0:T(8,128)(2,1)S(1)} %collective-permute-done.31.refs_4_), channel_id=1, source_target_pairs={{0,2},{1,7},{2,4},{3,1},{4,6},{5,3},{6,0},{7,5},{8,10},{9,15},{10,... | collective-permute-start | bytes 2752520 | tf_op jit(solution)/shard_map/ppermute | solution.py:28
  45.7 2.4 %collective-permute-done.35.refs_1_ = bf16[256,1024]{1,0:T(8,128)(2,1)S(1)} collective-permute-done((bf16[256,1024]{1,0:T(8,128)(2,1)S(1)}, bf16[256,1024]{1,0:T(8,128)(2,1)S(1)}, u32[]{:S(2)}, u32[]{:S(2)}) %collective-permute-start.35) | collective-permute-done | bytes 524320 | tf_op jit(solution)/shard_map/ppermute | solution.py:28
  48.1 3.4 %collective-permute-start.36 = (bf16[256,1024]{1,0:T(8,128)(2,1)S(1)}, bf16[256,1024]{1,0:T(8,128)(2,1)S(1)}, u32[]{:S(2)}, u32[]{:S(2)}) collective-permute-start(bf16[256,1024]{1,0:T(8,128)(2,1)S(1)} %collective-permute-done.35.refs_1_), channel_id=1, source_target_pairs={{0,16},{1,49},{16,32},{17,1},{32,48},{33,17},{48,0},{49,33},{2,18}... | collective-permute-start | bytes 1572872 | tf_op jit(solution)/shard_map/ppermute | solution.py:28
  51.5 1.3 %shard_map.59.refs_1_ = bf16[1792,1024]{1,0:T(8,128)(2,1)S(1)} custom-call(s32[128]{0:T(128)S(1)} %copy-done.8, bf16[256,1024]{1,0:T(8,128)(2,1)S(1)} %collective-permute-done.32.refs_0_, bf16[256,1024]{1,0:T(8,128)(2,1)S(1)} %collective-permute-done.35.refs_1_, bf16[1792,1024]{1,0:T(8,128)(2,1)S(1)} %shard_map.58.refs_2_), custom_call_target="tpu_custom_call", output_to_operand_aliasing={{}: (3, {})} | custom-call | flops 5000000000 | tf_op jit(solution)/shard_map/pallas_call | solution.py:172
  52.8 1.7 %collective-permute-start.40 = (bf16[256,1792]{1,0:T(8,128)(2,1)S(1)}, bf16[256,1792]{1,0:T(8,128)(2,1)S(1)}, u32[]{:S(2)}, u32[]{:S(2)}) collective-permute-start(bf16[256,1792]{1,0:T(8,128)(2,1)S(1)} %collective-permute-done.37.refs_6_), channel_id=1, source_target_pairs={{0,8},{8,0},{1,9},{9,1},{2,10},{10,2},{3,11},{11,3},{4,12},{12,4},... | collective-permute-start | bytes 2752520 | tf_op jit(solution)/shard_map/ppermute | solution.py:32
  54.5 2.2 %collective-permute-done.34.refs_2_ = bf16[256,1792]{1,0:T(8,128)(2,1)S(1)} collective-permute-done((bf16[256,1792]{1,0:T(8,128)(2,1)S(1)}, bf16[256,1792]{1,0:T(8,128)(2,1)S(1)}, u32[]{:S(2)}, u32[]{:S(2)}) %collective-permute-start.34) | collective-permute-done | bytes 917536 | tf_op jit(solution)/shard_map/ppermute | solution.py:28
  56.7 2.5 %collective-permute-start.42 = (bf16[256,1792]{1,0:T(8,128)(2,1)S(1)}, bf16[256,1792]{1,0:T(8,128)(2,1)S(1)}, u32[]{:S(2)}, u32[]{:S(2)}) collective-permute-start(bf16[256,1792]{1,0:T(8,128)(2,1)S(1)} %collective-permute-done.33.refs_5_), channel_id=1, source_target_pairs={{0,2},{1,7},{2,4},{3,1},{4,6},{5,3},{6,0},{7,5},{8,10},{9,15},{10,... | collective-permute-start | bytes 2752520 | tf_op jit(solution)/shard_map/ppermute | solution.py:28
  59.8 1.2 %shard_map.60.rho_ref = bf16[1792,1024]{1,0:T(8,128)(2,1)S(1)} custom-call(s32[128]{0:T(128)S(1)} %copy-done.8, bf16[256,1024]{1,0:T(8,128)(2,1)S(1)} %collective-permute-done.36.refs_0_, bf16[1792,1024]{1,0:T(8,128)(2,1)S(1)} %shard_map.59.refs_1_), custom_call_target="tpu_custom_call", output_to_operand_aliasing={{}: (2, {})} | custom-call | flops 5000000000 | tf_op jit(solution)/shard_map/pallas_call | solution.py:172
  61.0 9.9 %shard_map.61 = (bf16[4096,1024]{1,0:T(8,128)(2,1)}, s32[8,128]{1,0:T(8,128)S(1)}) custom-call(s32[8,128]{1,0:T(8,128)S(1)} %get-tuple-element.102.live_ref, bf16[1792,1024]{1,0:T(8,128)(2,1)S(1)} %shard_map.60.rho_ref, bf16[256,1792]{1,0:T(8,128)(2,1)S(1)} %get-tuple-element.103.refs_0_, bf16[256,1792]{1,0:T(8,128)(2,1)S(1)} %collective-permute-done.22.refs_1_, ...), custom_call_target="tpu_custom_call" | custom-call | flops 7516192768 | bytes 4194304 | tf_op jit(solution)/shard_map/pallas_call | solution.py:217
  70.9 2.0 %collective-permute-start.43 = (bf16[256,1792]{1,0:T(8,128)(2,1)S(1)}, bf16[256,1792]{1,0:T(8,128)(2,1)S(1)}, u32[]{:S(2)}, u32[]{:S(2)}) collective-permute-start(bf16[256,1792]{1,0:T(8,128)(2,1)S(1)} %collective-permute-done.42.refs_2_), channel_id=1, source_target_pairs={{0,1},{1,0},{2,3},{3,2},{4,5},{5,4},{6,7},{7,6},{8,9},{9,8},{10,11... | collective-permute-start | bytes 2752520 | tf_op jit(solution)/shard_map/ppermute | solution.py:32
  73.3 5.2 %shard_map.62 = (bf16[4096,1024]{1,0:T(8,128)(2,1)}, s32[8,128]{1,0:T(8,128)S(1)}) custom-call(s32[8,128]{1,0:T(8,128)S(1)} %get-tuple-element.121.live_ref, bf16[1792,1024]{1,0:T(8,128)(2,1)S(1)} %shard_map.60.rho_ref, bf16[256,1792]{1,0:T(8,128)(2,1)S(1)} %collective-permute-done.30.refs_0_, ...), custom_call_target="tpu_custom_call", output_to_operand_aliasing={{0}: (6, {})} | custom-call | flops 3758096384 | bytes 2097152 | tf_op jit(solution)/shard_map/pallas_call | solution.py:217
  78.5 5.2 %shard_map.63 = (bf16[4096,1024]{1,0:T(8,128)(2,1)}, s32[8,128]{1,0:T(8,128)S(1)}) custom-call(s32[8,128]{1,0:T(8,128)S(1)} %get-tuple-element.125.live_ref, bf16[1792,1024]{1,0:T(8,128)(2,1)S(1)} %shard_map.60.rho_ref, bf16[256,1792]{1,0:T(8,128)(2,1)S(1)} %collective-permute-done.40.refs_0_, ...), custom_call_target="tpu_custom_call", output_to_operand_aliasing={{0}: (6, {})} | custom-call | flops 3758096384 | bytes 2097152 | tf_op jit(solution)/shard_map/pallas_call | solution.py:217
  83.7 0.5 slice.3
  (33 shorter events, 1.8 us)
Async XLA Ops:
  0.0 12.9 %copy-start.8 = (s32[128]{0:T(128)S(1)}, s32[128]{0:T(128)}, u32[]{:S(2)}) copy-start(s32[128]{0:T(128)} %sizes_hbm.6) | copy-start | bytes 1540
  2.2 11.6 %collective-permute-start.22 = (bf16[256,1792]{1,0:T(8,128)(2,1)S(1)}, bf16[256,1792]{1,0:T(8,128)(2,1)S(1)}, u32[]{:S(2)}, u32[]{:S(2)}) collective-permute-start(bf16[256,1792]{1,0:T(8,128)(2,1)S(1)} %get-tuple-element.103.refs_0_), channel_id=1, source_target_pairs={{0,1},{1,0},{2,3},{3,2},{4,5},{5,4},{6,7},{7,6},{8,9},{9,8},{10,11... | collective-permute-start | bytes 2752520 | tf_op jit(solution)/shard_map/ppermute | solution.py:32
  3.7 21.5 %collective-permute-start.24 = (bf16[256,1792]{1,0:T(8,128)(2,1)S(1)}, bf16[256,1792]{1,0:T(8,128)(2,1)S(1)}, u32[]{:S(2)}, u32[]{:S(2)}) collective-permute-start(bf16[256,1792]{1,0:T(8,128)(2,1)S(1)} %get-tuple-element.103.refs_0_), channel_id=1, source_target_pairs={{0,2},{1,7},{2,4},{3,1},{4,6},{5,3},{6,0},{7,5},{8,10},{9,15},{10,... | collective-permute-start | bytes 2752520 | tf_op jit(solution)/shard_map/ppermute | solution.py:28
  6.3 15.1 %collective-permute-start.26 = (bf16[256,1024]{1,0:T(8,128)(2,1)S(1)}, bf16[256,1024]{1,0:T(8,128)(2,1)S(1)}, u32[]{:S(2)}, u32[]{:S(2)}) collective-permute-start(bf16[256,1024]{1,0:T(8,128)(2,1)S(1)} %get-tuple-element.105.refs_0_), channel_id=1, source_target_pairs={{0,64},{64,0},{1,65},{65,1},{2,66},{66,2},{3,67},{67,3},{4,68},{68... | collective-permute-start | bytes 1572872 | tf_op jit(solution)/shard_map/ppermute | solution.py:32
  9.2 12.2 %collective-permute-start.25 = (bf16[256,1024]{1,0:T(8,128)(2,1)S(1)}, bf16[256,1024]{1,0:T(8,128)(2,1)S(1)}, u32[]{:S(2)}, u32[]{:S(2)}) collective-permute-start(bf16[256,1024]{1,0:T(8,128)(2,1)S(1)} %get-tuple-element.105.refs_0_), channel_id=1, source_target_pairs={{0,16},{1,49},{16,32},{17,1},{32,48},{33,17},{48,0},{49,33},{2,18}... | collective-permute-start | bytes 1572872 | tf_op jit(solution)/shard_map/ppermute | solution.py:28
  13.9 12.6 %collective-permute-start.23 = (bf16[256,1792]{1,0:T(8,128)(2,1)S(1)}, bf16[256,1792]{1,0:T(8,128)(2,1)S(1)}, u32[]{:S(2)}, u32[]{:S(2)}) collective-permute-start(bf16[256,1792]{1,0:T(8,128)(2,1)S(1)} %collective-permute-done.22.refs_1_), channel_id=1, source_target_pairs={{0,2},{1,7},{2,4},{3,1},{4,6},{5,3},{6,0},{7,5},{8,10},{9,15},{10,... | collective-permute-start | bytes 2752520 | tf_op jit(solution)/shard_map/ppermute | solution.py:28
  14.5 27.1 %collective-permute-start.31 = (bf16[256,1792]{1,0:T(8,128)(2,1)S(1)}, bf16[256,1792]{1,0:T(8,128)(2,1)S(1)}, u32[]{:S(2)}, u32[]{:S(2)}) collective-permute-start(bf16[256,1792]{1,0:T(8,128)(2,1)S(1)} %get-tuple-element.103.refs_0_), channel_id=1, source_target_pairs={{0,8},{8,0},{1,9},{9,1},{2,10},{10,2},{3,11},{11,3},{4,12},{12,4},... | collective-permute-start | bytes 2752520 | tf_op jit(solution)/shard_map/ppermute | solution.py:32
  21.4 9.9 %collective-permute-start.28 = (bf16[256,1024]{1,0:T(8,128)(2,1)S(1)}, bf16[256,1024]{1,0:T(8,128)(2,1)S(1)}, u32[]{:S(2)}, u32[]{:S(2)}) collective-permute-start(bf16[256,1024]{1,0:T(8,128)(2,1)S(1)} %collective-permute-done.25.refs_0_), channel_id=1, source_target_pairs={{0,16},{1,49},{16,32},{17,1},{32,48},{33,17},{48,0},{49,33},{2,18}... | collective-permute-start | bytes 1572872 | tf_op jit(solution)/shard_map/ppermute | solution.py:28
  25.1 11.7 %collective-permute-start.29 = (bf16[256,1024]{1,0:T(8,128)(2,1)S(1)}, bf16[256,1024]{1,0:T(8,128)(2,1)S(1)}, u32[]{:S(2)}, u32[]{:S(2)}) collective-permute-start(bf16[256,1024]{1,0:T(8,128)(2,1)S(1)} %collective-permute-done.26.refs_1_), channel_id=1, source_target_pairs={{0,16},{1,49},{16,32},{17,1},{32,48},{33,17},{48,0},{49,33},{2,18}... | collective-permute-start | bytes 1572872 | tf_op jit(solution)/shard_map/ppermute | solution.py:28
  26.5 19.0 %collective-permute-start.27 = (bf16[256,1792]{1,0:T(8,128)(2,1)S(1)}, bf16[256,1792]{1,0:T(8,128)(2,1)S(1)}, u32[]{:S(2)}, u32[]{:S(2)}) collective-permute-start(bf16[256,1792]{1,0:T(8,128)(2,1)S(1)} %collective-permute-done.24.refs_2_), channel_id=1, source_target_pairs={{0,1},{1,0},{2,3},{3,2},{4,5},{5,4},{6,7},{7,6},{8,9},{9,8},{10,11... | collective-permute-start | bytes 2752520 | tf_op jit(solution)/shard_map/ppermute | solution.py:32
  31.2 11.2 %collective-permute-start.32 = (bf16[256,1024]{1,0:T(8,128)(2,1)S(1)}, bf16[256,1024]{1,0:T(8,128)(2,1)S(1)}, u32[]{:S(2)}, u32[]{:S(2)}) collective-permute-start(bf16[256,1024]{1,0:T(8,128)(2,1)S(1)} %collective-permute-done.28.refs_0_), channel_id=1, source_target_pairs={{0,16},{1,49},{16,32},{17,1},{32,48},{33,17},{48,0},{49,33},{2,18}... | collective-permute-start | bytes 1572872 | tf_op jit(solution)/shard_map/ppermute | solution.py:28
  34.4 17.2 %collective-permute-start.37 = (bf16[256,1792]{1,0:T(8,128)(2,1)S(1)}, bf16[256,1792]{1,0:T(8,128)(2,1)S(1)}, u32[]{:S(2)}, u32[]{:S(2)}) collective-permute-start(bf16[256,1792]{1,0:T(8,128)(2,1)S(1)} %collective-permute-done.24.refs_2_), channel_id=1, source_target_pairs={{0,2},{1,7},{2,4},{3,1},{4,6},{5,3},{6,0},{7,5},{8,10},{9,15},{10,... | collective-permute-start | bytes 2752520 | tf_op jit(solution)/shard_map/ppermute | solution.py:28
  36.9 11.2 %collective-permute-start.35 = (bf16[256,1024]{1,0:T(8,128)(2,1)S(1)}, bf16[256,1024]{1,0:T(8,128)(2,1)S(1)}, u32[]{:S(2)}, u32[]{:S(2)}) collective-permute-start(bf16[256,1024]{1,0:T(8,128)(2,1)S(1)} %collective-permute-done.29.refs_1_), channel_id=1, source_target_pairs={{0,16},{1,49},{16,32},{17,1},{32,48},{33,17},{48,0},{49,33},{2,18}... | collective-permute-start | bytes 1572872 | tf_op jit(solution)/shard_map/ppermute | solution.py:28
  42.5 12.0 %collective-permute-start.33 = (bf16[256,1792]{1,0:T(8,128)(2,1)S(1)}, bf16[256,1792]{1,0:T(8,128)(2,1)S(1)}, u32[]{:S(2)}, u32[]{:S(2)}) collective-permute-start(bf16[256,1792]{1,0:T(8,128)(2,1)S(1)} %collective-permute-done.31.refs_4_), channel_id=1, source_target_pairs={{0,1},{1,0},{2,3},{3,2},{4,5},{5,4},{6,7},{7,6},{8,9},{9,8},{10,11... | collective-permute-start | bytes 2752520 | tf_op jit(solution)/shard_map/ppermute | solution.py:32
  43.7 13.0 %collective-permute-start.34 = (bf16[256,1792]{1,0:T(8,128)(2,1)S(1)}, bf16[256,1792]{1,0:T(8,128)(2,1)S(1)}, u32[]{:S(2)}, u32[]{:S(2)}) collective-permute-start(bf16[256,1792]{1,0:T(8,128)(2,1)S(1)} %collective-permute-done.31.refs_4_), channel_id=1, source_target_pairs={{0,2},{1,7},{2,4},{3,1},{4,6},{5,3},{6,0},{7,5},{8,10},{9,15},{10,... | collective-permute-start | bytes 2752520 | tf_op jit(solution)/shard_map/ppermute | solution.py:28
  45.5 13.8 %collective-permute-start.30 = (bf16[256,1792]{1,0:T(8,128)(2,1)S(1)}, bf16[256,1792]{1,0:T(8,128)(2,1)S(1)}, u32[]{:S(2)}, u32[]{:S(2)}) collective-permute-start(bf16[256,1792]{1,0:T(8,128)(2,1)S(1)} %collective-permute-done.23.refs_3_), channel_id=1, source_target_pairs={{0,1},{1,0},{2,3},{3,2},{4,5},{5,4},{6,7},{7,6},{8,9},{9,8},{10,11... | collective-permute-start | bytes 2752520 | tf_op jit(solution)/shard_map/ppermute | solution.py:32
  48.1 11.7 %collective-permute-start.36 = (bf16[256,1024]{1,0:T(8,128)(2,1)S(1)}, bf16[256,1024]{1,0:T(8,128)(2,1)S(1)}, u32[]{:S(2)}, u32[]{:S(2)}) collective-permute-start(bf16[256,1024]{1,0:T(8,128)(2,1)S(1)} %collective-permute-done.35.refs_1_), channel_id=1, source_target_pairs={{0,16},{1,49},{16,32},{17,1},{32,48},{33,17},{48,0},{49,33},{2,18}... | collective-permute-start | bytes 1572872 | tf_op jit(solution)/shard_map/ppermute | solution.py:28
  52.8 20.4 %collective-permute-start.40 = (bf16[256,1792]{1,0:T(8,128)(2,1)S(1)}, bf16[256,1792]{1,0:T(8,128)(2,1)S(1)}, u32[]{:S(2)}, u32[]{:S(2)}) collective-permute-start(bf16[256,1792]{1,0:T(8,128)(2,1)S(1)} %collective-permute-done.37.refs_6_), channel_id=1, source_target_pairs={{0,8},{8,0},{1,9},{9,1},{2,10},{10,2},{3,11},{11,3},{4,12},{12,4},... | collective-permute-start | bytes 2752520 | tf_op jit(solution)/shard_map/ppermute | solution.py:32
  56.7 14.2 %collective-permute-start.42 = (bf16[256,1792]{1,0:T(8,128)(2,1)S(1)}, bf16[256,1792]{1,0:T(8,128)(2,1)S(1)}, u32[]{:S(2)}, u32[]{:S(2)}) collective-permute-start(bf16[256,1792]{1,0:T(8,128)(2,1)S(1)} %collective-permute-done.33.refs_5_), channel_id=1, source_target_pairs={{0,2},{1,7},{2,4},{3,1},{4,6},{5,3},{6,0},{7,5},{8,10},{9,15},{10,... | collective-permute-start | bytes 2752520 | tf_op jit(solution)/shard_map/ppermute | solution.py:28
  59.2 14.0 %collective-permute-start.39 = (bf16[256,1792]{1,0:T(8,128)(2,1)S(1)}, bf16[256,1792]{1,0:T(8,128)(2,1)S(1)}, u32[]{:S(2)}, u32[]{:S(2)}) collective-permute-start(bf16[256,1792]{1,0:T(8,128)(2,1)S(1)} %collective-permute-done.34.refs_2_), channel_id=1, source_target_pairs={{0,1},{1,0},{2,3},{3,2},{4,5},{5,4},{6,7},{7,6},{8,9},{9,8},{10,11... | collective-permute-start | bytes 2752520 | tf_op jit(solution)/shard_map/ppermute | solution.py:32
  59.3 14.0 %collective-permute-start.38 = (bf16[256,1792]{1,0:T(8,128)(2,1)S(1)}, bf16[256,1792]{1,0:T(8,128)(2,1)S(1)}, u32[]{:S(2)}, u32[]{:S(2)}) collective-permute-start(bf16[256,1792]{1,0:T(8,128)(2,1)S(1)} %collective-permute-done.37.refs_6_), channel_id=1, source_target_pairs={{0,1},{1,0},{2,3},{3,2},{4,5},{5,4},{6,7},{7,6},{8,9},{9,8},{10,11... | collective-permute-start | bytes 2752520 | tf_op jit(solution)/shard_map/ppermute | solution.py:32
  70.9 7.5 %collective-permute-start.43 = (bf16[256,1792]{1,0:T(8,128)(2,1)S(1)}, bf16[256,1792]{1,0:T(8,128)(2,1)S(1)}, u32[]{:S(2)}, u32[]{:S(2)}) collective-permute-start(bf16[256,1792]{1,0:T(8,128)(2,1)S(1)} %collective-permute-done.42.refs_2_), channel_id=1, source_target_pairs={{0,1},{1,0},{2,3},{3,2},{4,5},{5,4},{6,7},{7,6},{8,9},{9,8},{10,11... | collective-permute-start | bytes 2752520 | tf_op jit(solution)/shard_map/ppermute | solution.py:32
  73.2 5.2 %collective-permute-start.41 = (bf16[256,1792]{1,0:T(8,128)(2,1)S(1)}, bf16[256,1792]{1,0:T(8,128)(2,1)S(1)}, u32[]{:S(2)}, u32[]{:S(2)}) collective-permute-start(bf16[256,1792]{1,0:T(8,128)(2,1)S(1)} %collective-permute-done.40.refs_0_), channel_id=1, source_target_pairs={{0,1},{1,0},{2,3},{3,2},{4,5},{5,4},{6,7},{7,6},{8,9},{9,8},{10,11... | collective-permute-start | bytes 2752520 | tf_op jit(solution)/shard_map/ppermute | solution.py:32
  78.5 6.3 %copy-start.2 = (bf16[1,256,2048]{2,1,0:T(8,128)(2,1)S(1)}, bf16[1,256,2048]{2,1,0:T(8,128)(2,1)}, u32[]{:S(2)}) copy-start(bf16[1,256,2048]{2,1,0:T(8,128)(2,1)} %tensor_hbm.1) | copy-start | bytes 3145732
  78.5 6.3 %copy-start.4 = (bf16[256,1024]{1,0:T(8,128)(2,1)S(1)}, bf16[256,1024]{1,0:T(8,128)(2,1)}, u32[]{:S(2)}) copy-start(bf16[256,1024]{1,0:T(8,128)(2,1)} %density_hbm.1) | copy-start | bytes 1572868
  78.5 6.3 %copy-start.6 = (s32[32,16]{0,1:T(8,128)S(1)}, s32[32,16]{0,1:T(8,128)}, u32[]{:S(2)}) copy-start(s32[32,16]{0,1:T(8,128)} %param.9) | copy-start | bytes 6148
  78.5 6.3 %copy-start.7 = (s32[16,128]{1,0:T(8,128)S(1)}, s32[16,128]{1,0:T(8,128)}, u32[]{:S(2)}) copy-start(s32[16,128]{1,0:T(8,128)} %d_mask_hbm.1) | copy-start | bytes 24580

commit v3 on v2

--- a/solution.py
+++ b/solution.py
@@ -136,7 +136,14 @@
     )(sizes, t_mask.T, d_mask, tensor, density)
 
 
-def gather_body(origins, first, sizes_hbm, *refs):
+def in_spans(columns, total, span):
+    if span == total:
+        columns(0, 0)
+    else:
+        lax.fori_loop(0, total // span, columns, 0)
+
+
+def gather_body(origins, first, span, sizes_hbm, *refs):
     panels = len(origins)
     out_ref, sizes_ref, sem = refs[panels + (0 if first else 1) :]
     copy = pltpu.make_async_copy(sizes_hbm, sizes_ref, sem)
@@ -162,15 +169,21 @@
             pick = pick | (inside & (target == slot - b * BLK + base))
             base = base + size
         pick = pick.astype(jnp.float32).astype(jnp.bfloat16)
-        moved = jnp.dot(pick, refs[k][...], preferred_element_type=jnp.float32)
-        out_ref[pl.ds(start, window), :] += moved.astype(out_ref.dtype)
-
-
-def gather(sizes, panels, wide, out):
+
+        def columns(n, carry):
+            at = slice(None) if span == out_ref.shape[1] else pl.ds(pl.multiple_of(n * span, span), span)
+            moved = jnp.dot(pick, refs[k][:, at], preferred_element_type=jnp.float32)
+            out_ref[pl.ds(start, window), at] += moved.astype(out_ref.dtype)
+            return carry
+
+        in_spans(columns, out_ref.shape[1], span)
+
+
+def gather(sizes, panels, wide, out, span):
     cols = panels[0][1].shape[1]
     first = out is None
     return pl.pallas_call(
-        functools.partial(gather_body, [o for o, _ in panels], first),
+        functools.partial(gather_body, [o for o, _ in panels], first, span),
         in_specs=[HBM] + [VMEM] * (len(panels) + (0 if first else 1)),
         out_specs=VMEM,
         out_shape=jax.ShapeDtypeStruct((wide, cols), jnp.bfloat16),
@@ -181,10 +194,10 @@
     )(sizes, *[p for _, p in panels], *([] if first else [out]))
 
 
-def product_body(origins, split, first, live_ref, rho_ref, *refs):
+def product_body(origins, first, span, live_ref, rho_ref, *refs):
     count = len(origins)
-    a_refs = refs[: sum(split)]
-    out_ref, token_ref, o_buf, o_sem = refs[sum(split) + (0 if first else 1) :]
+    a_refs = refs[:count]
+    out_ref, token_ref, o_buf, o_sem = refs[count + (0 if first else 1) :]
     tall = o_buf.shape[1]
 
     def out_copy(i):
@@ -193,29 +206,30 @@
             o_buf.at[i % 2], out_ref.at[pl.ds(start, tall)], o_sem.at[i % 2]
         )
 
-    k = 0
-    for i, parts in enumerate(split):
+    for i in range(count):
         if i >= 2:
             out_copy(i - 2).wait()
-        rows = [a_refs[k + part][...] for part in range(parts)]
-        k += parts
-        rows = rows[0] if parts == 1 else jnp.concatenate(rows, axis=0)
-        o_buf[i % 2] = jnp.dot(
-            rows, rho_ref[...], preferred_element_type=jnp.float32
-        ).astype(o_buf.dtype)
+
+        def columns(n, carry):
+            at = slice(None) if span == out_ref.shape[1] else pl.ds(pl.multiple_of(n * span, span), span)
+            o_buf[i % 2, :, at] = jnp.dot(
+                a_refs[i][...], rho_ref[:, at], preferred_element_type=jnp.float32
+            ).astype(o_buf.dtype)
+            return carry
+
+        in_spans(columns, o_buf.shape[2], span)
         out_copy(i).start()
     for i in range(max(count - 2, 0), count):
         out_copy(i).wait()
     token_ref[...] = live_ref[...]
 
 
-def product(live, rho, chunks, out, shape):
-    split = [len(parts) for _, parts in chunks]
-    flat = [p for _, parts in chunks for p in parts]
-    tall, wide = sum(p.shape[0] for p in chunks[0][1]), rho.shape[0]
+def product(live, rho, chunks, out, shape, span, cost=1):
+    flat = [part for _, (part,) in chunks]
+    tall, wide = flat[0].shape
     count, first = len(chunks), out is None
     return pl.pallas_call(
-        functools.partial(product_body, [o for o, _ in chunks], split, first),
+        functools.partial(product_body, [o for o, _ in chunks], first, span),
         in_specs=[VMEM] * (2 + len(flat)) + ([] if first else [ANY]),
         out_specs=[ANY, VMEM],
         scratch_shapes=[
@@ -227,65 +241,114 @@
             jax.ShapeDtypeStruct(live.shape, live.dtype),
         ],
         input_output_aliases={} if first else {2 + len(flat): 0},
-        compiler_params=pltpu.CompilerParams(vmem_limit_bytes=8 * MIB),
+        compiler_params=pltpu.CompilerParams(vmem_limit_bytes=42 * MIB),
         cost_estimate=pl.CostEstimate(
-            flops=2 * count * tall * wide * shape[1],
-            bytes_accessed=2 * count * tall * shape[1],
+            flops=2 * cost * count * tall * wide * shape[1],
+            bytes_accessed=2 * cost * count * tall * shape[1],
             transcendentals=0,
         ),
     )(live, rho, *flat, *([] if first else [out]))
 
 
-def contract(wide, out, tensor, density, tensor_mask, density_mask, block_sizes):
+def contract(wide, span, out, tensor, density, tensor_mask, density_mask, block_sizes):
     nz, nx = lax.axis_size("z"), lax.axis_size("x")
     own, rho, live = start(block_sizes, tensor_mask, density_mask, tensor, density, wide)
 
     def add(panels, out, *earlier):
-        return gather(after(block_sizes, *earlier), panels, wide, out)
+        return gather(after(block_sizes, *earlier), panels, wide, out, span)
 
     a1, c_own = passed(own, "x"), swapped(own, "c")
     s1, t0 = passed(rho, "z"), swapped(rho, "yh")
     y0 = swapped(own, "yl")
     g = add([((0, 0), rho)], None, own)
-    b1, a2 = passed(after(c_own, g), "x"), passed(after(a1, g), "x")
-    s2, t1 = passed(after(s1, g), "z"), passed(after(t0, g), "z")
-    g = add([((0, 1), s1), ((1, 0), t0)], g, c_own, a1)
+    b1 = passed(after(c_own, g), "x")
+    s2 = passed(after(s1, g), "z")
+    g = add([((0, 1), s1)], g, c_own)
+    a2, t1 = passed(after(a1, g), "x"), passed(after(t0, g), "z")
+    g = add([((1, 0), t0)], g, a1)
     s3, t2 = passed(after(s2, g), "z"), passed(after(t1, g), "z")
     c_a1 = swapped(after(a1, b1, g), "c")
-    g = add([((0, 2), s2), ((1, 1), t1)], g, b1)
+    g = add([((0, 2), s2), ((1, 1), t1)], g, b1, a2, y0)
     qa, q2 = passed(after(y0, g), "x"), swapped(after(a2, y0, g), "yl")
     c_y0 = swapped(after(y0, s3, g), "c")
     c_b1 = swapped(after(b1, c_a1, g), "c")
     t3 = passed(after(t2, g), "z")
-    g = add([((0, 3), s3), ((1, 2), t2)], g, y0, a2, c_a1)
+    g = add([((0, 3), s3), ((1, 2), t2)], g, c_a1)
     qb = passed(after(c_y0, g), "x")
     c_a2 = swapped(after(a2, c_b1, g), "c")
-    c_qa = swapped(after(qa, c_y0, g), "c")
-    g = add([((1, 3), t3)], g, c_b1, c_y0, qa)
+    g = add([((1, 3), t3)], g, c_b1, c_y0)
     shape = (own.shape[0] * 4 * nx, density.shape[1])
     out, live = product(live, g, [
         ((0, 0, 0), (own,)), ((0, 0, 1), (c_own,)), ((0, 1, 0), (a1,)), ((0, 1, 1), (b1,)),
-        ((1, 0, 0), (y0,)), ((1, 0, 1), (c_y0,)), ((0, 2, 0), (a2,)), ((0, -1, 1), (c_a1,)),
-    ], out, shape)
+        ((1, 0, 0), (y0,)), ((1, 0, 1), (c_y0,)), ((0, -1, 1), (c_a1,)), ((0, -1, 0), (c_b1,)),
+    ], out, shape, span, 0)
+    c_qa = swapped(after(qa, live), "c")
     c_q2 = swapped(after(q2, live), "c")
+    out, live = product(live, g, [
+        ((0, 2, 0), (a2,)), ((0, 2, 1), (c_a2,)), ((1, 1, 0), (qa,)), ((1, 2, 0), (q2,)),
+    ], out, shape, span)
     c_qb = swapped(after(qb, live), "c")
     out, live = product(live, g, [
-        ((0, -1, 0), (c_b1,)), ((0, 2, 1), (c_a2,)), ((1, 1, 0), (qa,)), ((1, -1, 1), (c_qa,)),
-    ], out, shape)
-    out, live = product(live, g, [
-        ((1, 2, 0), (q2,)), ((1, 2, 1), (c_q2,)), ((1, 1, 1), (qb,)), ((1, -1, 0), (c_qb,)),
-    ], out, shape)
+        ((1, -1, 1), (c_qa,)), ((1, 2, 1), (c_q2,)), ((1, 1, 1), (qb,)),
+    ], out, shape, span)
+    out, live = product(live, g, [((1, -1, 0), (c_qb,))], out, shape, span)
     return out, live
+
+
+def expand_keep(block_mask, row_live, col_live):
+    wide = jnp.repeat(jnp.repeat(block_mask == 1, BLK, 0), BLK, 1)
+    return wide & row_live[:, None] & col_live[None, :]
+
+
+def ring(value, axes, count):
+    return lax.ppermute(value, axes, [(i, (i + 1) % count) for i in range(count)])
+
+
+def full_width(out, tensor, density, mask_t, density_mask, block_sizes):
+    rows = lax.axis_size("yh") * lax.axis_size("z")
+    cols = lax.axis_size("yl") * lax.axis_size("x") * lax.axis_size("c")
+    row_at, col_at = at_row(), at_col()
+    _, mu, nu = tensor.shape
+    deep, sig = density.shape
+    live = (jnp.arange(BLK)[None, :] < block_sizes[:, None]).reshape(-1)
+    part = lax.dynamic_slice_in_dim
+    own = jnp.where(
+        expand_keep(part(mask_t, col_at * (mu // BLK), mu // BLK, 1).T, part(live, col_at * mu, mu), live[:nu]),
+        tensor[0], jnp.zeros((), tensor.dtype),
+    )
+    mask = lax.dynamic_slice(
+        density_mask, (row_at * (deep // BLK), col_at * (sig // BLK)), (deep // BLK, sig // BLK)
+    )
+    rho = jnp.where(
+        expand_keep(mask, part(live, row_at * deep, deep), part(live, col_at * sig, sig)),
+        density, jnp.zeros((), density.dtype),
+    )
+
+    def collect(i, carry):
+        whole, panel = carry
+        at = lax.rem(row_at - i + rows, rows) * deep
+        return lax.dynamic_update_slice(whole, panel, (at, 0)), ring(panel, ROW, rows)
+
+    whole, _ = lax.fori_loop(0, rows, collect, (jnp.zeros((nu, sig), rho.dtype), rho))
+
+    def multiply(i, carry):
+        total, chunk = carry
+        at = lax.rem(col_at - i + cols, cols) * mu
+        block = jnp.dot(chunk, whole, preferred_element_type=jnp.float32).astype(total.dtype)
+        return lax.dynamic_update_slice(total, block, (at, 0)), ring(chunk, COL, cols)
+
+    return lax.fori_loop(0, cols, multiply, (out, own))[0]
 
 
 def local(*args):
     nu = args[0].shape[2]
     narrow = nu * 7 // 8
-    out, live = contract(narrow, None, *args)
+    out, live = contract(narrow, args[1].shape[1], None, *args)
     more = live[0, 0] > narrow
+    mask_t = after(args[2], live).T
 
     def again(carry):
-        return jnp.bool_(False), contract(nu, carry[1], *args)[0]
+        return jnp.bool_(False), full_width(carry[1], *args[:2], mask_t, *args[3:])
 
     return lax.while_loop(lambda carry: carry[0], again, (more, out))[1][None]
 

time: 85.4 us -> 85.7 us (level)
  starting transfers between devices: 37.7 us -> 30.8 us
  waiting for transfers between devices: 17.4 us -> 22.7 us
  Pallas kernels: 28.4 us -> 29.5 us
    ppermute x11, starting transfers between devices: 25.6 us -> 20.9 us  [passed(): return lax.ppermute(value, (axis, 'c'), pairs)]
    ppermute x11, waiting for transfers between devices: 6.81 us -> 10.6 us  [swapped(): return lax.ppermute(value, axis, [(0, 1), (1, 0)])]
    ppermute x11, starting transfers between devices: 12.2 us -> 9.95 us  [swapped(): return lax.ppermute(value, axis, [(0, 1), (1, 0)])]
    ppermute x11, waiting for transfers between devices: 10.6 us -> 12.1 us  [passed(): return lax.ppermute(value, (axis, 'c'), pairs)]
    pallas_call x3 -> x4, Pallas kernels: 20.3 us -> 20.9 us  [product(): pl.pallas_call(functools.partial(product_body, [o for o, _ in chunks], fi...]
    pallas_call x5 -> x6, Pallas kernels: 5.93 us -> 6.4 us  [gather(): pl.pallas_call(functools.partial(gather_body, [o for o, _ in panels], fir...]
  transfers between devices with their start and end apart: 22 -> 22, of which waited for: 7 -> 6; matrix products, arithmetic and copies ran while one was open for 0% -> 0% of each run, Pallas kernels for 25% -> 30%
where the time goes in v3:
time: 85.7 us; the launch traced here: 85.5 us
  starting transfers between devices  30.8 us (36%)
  Pallas kernels  29.5 us (34%)
  waiting for transfers between devices  22.7 us (26%)
  local copies, waits for them, and re-layouts  1.36 us (2%)
  between operations  1.08 us (1%)
    pallas_call x4, Pallas kernels, product(): pl.pallas_call(functools.partial(product_body, [o for o, _ in chunks], fi...  20.9 us
    ppermute x11, starting transfers between devices, passed(): return lax.ppermute(value, (axis, 'c'), pairs)  20.9 us
    ppermute x11, waiting for transfers between devices, passed(): return lax.ppermute(value, (axis, 'c'), pairs)  12.1 us
    ppermute x11, waiting for transfers between devices, swapped(): return lax.ppermute(value, axis, [(0, 1), (1, 0)])  10.6 us
    ppermute x11, starting transfers between devices, swapped(): return lax.ppermute(value, axis, [(0, 1), (1, 0)])  9.95 us
    pallas_call x6, Pallas kernels, gather(): pl.pallas_call(functools.partial(gather_body, [o for o, _ in panels], fir...  6.4 us
    pallas_call x1, Pallas kernels, start(): pl.pallas_call(start_body, in_specs=[HBM] * 5, out_specs=[VMEM] * 3, out_...  2.2 us
  transfers between devices with their start and end apart: 22, of which 6 were waited for; matrix products, arithmetic and copies ran while one was open for 0% of the time, Pallas kernels for 30%

profile of v3, /device:TPU:1, one launch (start us, length us, event | category | flops | bytes accessed | tf_op | source)
XLA Modules:
  0.0 85.5 jit_solution(3973303347460729090)
XLA Ops:
  0.0 0.7 copy-done
  0.7 2.2 %shard_map.55 = (bf16[256,1792]{1,0:T(8,128)(2,1)S(1)}, bf16[256,1024]{1,0:T(8,128)(2,1)S(1)}, s32[8,128]{1,0:T(8,128)S(1)}) custom-call(s32[128]{0:T(128)} %sizes_hbm.7, s32[16,32]{1,0:T(8,128)S(1)} %bitcast.34, s32[16,128]{1,0:T(8,128)} %d_mask_hbm.1, bf16[1,256,2048]{2,1,0:T(8,128)(2,1)} %tensor_hbm.1, bf16[256,1024]{1,0:T(8,128)(2,1)} %density_hbm.1), custom_call_target="tpu_custom_call" | custom-call | flops 5000000000 | tf_op jit(solution)/shard_map/pallas_call | solution.py:117
  2.9 3.4 %collective-permute-start.4 = (bf16[256,1792]{1,0:T(8,128)(2,1)S(1)}, bf16[256,1792]{1,0:T(8,128)(2,1)S(1)}, u32[]{:S(2)}, u32[]{:S(2)}) collective-permute-start(bf16[256,1792]{1,0:T(8,128)(2,1)S(1)} %get-tuple-element.250.refs_0_), channel_id=1, source_target_pairs={{0,2},{1,7},{2,4},{3,1},{4,6},{5,3},{6,0},{7,5},{8,10},{9,15},{10,... | collective-permute-start | bytes 2752520 | tf_op jit(solution)/shard_map/ppermute | solution.py:28
  6.3 3.8 %collective-permute-start.6 = (bf16[256,1024]{1,0:T(8,128)(2,1)S(1)}, bf16[256,1024]{1,0:T(8,128)(2,1)S(1)}, u32[]{:S(2)}, u32[]{:S(2)}) collective-permute-start(bf16[256,1024]{1,0:T(8,128)(2,1)S(1)} %get-tuple-element.252.refs_0_), channel_id=1, source_target_pairs={{0,16},{1,49},{16,32},{17,1},{32,48},{33,17},{48,0},{49,33},{2,18}... | collective-permute-start | bytes 1572872 | tf_op jit(solution)/shard_map/ppermute | solution.py:28
  10.0 2.9 %collective-permute-start.5 = (bf16[256,1024]{1,0:T(8,128)(2,1)S(1)}, bf16[256,1024]{1,0:T(8,128)(2,1)S(1)}, u32[]{:S(2)}, u32[]{:S(2)}) collective-permute-start(bf16[256,1024]{1,0:T(8,128)(2,1)S(1)} %get-tuple-element.252.refs_0_), channel_id=1, source_target_pairs={{0,64},{64,0},{1,65},{65,1},{2,66},{66,2},{3,67},{67,3},{4,68},{68... | collective-permute-start | bytes 1572872 | tf_op jit(solution)/shard_map/ppermute | solution.py:32
  13.0 0.9 %shard_map.56.refs_1_ = bf16[1792,1024]{1,0:T(8,128)(2,1)S(1)} custom-call(s32[128]{0:T(128)S(1)} %copy-done.3, bf16[256,1024]{1,0:T(8,128)(2,1)S(1)} %get-tuple-element.252.refs_0_), custom_call_target="tpu_custom_call" | custom-call | flops 5000000000 | tf_op jit(solution)/shard_map/pallas_call | solution.py:185
  14.3 1.8 %collective-permute-done.6.refs_0_ = bf16[256,1024]{1,0:T(8,128)(2,1)S(1)} collective-permute-done((bf16[256,1024]{1,0:T(8,128)(2,1)S(1)}, bf16[256,1024]{1,0:T(8,128)(2,1)S(1)}, u32[]{:S(2)}, u32[]{:S(2)}) %collective-permute-start.6) | collective-permute-done | bytes 524320 | tf_op jit(solution)/shard_map/ppermute | solution.py:28
  16.2 3.4 %collective-permute-start.10 = (bf16[256,1024]{1,0:T(8,128)(2,1)S(1)}, bf16[256,1024]{1,0:T(8,128)(2,1)S(1)}, u32[]{:S(2)}, u32[]{:S(2)}) collective-permute-start(bf16[256,1024]{1,0:T(8,128)(2,1)S(1)} %collective-permute-done.6.refs_0_), channel_id=1, source_target_pairs={{0,16},{1,49},{16,32},{17,1},{32,48},{33,17},{48,0},{49,33},{2,18}... | collective-permute-start | bytes 1572872 | tf_op jit(solution)/shard_map/ppermute | solution.py:28
  19.6 1.2 %collective-permute-start.3 = (bf16[256,1792]{1,0:T(8,128)(2,1)S(1)}, bf16[256,1792]{1,0:T(8,128)(2,1)S(1)}, u32[]{:S(2)}, u32[]{:S(2)}) collective-permute-start(bf16[256,1792]{1,0:T(8,128)(2,1)S(1)} %collective-permute-done.2.refs_1_), channel_id=1, source_target_pairs={{0,2},{1,7},{2,4},{3,1},{4,6},{5,3},{6,0},{7,5},{8,10},{9,15},{10,... | collective-permute-start | bytes 2752520 | tf_op jit(solution)/shard_map/ppermute | solution.py:28
  20.7 0.9 %shard_map.57.refs_1_ = bf16[1792,1024]{1,0:T(8,128)(2,1)S(1)} custom-call(s32[128]{0:T(128)S(1)} %copy-done.3, bf16[256,1024]{1,0:T(8,128)(2,1)S(1)} %collective-permute-done.6.refs_0_, bf16[1792,1024]{1,0:T(8,128)(2,1)S(1)} %shard_map.56.refs_1_), custom_call_target="tpu_custom_call", output_to_operand_aliasing={{}: (2, {})} | custom-call | flops 5000000000 | tf_op jit(solution)/shard_map/pallas_call | solution.py:185
  21.6 3.5 %collective-permute-done.5.refs_0_ = bf16[256,1024]{1,0:T(8,128)(2,1)S(1)} collective-permute-done((bf16[256,1024]{1,0:T(8,128)(2,1)S(1)}, bf16[256,1024]{1,0:T(8,128)(2,1)S(1)}, u32[]{:S(2)}, u32[]{:S(2)}) %collective-permute-start.5) | collective-permute-done | bytes 524320 | tf_op jit(solution)/shard_map/ppermute | solution.py:32
  25.2 1.3 %collective-permute-start.8 = (bf16[256,1792]{1,0:T(8,128)(2,1)S(1)}, bf16[256,1792]{1,0:T(8,128)(2,1)S(1)}, u32[]{:S(2)}, u32[]{:S(2)}) collective-permute-start(bf16[256,1792]{1,0:T(8,128)(2,1)S(1)} %collective-permute-done.4.refs_2_), channel_id=1, source_target_pairs={{0,2},{1,7},{2,4},{3,1},{4,6},{5,3},{6,0},{7,5},{8,10},{9,15},{10,... | collective-permute-start | bytes 2752520 | tf_op jit(solution)/shard_map/ppermute | solution.py:28
  26.5 0.9 %shard_map.58.refs_2_ = bf16[1792,1024]{1,0:T(8,128)(2,1)S(1)} custom-call(s32[128]{0:T(128)S(1)} %copy-done.3, bf16[256,1024]{1,0:T(8,128)(2,1)S(1)} %collective-permute-done.5.refs_0_, bf16[1792,1024]{1,0:T(8,128)(2,1)S(1)} %shard_map.57.refs_1_), custom_call_target="tpu_custom_call", output_to_operand_aliasing={{}: (2, {})} | custom-call | flops 5000000000 | tf_op jit(solution)/shard_map/pallas_call | solution.py:185
  27.4 4.7 %collective-permute-done.3.refs_3_ = bf16[256,1792]{1,0:T(8,128)(2,1)S(1)} collective-permute-done((bf16[256,1792]{1,0:T(8,128)(2,1)S(1)}, bf16[256,1792]{1,0:T(8,128)(2,1)S(1)}, u32[]{:S(2)}, u32[]{:S(2)}) %collective-permute-start.3) | collective-permute-done | bytes 917536 | tf_op jit(solution)/shard_map/ppermute | solution.py:28
  32.1 1.5 %collective-permute-start.7 = (bf16[256,1792]{1,0:T(8,128)(2,1)S(1)}, bf16[256,1792]{1,0:T(8,128)(2,1)S(1)}, u32[]{:S(2)}, u32[]{:S(2)}) collective-permute-start(bf16[256,1792]{1,0:T(8,128)(2,1)S(1)} %collective-permute-done.4.refs_2_), channel_id=1, source_target_pairs={{0,1},{1,0},{2,3},{3,2},{4,5},{5,4},{6,7},{7,6},{8,9},{9,8},{10,11... | collective-permute-start | bytes 2752520 | tf_op jit(solution)/shard_map/ppermute | solution.py:32
  33.6 3.8 %collective-permute-start.13 = (bf16[256,1024]{1,0:T(8,128)(2,1)S(1)}, bf16[256,1024]{1,0:T(8,128)(2,1)S(1)}, u32[]{:S(2)}, u32[]{:S(2)}) collective-permute-start(bf16[256,1024]{1,0:T(8,128)(2,1)S(1)} %collective-permute-done.10.refs_0_), channel_id=1, source_target_pairs={{0,16},{1,49},{16,32},{17,1},{32,48},{33,17},{48,0},{49,33},{2,18}... | collective-permute-start | bytes 1572872 | tf_op jit(solution)/shard_map/ppermute | solution.py:28
  37.6 7.0 %collective-permute-done.9.refs_4_ = bf16[256,1792]{1,0:T(8,128)(2,1)S(1)} collective-permute-done((bf16[256,1792]{1,0:T(8,128)(2,1)S(1)}, bf16[256,1792]{1,0:T(8,128)(2,1)S(1)}, u32[]{:S(2)}, u32[]{:S(2)}) %collective-permute-start.9) | collective-permute-done | bytes 917536 | tf_op jit(solution)/shard_map/ppermute | solution.py:32
  44.6 1.3 %shard_map.59.refs_2_ = bf16[1792,1024]{1,0:T(8,128)(2,1)S(1)} custom-call(s32[128]{0:T(128)S(1)} %copy-done.3, bf16[256,1024]{1,0:T(8,128)(2,1)S(1)} %collective-permute-done.10.refs_0_, bf16[256,1024]{1,0:T(8,128)(2,1)S(1)} %collective-permute-done.11.refs_1_, bf16[1792,1024]{1,0:T(8,128)(2,1)S(1)} %shard_map.58.refs_2_), custom_call_target="tpu_custom_call", output_to_operand_aliasing={{}: (3, {})} | custom-call | flops 5000000000 | tf_op jit(solution)/shard_map/pallas_call | solution.py:185
  46.5 0.6 collective-permute-start.18
  47.2 1.1 %collective-permute-start.19 = (bf16[256,1792]{1,0:T(8,128)(2,1)S(1)}, bf16[256,1792]{1,0:T(8,128)(2,1)S(1)}, u32[]{:S(2)}, u32[]{:S(2)}) collective-permute-start(bf16[256,1792]{1,0:T(8,128)(2,1)S(1)} %collective-permute-done.8.refs_0_), channel_id=1, source_target_pairs={{0,8},{8,0},{1,9},{9,1},{2,10},{10,2},{3,11},{11,3},{4,12},{12,4},... | collective-permute-start | bytes 2752520 | tf_op jit(solution)/shard_map/ppermute | solution.py:32
  48.2 1.0 %collective-permute-done.15.refs_1_ = bf16[256,1024]{1,0:T(8,128)(2,1)S(1)} collective-permute-done((bf16[256,1024]{1,0:T(8,128)(2,1)S(1)}, bf16[256,1024]{1,0:T(8,128)(2,1)S(1)}, u32[]{:S(2)}, u32[]{:S(2)}) %collective-permute-start.15) | collective-permute-done | bytes 524320 | tf_op jit(solution)/shard_map/ppermute | solution.py:28
  49.2 3.1 %collective-permute-start.16 = (bf16[256,1024]{1,0:T(8,128)(2,1)S(1)}, bf16[256,1024]{1,0:T(8,128)(2,1)S(1)}, u32[]{:S(2)}, u32[]{:S(2)}) collective-permute-start(bf16[256,1024]{1,0:T(8,128)(2,1)S(1)} %collective-permute-done.15.refs_1_), channel_id=1, source_target_pairs={{0,16},{1,49},{16,32},{17,1},{32,48},{33,17},{48,0},{49,33},{2,18}... | collective-permute-start | bytes 1572872 | tf_op jit(solution)/shard_map/ppermute | solution.py:28
  52.3 1.3 %shard_map.60.refs_1_ = bf16[1792,1024]{1,0:T(8,128)(2,1)S(1)} custom-call(s32[128]{0:T(128)S(1)} %copy-done.3, bf16[256,1024]{1,0:T(8,128)(2,1)S(1)} %collective-permute-done.13.refs_0_, bf16[256,1024]{1,0:T(8,128)(2,1)S(1)} %collective-permute-done.15.refs_1_, bf16[1792,1024]{1,0:T(8,128)(2,1)S(1)} %shard_map.59.refs_2_), custom_call_target="tpu_custom_call", output_to_operand_aliasing={{}: (3, {})} | custom-call | flops 5000000000 | tf_op jit(solution)/shard_map/pallas_call | solution.py:185
  53.9 4.6 %collective-permute-done.16.refs_0_ = bf16[256,1024]{1,0:T(8,128)(2,1)S(1)} collective-permute-done((bf16[256,1024]{1,0:T(8,128)(2,1)S(1)}, bf16[256,1024]{1,0:T(8,128)(2,1)S(1)}, u32[]{:S(2)}, u32[]{:S(2)}) %collective-permute-start.16) | collective-permute-done | bytes 524320 | tf_op jit(solution)/shard_map/ppermute | solution.py:28
  58.4 1.1 %shard_map.61.rho_ref = bf16[1792,1024]{1,0:T(8,128)(2,1)S(1)} custom-call(s32[128]{0:T(128)S(1)} %copy-done.3, bf16[256,1024]{1,0:T(8,128)(2,1)S(1)} %collective-permute-done.16.refs_0_, bf16[1792,1024]{1,0:T(8,128)(2,1)S(1)} %shard_map.60.refs_1_), custom_call_target="tpu_custom_call", output_to_operand_aliasing={{}: (2, {})} | custom-call | flops 5000000000 | tf_op jit(solution)/shard_map/pallas_call | solution.py:185
  59.6 9.7 %shard_map.62 = (bf16[4096,1024]{1,0:T(8,128)(2,1)}, s32[8,128]{1,0:T(8,128)S(1)}) custom-call(s32[8,128]{1,0:T(8,128)S(1)} %get-tuple-element.249.live_ref, bf16[1792,1024]{1,0:T(8,128)(2,1)S(1)} %shard_map.61.rho_ref, bf16[256,1792]{1,0:T(8,128)(2,1)S(1)} %get-tuple-element.250.refs_0_, bf16[256,1792]{1,0:T(8,128)(2,1)S(1)} %collective-permute-done.2.refs_1_, ...), custom_call_target="tpu_custom_call" | custom-call | tf_op jit(solution)/shard_map/pallas_call | solution.py:231
  69.3 2.5 %collective-permute-start.20 = (bf16[256,1792]{1,0:T(8,128)(2,1)S(1)}, bf16[256,1792]{1,0:T(8,128)(2,1)S(1)}, u32[]{:S(2)}, u32[]{:S(2)}) collective-permute-start(bf16[256,1792]{1,0:T(8,128)(2,1)S(1)} %collective-permute-done.18.refs_2_), channel_id=1, source_target_pairs={{0,1},{1,0},{2,3},{3,2},{4,5},{5,4},{6,7},{7,6},{8,9},{9,8},{10,11... | collective-permute-start | bytes 2752520 | tf_op jit(solution)/shard_map/ppermute | solution.py:32
  71.9 5.2 %shard_map.63 = (bf16[4096,1024]{1,0:T(8,128)(2,1)}, s32[8,128]{1,0:T(8,128)S(1)}) custom-call(s32[8,128]{1,0:T(8,128)S(1)} %get-tuple-element.268.live_ref, bf16[1792,1024]{1,0:T(8,128)(2,1)S(1)} %shard_map.61.rho_ref, bf16[256,1792]{1,0:T(8,128)(2,1)S(1)} %collective-permute-done.8.refs_0_, ...), custom_call_target="tpu_custom_call", output_to_operand_aliasing={{0}: (6, {})} | custom-call | flops 3758096384 | bytes 2097152 | tf_op jit(solution)/shard_map/pallas_call | solution.py:231
  77.2 0.7 collective-permute-start.23
  77.9 4.1 %shard_map.64 = (bf16[4096,1024]{1,0:T(8,128)(2,1)}, s32[8,128]{1,0:T(8,128)S(1)}) custom-call(s32[8,128]{1,0:T(8,128)S(1)} %get-tuple-element.273.live_ref, bf16[1792,1024]{1,0:T(8,128)(2,1)S(1)} %shard_map.61.rho_ref, bf16[256,1792]{1,0:T(8,128)(2,1)S(1)} %collective-permute-done.20.refs_0_, ...), custom_call_target="tpu_custom_call", output_to_operand_aliasing={{0}: (5, {})} | custom-call | flops 2818572288 | bytes 1572864 | tf_op jit(solution)/shard_map/pallas_call | solution.py:231
  82.0 2.0 %shard_map.65 = (bf16[4096,1024]{1,0:T(8,128)(2,1)}, s32[8,128]{1,0:T(8,128)S(1)}) custom-call(s32[8,128]{1,0:T(8,128)S(1)} %get-tuple-element.278.live_ref, bf16[1792,1024]{1,0:T(8,128)(2,1)S(1)} %shard_map.61.rho_ref, bf16[256,1792]{1,0:T(8,128)(2,1)S(1)} %collective-permute-done.23.refs_0_, ...), custom_call_target="tpu_custom_call", output_to_operand_aliasing={{0}: (3, {})} | custom-call | flops 939524096 | bytes 524288 | tf_op jit(solution)/shard_map/pallas_call | solution.py:231
  84.0 0.6 slice.7
  (34 shorter events, 1.6 us)
Async XLA Ops:
  0.0 0.7 copy-start
  0.7 12.3 %copy-start.3 = (s32[128]{0:T(128)S(1)}, s32[128]{0:T(128)}, u32[]{:S(2)}) copy-start(s32[128]{0:T(128)} %sizes_hbm.7) | copy-start | bytes 1540
  2.9 16.7 %collective-permute-start.4 = (bf16[256,1792]{1,0:T(8,128)(2,1)S(1)}, bf16[256,1792]{1,0:T(8,128)(2,1)S(1)}, u32[]{:S(2)}, u32[]{:S(2)}) collective-permute-start(bf16[256,1792]{1,0:T(8,128)(2,1)S(1)} %get-tuple-element.250.refs_0_), channel_id=1, source_target_pairs={{0,2},{1,7},{2,4},{3,1},{4,6},{5,3},{6,0},{7,5},{8,10},{9,15},{10,... | collective-permute-start | bytes 2752520 | tf_op jit(solution)/shard_map/ppermute | solution.py:28
  6.3 13.3 %collective-permute-start.2 = (bf16[256,1792]{1,0:T(8,128)(2,1)S(1)}, bf16[256,1792]{1,0:T(8,128)(2,1)S(1)}, u32[]{:S(2)}, u32[]{:S(2)}) collective-permute-start(bf16[256,1792]{1,0:T(8,128)(2,1)S(1)} %get-tuple-element.250.refs_0_), channel_id=1, source_target_pairs={{0,1},{1,0},{2,3},{3,2},{4,5},{5,4},{6,7},{7,6},{8,9},{9,8},{10,11... | collective-permute-start | bytes 2752520 | tf_op jit(solution)/shard_map/ppermute | solution.py:32
  6.3 9.9 %collective-permute-start.6 = (bf16[256,1024]{1,0:T(8,128)(2,1)S(1)}, bf16[256,1024]{1,0:T(8,128)(2,1)S(1)}, u32[]{:S(2)}, u32[]{:S(2)}) collective-permute-start(bf16[256,1024]{1,0:T(8,128)(2,1)S(1)} %get-tuple-element.252.refs_0_), channel_id=1, source_target_pairs={{0,16},{1,49},{16,32},{17,1},{32,48},{33,17},{48,0},{49,33},{2,18}... | collective-permute-start | bytes 1572872 | tf_op jit(solution)/shard_map/ppermute | solution.py:28
  10.0 15.1 %collective-permute-start.5 = (bf16[256,1024]{1,0:T(8,128)(2,1)S(1)}, bf16[256,1024]{1,0:T(8,128)(2,1)S(1)}, u32[]{:S(2)}, u32[]{:S(2)}) collective-permute-start(bf16[256,1024]{1,0:T(8,128)(2,1)S(1)} %get-tuple-element.252.refs_0_), channel_id=1, source_target_pairs={{0,64},{64,0},{1,65},{65,1},{2,66},{66,2},{3,67},{67,3},{4,68},{68... | collective-permute-start | bytes 1572872 | tf_op jit(solution)/shard_map/ppermute | solution.py:32
  13.9 30.8 %collective-permute-start.9 = (bf16[256,1792]{1,0:T(8,128)(2,1)S(1)}, bf16[256,1792]{1,0:T(8,128)(2,1)S(1)}, u32[]{:S(2)}, u32[]{:S(2)}) collective-permute-start(bf16[256,1792]{1,0:T(8,128)(2,1)S(1)} %get-tuple-element.250.refs_0_), channel_id=1, source_target_pairs={{0,8},{8,0},{1,9},{9,1},{2,10},{10,2},{3,11},{11,3},{4,12},{12,4},... | collective-permute-start | bytes 2752520 | tf_op jit(solution)/shard_map/ppermute | solution.py:32
  16.2 17.4 %collective-permute-start.10 = (bf16[256,1024]{1,0:T(8,128)(2,1)S(1)}, bf16[256,1024]{1,0:T(8,128)(2,1)S(1)}, u32[]{:S(2)}, u32[]{:S(2)}) collective-permute-start(bf16[256,1024]{1,0:T(8,128)(2,1)S(1)} %collective-permute-done.6.refs_0_), channel_id=1, source_target_pairs={{0,16},{1,49},{16,32},{17,1},{32,48},{33,17},{48,0},{49,33},{2,18}... | collective-permute-start | bytes 1572872 | tf_op jit(solution)/shard_map/ppermute | solution.py:28
  19.6 12.5 %collective-permute-start.3 = (bf16[256,1792]{1,0:T(8,128)(2,1)S(1)}, bf16[256,1792]{1,0:T(8,128)(2,1)S(1)}, u32[]{:S(2)}, u32[]{:S(2)}) collective-permute-start(bf16[256,1792]{1,0:T(8,128)(2,1)S(1)} %collective-permute-done.2.refs_1_), channel_id=1, source_target_pairs={{0,2},{1,7},{2,4},{3,1},{4,6},{5,3},{6,0},{7,5},{8,10},{9,15},{10,... | collective-permute-start | bytes 2752520 | tf_op jit(solution)/shard_map/ppermute | solution.py:28
  25.2 12.3 %collective-permute-start.11 = (bf16[256,1024]{1,0:T(8,128)(2,1)S(1)}, bf16[256,1024]{1,0:T(8,128)(2,1)S(1)}, u32[]{:S(2)}, u32[]{:S(2)}) collective-permute-start(bf16[256,1024]{1,0:T(8,128)(2,1)S(1)} %collective-permute-done.5.refs_0_), channel_id=1, source_target_pairs={{0,16},{1,49},{16,32},{17,1},{32,48},{33,17},{48,0},{49,33},{2,18}... | collective-permute-start | bytes 1572872 | tf_op jit(solution)/shard_map/ppermute | solution.py:28
  25.2 19.4 %collective-permute-start.8 = (bf16[256,1792]{1,0:T(8,128)(2,1)S(1)}, bf16[256,1792]{1,0:T(8,128)(2,1)S(1)}, u32[]{:S(2)}, u32[]{:S(2)}) collective-permute-start(bf16[256,1792]{1,0:T(8,128)(2,1)S(1)} %collective-permute-done.4.refs_2_), channel_id=1, source_target_pairs={{0,2},{1,7},{2,4},{3,1},{4,6},{5,3},{6,0},{7,5},{8,10},{9,15},{10,... | collective-permute-start | bytes 2752520 | tf_op jit(solution)/shard_map/ppermute | solution.py:28
  32.1 13.8 %collective-permute-start.7 = (bf16[256,1792]{1,0:T(8,128)(2,1)S(1)}, bf16[256,1792]{1,0:T(8,128)(2,1)S(1)}, u32[]{:S(2)}, u32[]{:S(2)}) collective-permute-start(bf16[256,1792]{1,0:T(8,128)(2,1)S(1)} %collective-permute-done.4.refs_2_), channel_id=1, source_target_pairs={{0,1},{1,0},{2,3},{3,2},{4,5},{5,4},{6,7},{7,6},{8,9},{9,8},{10,11... | collective-permute-start | bytes 2752520 | tf_op jit(solution)/shard_map/ppermute | solution.py:32
  33.6 12.4 %collective-permute-start.13 = (bf16[256,1024]{1,0:T(8,128)(2,1)S(1)}, bf16[256,1024]{1,0:T(8,128)(2,1)S(1)}, u32[]{:S(2)}, u32[]{:S(2)}) collective-permute-start(bf16[256,1024]{1,0:T(8,128)(2,1)S(1)} %collective-permute-done.10.refs_0_), channel_id=1, source_target_pairs={{0,16},{1,49},{16,32},{17,1},{32,48},{33,17},{48,0},{49,33},{2,18}... | collective-permute-start | bytes 1572872 | tf_op jit(solution)/shard_map/ppermute | solution.py:28
  37.5 11.7 %collective-permute-start.15 = (bf16[256,1024]{1,0:T(8,128)(2,1)S(1)}, bf16[256,1024]{1,0:T(8,128)(2,1)S(1)}, u32[]{:S(2)}, u32[]{:S(2)}) collective-permute-start(bf16[256,1024]{1,0:T(8,128)(2,1)S(1)} %collective-permute-done.11.refs_1_), channel_id=1, source_target_pairs={{0,16},{1,49},{16,32},{17,1},{32,48},{33,17},{48,0},{49,33},{2,18}... | collective-permute-start | bytes 1572872 | tf_op jit(solution)/shard_map/ppermute | solution.py:28
  45.9 7.7 %collective-permute-start.12 = (bf16[256,1792]{1,0:T(8,128)(2,1)S(1)}, bf16[256,1792]{1,0:T(8,128)(2,1)S(1)}, u32[]{:S(2)}, u32[]{:S(2)}) collective-permute-start(bf16[256,1792]{1,0:T(8,128)(2,1)S(1)} %collective-permute-done.3.refs_3_), channel_id=1, source_target_pairs={{0,1},{1,0},{2,3},{3,2},{4,5},{5,4},{6,7},{7,6},{8,9},{9,8},{10,11... | collective-permute-start | bytes 2752520 | tf_op jit(solution)/shard_map/ppermute | solution.py:32
  46.0 7.7 %collective-permute-start.14 = (bf16[256,1792]{1,0:T(8,128)(2,1)S(1)}, bf16[256,1792]{1,0:T(8,128)(2,1)S(1)}, u32[]{:S(2)}, u32[]{:S(2)}) collective-permute-start(bf16[256,1792]{1,0:T(8,128)(2,1)S(1)} %collective-permute-done.9.refs_4_), channel_id=1, source_target_pairs={{0,1},{1,0},{2,3},{3,2},{4,5},{5,4},{6,7},{7,6},{8,9},{9,8},{10,11... | collective-permute-start | bytes 2752520 | tf_op jit(solution)/shard_map/ppermute | solution.py:32
  46.5 22.8 %collective-permute-start.18 = (bf16[256,1792]{1,0:T(8,128)(2,1)S(1)}, bf16[256,1792]{1,0:T(8,128)(2,1)S(1)}, u32[]{:S(2)}, u32[]{:S(2)}) collective-permute-start(bf16[256,1792]{1,0:T(8,128)(2,1)S(1)} %collective-permute-done.9.refs_4_), channel_id=1, source_target_pairs={{0,2},{1,7},{2,4},{3,1},{4,6},{5,3},{6,0},{7,5},{8,10},{9,15},{10,... | collective-permute-start | bytes 2752520 | tf_op jit(solution)/shard_map/ppermute | solution.py:28
  47.2 22.1 %collective-permute-start.19 = (bf16[256,1792]{1,0:T(8,128)(2,1)S(1)}, bf16[256,1792]{1,0:T(8,128)(2,1)S(1)}, u32[]{:S(2)}, u32[]{:S(2)}) collective-permute-start(bf16[256,1792]{1,0:T(8,128)(2,1)S(1)} %collective-permute-done.8.refs_0_), channel_id=1, source_target_pairs={{0,8},{8,0},{1,9},{9,1},{2,10},{10,2},{3,11},{11,3},{4,12},{12,4},... | collective-permute-start | bytes 2752520 | tf_op jit(solution)/shard_map/ppermute | solution.py:32
  49.2 9.2 %collective-permute-start.16 = (bf16[256,1024]{1,0:T(8,128)(2,1)S(1)}, bf16[256,1024]{1,0:T(8,128)(2,1)S(1)}, u32[]{:S(2)}, u32[]{:S(2)}) collective-permute-start(bf16[256,1024]{1,0:T(8,128)(2,1)S(1)} %collective-permute-done.15.refs_1_), channel_id=1, source_target_pairs={{0,16},{1,49},{16,32},{17,1},{32,48},{33,17},{48,0},{49,33},{2,18}... | collective-permute-start | bytes 1572872 | tf_op jit(solution)/shard_map/ppermute | solution.py:28
  53.6 18.3 %collective-permute-start.17 = (bf16[256,1792]{1,0:T(8,128)(2,1)S(1)}, bf16[256,1792]{1,0:T(8,128)(2,1)S(1)}, u32[]{:S(2)}, u32[]{:S(2)}) collective-permute-start(bf16[256,1792]{1,0:T(8,128)(2,1)S(1)} %collective-permute-done.8.refs_0_), channel_id=1, source_target_pairs={{0,1},{1,0},{2,3},{3,2},{4,5},{5,4},{6,7},{7,6},{8,9},{9,8},{10,11... | collective-permute-start | bytes 2752520 | tf_op jit(solution)/shard_map/ppermute | solution.py:32
  53.7 23.4 %collective-permute-start.22 = (bf16[256,1792]{1,0:T(8,128)(2,1)S(1)}, bf16[256,1792]{1,0:T(8,128)(2,1)S(1)}, u32[]{:S(2)}, u32[]{:S(2)}) collective-permute-start(bf16[256,1792]{1,0:T(8,128)(2,1)S(1)} %collective-permute-done.14.refs_5_), channel_id=1, source_target_pairs={{0,2},{1,7},{2,4},{3,1},{4,6},{5,3},{6,0},{7,5},{8,10},{9,15},{10,... | collective-permute-start | bytes 2752520 | tf_op jit(solution)/shard_map/ppermute | solution.py:28
  69.3 8.6 %collective-permute-start.20 = (bf16[256,1792]{1,0:T(8,128)(2,1)S(1)}, bf16[256,1792]{1,0:T(8,128)(2,1)S(1)}, u32[]{:S(2)}, u32[]{:S(2)}) collective-permute-start(bf16[256,1792]{1,0:T(8,128)(2,1)S(1)} %collective-permute-done.18.refs_2_), channel_id=1, source_target_pairs={{0,1},{1,0},{2,3},{3,2},{4,5},{5,4},{6,7},{7,6},{8,9},{9,8},{10,11... | collective-permute-start | bytes 2752520 | tf_op jit(solution)/shard_map/ppermute | solution.py:32
  71.8 6.1 %collective-permute-start.21 = (bf16[256,1792]{1,0:T(8,128)(2,1)S(1)}, bf16[256,1792]{1,0:T(8,128)(2,1)S(1)}, u32[]{:S(2)}, u32[]{:S(2)}) collective-permute-start(bf16[256,1792]{1,0:T(8,128)(2,1)S(1)} %collective-permute-done.19.refs_3_), channel_id=1, source_target_pairs={{0,1},{1,0},{2,3},{3,2},{4,5},{5,4},{6,7},{7,6},{8,9},{9,8},{10,11... | collective-permute-start | bytes 2752520 | tf_op jit(solution)/shard_map/ppermute | solution.py:32
  77.2 4.8 %collective-permute-start.23 = (bf16[256,1792]{1,0:T(8,128)(2,1)S(1)}, bf16[256,1792]{1,0:T(8,128)(2,1)S(1)}, u32[]{:S(2)}, u32[]{:S(2)}) collective-permute-start(bf16[256,1792]{1,0:T(8,128)(2,1)S(1)} %collective-permute-done.22.refs_2_), channel_id=1, source_target_pairs={{0,1},{1,0},{2,3},{3,2},{4,5},{5,4},{6,7},{7,6},{8,9},{9,8},{10,11... | collective-permute-start | bytes 2752520 | tf_op jit(solution)/shard_map/ppermute | solution.py:32
  82.0 2.6 %copy-start.1 = (s32[32,16]{0,1:T(8,128)S(1)}, s32[32,16]{0,1:T(8,128)}, u32[]{:S(2)}) copy-start(s32[32,16]{0,1:T(8,128)} %param.13) | copy-start | bytes 6148
  82.0 3.3 %copy-start.2 = (bf16[1,256,2048]{2,1,0:T(8,128)(2,1)S(1)}, bf16[1,256,2048]{2,1,0:T(8,128)(2,1)}, u32[]{:S(2)}) copy-start(bf16[1,256,2048]{2,1,0:T(8,128)(2,1)} %tensor_hbm.1) | copy-start | bytes 3145732

commit v4 on v3

--- a/solution.py
+++ b/solution.py
@@ -241,13 +241,91 @@
             jax.ShapeDtypeStruct(live.shape, live.dtype),
         ],
         input_output_aliases={} if first else {2 + len(flat): 0},
-        compiler_params=pltpu.CompilerParams(vmem_limit_bytes=42 * MIB),
+        compiler_params=pltpu.CompilerParams(vmem_limit_bytes=44 * MIB),
         cost_estimate=pl.CostEstimate(
             flops=2 * cost * count * tall * wide * shape[1],
             bytes_accessed=2 * cost * count * tall * shape[1],
             transcendentals=0,
         ),
     )(live, rho, *flat, *([] if first else [out]))
+
+
+def early_body(count, rho_ref, *refs):
+    sum_ref = refs[count]
+    for i in range(count):
+        sum_ref[i] = jnp.dot(refs[i][...], rho_ref[...], preferred_element_type=jnp.float32)
+
+
+def early(rho, chunks):
+    tall, wide = chunks[0].shape
+    count, sig = len(chunks), rho.shape[1]
+    return pl.pallas_call(
+        functools.partial(early_body, count),
+        in_specs=[VMEM] * (1 + count),
+        out_specs=VMEM,
+        out_shape=jax.ShapeDtypeStruct((count, tall, sig), jnp.float32),
+        compiler_params=pltpu.CompilerParams(vmem_limit_bytes=8 * MIB),
+        cost_estimate=pl.CostEstimate(
+            flops=2 * count * tall * wide * sig, bytes_accessed=0, transcendentals=0
+        ),
+    )(rho, *chunks)
+
+
+def finish_body(origins, panel_at, sizes_hbm, panel_ref, sum_ref, *refs):
+    count = len(origins)
+    out_ref, sizes_ref, late_ref, o_buf, sem, o_sem = refs[count:]
+    copy = pltpu.make_async_copy(sizes_hbm, sizes_ref, sem)
+    copy.start()
+    rows, wide, tall = panel_ref.shape[0], refs[0].shape[1], o_buf.shape[1]
+    per, window = rows // BLK, late_ref.shape[0]
+    target = lax.broadcasted_iota(jnp.int32, (window, rows), 0)
+    slot = lax.broadcasted_iota(jnp.int32, (window, rows), 1)
+    copy.wait()
+    at = panel_place(*panel_at) * per
+    offset = offset_of(sizes_ref, at)
+    start = pl.multiple_of(jnp.minimum(offset // BLK * BLK, wide - window), BLK)
+    base = offset - start
+    pick = jnp.zeros((window, rows), jnp.bool_)
+    for b in range(per):
+        size = sizes_ref[at + b]
+        inside = (slot >= b * BLK) & (slot < b * BLK + size)
+        pick = pick | (inside & (target == slot - b * BLK + base))
+        base = base + size
+    pick = pick.astype(jnp.float32).astype(jnp.bfloat16)
+    moved = jnp.dot(pick, panel_ref[...], preferred_element_type=jnp.float32)
+    late_ref[...] = moved.astype(late_ref.dtype)
+
+    def out_copy(i):
+        where = pl.multiple_of(chunk_place(*origins[i]) * tall, tall)
+        return pltpu.make_async_copy(o_buf.at[i], out_ref.at[pl.ds(where, tall)], o_sem.at[i])
+
+    for i in range(count):
+        more = jnp.dot(
+            refs[i][:, pl.ds(start, window)], late_ref[...], preferred_element_type=jnp.float32
+        )
+        o_buf[i] = (sum_ref[i] + more).astype(o_buf.dtype)
+        out_copy(i).start()
+    for i in range(count):
+        out_copy(i).wait()
+
+
+def finish(sizes, panel_at, panel, sums, chunks, shape):
+    count, tall = len(chunks), sums.shape[1]
+    return pl.pallas_call(
+        functools.partial(finish_body, [o for o, _ in chunks], panel_at),
+        in_specs=[HBM] + [VMEM] * (2 + count),
+        out_specs=ANY,
+        scratch_shapes=[
+            pltpu.SMEM(sizes.shape, jnp.int32),
+            pltpu.VMEM((panel.shape[0] + BLK, shape[1]), jnp.bfloat16),
+            pltpu.VMEM((count, tall, shape[1]), jnp.bfloat16),
+            pltpu.SemaphoreType.DMA,
+            pltpu.SemaphoreType.DMA((count,)),
+        ],
+        out_shape=jax.ShapeDtypeStruct(shape, jnp.bfloat16),
+        compiler_params=pltpu.CompilerParams(vmem_limit_bytes=38 * MIB),
+        cost_estimate=pl.CostEstimate(flops=0, bytes_accessed=0, transcendentals=0),
+    )(sizes, panel, sums, *[part for _, (part,) in chunks])
 
 
 def contract(wide, span, out, tensor, density, tensor_mask, density_mask, block_sizes):
@@ -276,10 +354,12 @@
     g = add([((0, 3), s3), ((1, 2), t2)], g, c_a1)
     qb = passed(after(c_y0, g), "x")
     c_a2 = swapped(after(a2, c_b1, g), "c")
-    g = add([((1, 3), t3)], g, c_b1, c_y0)
+    sums = early(after(g, c_b1, c_y0), [own, c_own, a1, b1])
+    g = add([((1, 3), t3)], g)
     shape = (own.shape[0] * 4 * nx, density.shape[1])
+    ready = [((0, 0, 0), (own,)), ((0, 0, 1), (c_own,)), ((0, 1, 0), (a1,)), ((0, 1, 1), (b1,))]
+    out = finish(block_sizes, (1, 3), t3, sums, ready, shape)
     out, live = product(live, g, [
-        ((0, 0, 0), (own,)), ((0, 0, 1), (c_own,)), ((0, 1, 0), (a1,)), ((0, 1, 1), (b1,)),
         ((1, 0, 0), (y0,)), ((1, 0, 1), (c_y0,)), ((0, -1, 1), (c_a1,)), ((0, -1, 0), (c_b1,)),
     ], out, shape, span, 0)
     c_qa = swapped(after(qa, live), "c")

time: 85.7 us -> 82.2 us (0.959)
  waiting for transfers between devices: 22.7 us -> 19.4 us
  Pallas kernels: 29.5 us -> 31.8 us
  starting transfers between devices: 30.8 us -> 28.6 us
    ppermute x11, waiting for transfers between devices: 12.1 us -> 4.91 us  [passed(): return lax.ppermute(value, (axis, 'c'), pairs)]
    pallas_call x0 -> x2, Pallas kernels: none -> 6.96 us  [the longest x1 3.97 us: early(): pl.pallas_call(functools.partial(early_body, count), in_specs=[VMEM] * (1...]
    pallas_call x4, Pallas kernels: 20.9 us -> 16.4 us  [product(): pl.pallas_call(functools.partial(product_body, [o for o, _ in chunks], fi...]
    ppermute x11, waiting for transfers between devices: 10.6 us -> 14.5 us  [swapped(): return lax.ppermute(value, axis, [(0, 1), (1, 0)])]
    ppermute x11, starting transfers between devices: 9.95 us -> 8.26 us  [swapped(): return lax.ppermute(value, axis, [(0, 1), (1, 0)])]
  transfers between devices with their start and end apart: 22 -> 22, of which waited for: 6 -> 5; matrix products, arithmetic and copies ran while one was open for 0% -> 0% of each run, Pallas kernels for 30% -> 34%
where the time goes in v4:
time: 82.2 us; the launch traced here: 82 us
  Pallas kernels  31.8 us (39%)
  starting transfers between devices  28.6 us (35%)
  waiting for transfers between devices  19.4 us (24%)
  local copies, waits for them, and re-layouts  1.29 us (2%)
  between operations  0.96 us (1%)
    ppermute x11, starting transfers between devices, passed(): return lax.ppermute(value, (axis, 'c'), pairs)  20.3 us
    pallas_call x4, Pallas kernels, product(): pl.pallas_call(functools.partial(product_body, [o for o, _ in chunks], fi...  16.4 us
    ppermute x11, waiting for transfers between devices, swapped(): return lax.ppermute(value, axis, [(0, 1), (1, 0)])  14.5 us
    ppermute x11, starting transfers between devices, swapped(): return lax.ppermute(value, axis, [(0, 1), (1, 0)])  8.26 us
    pallas_call x6, Pallas kernels, gather(): pl.pallas_call(functools.partial(gather_body, [o for o, _ in panels], fir...  6.22 us
    ppermute x11, waiting for transfers between devices, passed(): return lax.ppermute(value, (axis, 'c'), pairs)  4.91 us
    pallas_call x1, Pallas kernels, early(): pl.pallas_call(functools.partial(early_body, count), in_specs=[VMEM] * (1...  3.97 us
    pallas_call x1, Pallas kernels, finish(): pl.pallas_call(functools.partial(finish_body, [o for o, _ in chunks], pan...  2.99 us
  transfers between devices with their start and end apart: 22, of which 5 were waited for; matrix products, arithmetic and copies ran while one was open for 0% of the time, Pallas kernels for 34%

profile of v4, /device:TPU:1, one launch (start us, length us, event | category | flops | bytes accessed | tf_op | source)
XLA Modules:
  0.0 82.0 jit_solution(2438806309777165304)
XLA Ops:
  0.7 2.2 %shard_map.55 = (bf16[256,1792]{1,0:T(8,128)(2,1)S(1)}, bf16[256,1024]{1,0:T(8,128)(2,1)S(1)}, s32[8,128]{1,0:T(8,128)S(1)}) custom-call(s32[128]{0:T(128)} %sizes_hbm.9, s32[16,32]{1,0:T(8,128)S(1)} %bitcast.34, s32[16,128]{1,0:T(8,128)} %d_mask_hbm.1, bf16[1,256,2048]{2,1,0:T(8,128)(2,1)} %tensor_hbm.1, bf16[256,1024]{1,0:T(8,128)(2,1)} %density_hbm.1), custom_call_target="tpu_custom_call" | custom-call | flops 5000000000 | tf_op jit(solution)/shard_map/pallas_call | solution.py:117
  2.9 1.5 %collective-permute-start.3 = (bf16[256,1792]{1,0:T(8,128)(2,1)S(1)}, bf16[256,1792]{1,0:T(8,128)(2,1)S(1)}, u32[]{:S(2)}, u32[]{:S(2)}) collective-permute-start(bf16[256,1792]{1,0:T(8,128)(2,1)S(1)} %get-tuple-element.251.refs_0_), channel_id=1, source_target_pairs={{0,1},{1,0},{2,3},{3,2},{4,5},{5,4},{6,7},{7,6},{8,9},{9,8},{10,11... | collective-permute-start | bytes 2752520 | tf_op jit(solution)/shard_map/ppermute | solution.py:32
  4.4 3.8 %collective-permute-start.4 = (bf16[256,1024]{1,0:T(8,128)(2,1)S(1)}, bf16[256,1024]{1,0:T(8,128)(2,1)S(1)}, u32[]{:S(2)}, u32[]{:S(2)}) collective-permute-start(bf16[256,1024]{1,0:T(8,128)(2,1)S(1)} %get-tuple-element.250.refs_0_), channel_id=1, source_target_pairs={{0,16},{1,49},{16,32},{17,1},{32,48},{33,17},{48,0},{49,33},{2,18}... | collective-permute-start | bytes 1572872 | tf_op jit(solution)/shard_map/ppermute | solution.py:28
  8.3 2.5 %collective-permute-start.6 = (bf16[256,1792]{1,0:T(8,128)(2,1)S(1)}, bf16[256,1792]{1,0:T(8,128)(2,1)S(1)}, u32[]{:S(2)}, u32[]{:S(2)}) collective-permute-start(bf16[256,1792]{1,0:T(8,128)(2,1)S(1)} %get-tuple-element.251.refs_0_), channel_id=1, source_target_pairs={{0,2},{1,7},{2,4},{3,1},{4,6},{5,3},{6,0},{7,5},{8,10},{9,15},{10,... | collective-permute-start | bytes 2752520 | tf_op jit(solution)/shard_map/ppermute | solution.py:28
  10.7 2.9 %collective-permute-start.2 = (bf16[256,1024]{1,0:T(8,128)(2,1)S(1)}, bf16[256,1024]{1,0:T(8,128)(2,1)S(1)}, u32[]{:S(2)}, u32[]{:S(2)}) collective-permute-start(bf16[256,1024]{1,0:T(8,128)(2,1)S(1)} %get-tuple-element.250.refs_0_), channel_id=1, source_target_pairs={{0,64},{64,0},{1,65},{65,1},{2,66},{66,2},{3,67},{67,3},{4,68},{68... | collective-permute-start | bytes 1572872 | tf_op jit(solution)/shard_map/ppermute | solution.py:32
  13.6 0.9 %shard_map.56.refs_1_ = bf16[1792,1024]{1,0:T(8,128)(2,1)S(1)} custom-call(s32[128]{0:T(128)S(1)} %copy-done.3, bf16[256,1024]{1,0:T(8,128)(2,1)S(1)} %get-tuple-element.250.refs_0_), custom_call_target="tpu_custom_call" | custom-call | flops 5000000000 | tf_op jit(solution)/shard_map/pallas_call | solution.py:185
  15.0 1.8 %collective-permute-start.8 = (bf16[256,1792]{1,0:T(8,128)(2,1)S(1)}, bf16[256,1792]{1,0:T(8,128)(2,1)S(1)}, u32[]{:S(2)}, u32[]{:S(2)}) collective-permute-start(bf16[256,1792]{1,0:T(8,128)(2,1)S(1)} %collective-permute-done.3.refs_1_), channel_id=1, source_target_pairs={{0,2},{1,7},{2,4},{3,1},{4,6},{5,3},{6,0},{7,5},{8,10},{9,15},{10,... | collective-permute-start | bytes 2752520 | tf_op jit(solution)/shard_map/ppermute | solution.py:28
  16.9 0.9 %shard_map.57.refs_1_ = bf16[1792,1024]{1,0:T(8,128)(2,1)S(1)} custom-call(s32[128]{0:T(128)S(1)} %copy-done.3, bf16[256,1024]{1,0:T(8,128)(2,1)S(1)} %collective-permute-done.4.refs_0_, bf16[1792,1024]{1,0:T(8,128)(2,1)S(1)} %shard_map.56.refs_1_), custom_call_target="tpu_custom_call", output_to_operand_aliasing={{}: (2, {})} | custom-call | flops 5000000000 | tf_op jit(solution)/shard_map/pallas_call | solution.py:185
  17.8 3.5 %collective-permute-start.11 = (bf16[256,1024]{1,0:T(8,128)(2,1)S(1)}, bf16[256,1024]{1,0:T(8,128)(2,1)S(1)}, u32[]{:S(2)}, u32[]{:S(2)}) collective-permute-start(bf16[256,1024]{1,0:T(8,128)(2,1)S(1)} %collective-permute-done.4.refs_0_), channel_id=1, source_target_pairs={{0,16},{1,49},{16,32},{17,1},{32,48},{33,17},{48,0},{49,33},{2,18}... | collective-permute-start | bytes 1572872 | tf_op jit(solution)/shard_map/ppermute | solution.py:28
  21.2 4.7 %collective-permute-done.2.refs_0_ = bf16[256,1024]{1,0:T(8,128)(2,1)S(1)} collective-permute-done((bf16[256,1024]{1,0:T(8,128)(2,1)S(1)}, bf16[256,1024]{1,0:T(8,128)(2,1)S(1)}, u32[]{:S(2)}, u32[]{:S(2)}) %collective-permute-start.2) | collective-permute-done | bytes 524320 | tf_op jit(solution)/shard_map/ppermute | solution.py:32
  26.5 0.9 %shard_map.58.refs_2_ = bf16[1792,1024]{1,0:T(8,128)(2,1)S(1)} custom-call(s32[128]{0:T(128)S(1)} %copy-done.3, bf16[256,1024]{1,0:T(8,128)(2,1)S(1)} %collective-permute-done.2.refs_0_, bf16[1792,1024]{1,0:T(8,128)(2,1)S(1)} %shard_map.57.refs_1_), custom_call_target="tpu_custom_call", output_to_operand_aliasing={{}: (2, {})} | custom-call | flops 5000000000 | tf_op jit(solution)/shard_map/pallas_call | solution.py:185
  27.4 3.5 %collective-permute-done.8.refs_3_ = bf16[256,1792]{1,0:T(8,128)(2,1)S(1)} collective-permute-done((bf16[256,1792]{1,0:T(8,128)(2,1)S(1)}, bf16[256,1792]{1,0:T(8,128)(2,1)S(1)}, u32[]{:S(2)}, u32[]{:S(2)}) %collective-permute-start.8) | collective-permute-done | bytes 917536 | tf_op jit(solution)/shard_map/ppermute | solution.py:28
  30.9 1.9 %collective-permute-start.14 = (bf16[256,1024]{1,0:T(8,128)(2,1)S(1)}, bf16[256,1024]{1,0:T(8,128)(2,1)S(1)}, u32[]{:S(2)}, u32[]{:S(2)}) collective-permute-start(bf16[256,1024]{1,0:T(8,128)(2,1)S(1)} %collective-permute-done.11.refs_0_), channel_id=1, source_target_pairs={{0,16},{1,49},{16,32},{17,1},{32,48},{33,17},{48,0},{49,33},{2,18}... | collective-permute-start | bytes 1572872 | tf_op jit(solution)/shard_map/ppermute | solution.py:28
  32.9 1.4 %collective-permute-done.5.refs_1_ = bf16[256,1024]{1,0:T(8,128)(2,1)S(1)} collective-permute-done((bf16[256,1024]{1,0:T(8,128)(2,1)S(1)}, bf16[256,1024]{1,0:T(8,128)(2,1)S(1)}, u32[]{:S(2)}, u32[]{:S(2)}) %collective-permute-start.5) | collective-permute-done | bytes 524320 | tf_op jit(solution)/shard_map/ppermute | solution.py:28
  34.3 2.1 %collective-permute-start.7 = (bf16[256,1024]{1,0:T(8,128)(2,1)S(1)}, bf16[256,1024]{1,0:T(8,128)(2,1)S(1)}, u32[]{:S(2)}, u32[]{:S(2)}) collective-permute-start(bf16[256,1024]{1,0:T(8,128)(2,1)S(1)} %collective-permute-done.5.refs_1_), channel_id=1, source_target_pairs={{0,16},{1,49},{16,32},{17,1},{32,48},{33,17},{48,0},{49,33},{2,18}... | collective-permute-start | bytes 1572872 | tf_op jit(solution)/shard_map/ppermute | solution.py:28
  36.4 7.5 %collective-permute-done.10.refs_0_ = bf16[256,1792]{1,0:T(8,128)(2,1)S(1)} collective-permute-done((bf16[256,1792]{1,0:T(8,128)(2,1)S(1)}, bf16[256,1792]{1,0:T(8,128)(2,1)S(1)}, u32[]{:S(2)}, u32[]{:S(2)}) %collective-permute-start.10) | collective-permute-done | bytes 917536 | tf_op jit(solution)/shard_map/ppermute | solution.py:32
  43.9 1.3 %shard_map.59.refs_2_ = bf16[1792,1024]{1,0:T(8,128)(2,1)S(1)} custom-call(s32[128]{0:T(128)S(1)} %copy-done.3, bf16[256,1024]{1,0:T(8,128)(2,1)S(1)} %collective-permute-done.11.refs_0_, bf16[256,1024]{1,0:T(8,128)(2,1)S(1)} %collective-permute-done.5.refs_1_, bf16[1792,1024]{1,0:T(8,128)(2,1)S(1)} %shard_map.58.refs_2_), custom_call_target="tpu_custom_call", output_to_operand_aliasing={{}: (3, {})} | custom-call | flops 5000000000 | tf_op jit(solution)/shard_map/pallas_call | solution.py:185
  45.8 1.1 %collective-permute-start.19 = (bf16[256,1792]{1,0:T(8,128)(2,1)S(1)}, bf16[256,1792]{1,0:T(8,128)(2,1)S(1)}, u32[]{:S(2)}, u32[]{:S(2)}) collective-permute-start(bf16[256,1792]{1,0:T(8,128)(2,1)S(1)} %collective-permute-done.9.refs_0_), channel_id=1, source_target_pairs={{0,8},{8,0},{1,9},{9,1},{2,10},{10,2},{3,11},{11,3},{4,12},{12,4},... | collective-permute-start | bytes 2752520 | tf_op jit(solution)/shard_map/ppermute | solution.py:32
  46.9 1.9 %collective-permute-start.12 = (bf16[256,1024]{1,0:T(8,128)(2,1)S(1)}, bf16[256,1024]{1,0:T(8,128)(2,1)S(1)}, u32[]{:S(2)}, u32[]{:S(2)}) collective-permute-start(bf16[256,1024]{1,0:T(8,128)(2,1)S(1)} %collective-permute-done.7.refs_1_), channel_id=1, source_target_pairs={{0,16},{1,49},{16,32},{17,1},{32,48},{33,17},{48,0},{49,33},{2,18}... | collective-permute-start | bytes 1572872 | tf_op jit(solution)/shard_map/ppermute | solution.py:28
  48.8 1.3 %shard_map.60.refs_1_.rho_ref = bf16[1792,1024]{1,0:T(8,128)(2,1)S(1)} custom-call(s32[128]{0:T(128)S(1)} %copy-done.3, bf16[256,1024]{1,0:T(8,128)(2,1)S(1)} %collective-permute-done.14.refs_0_, bf16[256,1024]{1,0:T(8,128)(2,1)S(1)} %collective-permute-done.7.refs_1_, bf16[1792,1024]{1,0:T(8,128)(2,1)S(1)} %shard_map.59.refs_2_), custom_call_target="tpu_custom_call", output_to_operand_aliasing={{}: (3, {})} | custom-call | flops 5000000000 | tf_op jit(solution)/shard_map/pallas_call | solution.py:185
  50.1 1.1 %collective-permute-start.18 = (bf16[256,1792]{1,0:T(8,128)(2,1)S(1)}, bf16[256,1792]{1,0:T(8,128)(2,1)S(1)}, u32[]{:S(2)}, u32[]{:S(2)}) collective-permute-start(bf16[256,1792]{1,0:T(8,128)(2,1)S(1)} %collective-permute-done.10.refs_0_), channel_id=1, source_target_pairs={{0,2},{1,7},{2,4},{3,1},{4,6},{5,3},{6,0},{7,5},{8,10},{9,15},{10,... | collective-permute-start | bytes 2752520 | tf_op jit(solution)/shard_map/ppermute | solution.py:28
  51.2 1.1 %collective-permute-start.22 = (bf16[256,1792]{1,0:T(8,128)(2,1)S(1)}, bf16[256,1792]{1,0:T(8,128)(2,1)S(1)}, u32[]{:S(2)}, u32[]{:S(2)}) collective-permute-start(bf16[256,1792]{1,0:T(8,128)(2,1)S(1)} %collective-permute-done.15.refs_1_), channel_id=1, source_target_pairs={{0,2},{1,7},{2,4},{3,1},{4,6},{5,3},{6,0},{7,5},{8,10},{9,15},{10,... | collective-permute-start | bytes 2752520 | tf_op jit(solution)/shard_map/ppermute | solution.py:28
  52.3 4.0 %shard_map.62.sum_ref = f32[4,256,1024]{2,1,0:T(8,128)S(1)} custom-call(bf16[1792,1024]{1,0:T(8,128)(2,1)S(1)} %shard_map.60.refs_1_.rho_ref, bf16[256,1792]{1,0:T(8,128)(2,1)S(1)} %get-tuple-element.251.refs_0_, bf16[256,1792]{1,0:T(8,128)(2,1)S(1)} %collective-permute-done.3.refs_1_, bf16[256,1792]{1,0:T(8,128)(2,1)S(1)} %collective-permute-done.6.refs_2_, ...), custom_call_target="tpu_custom_call" | custom-call | flops 3758096384 | tf_op jit(solution)/shard_map/pallas_call | solution.py:262
  56.3 3.0 %shard_map.63.refs_4_ = bf16[4096,1024]{1,0:T(8,128)(2,1)} custom-call(s32[128]{0:T(128)S(1)} %copy-done.3, bf16[256,1024]{1,0:T(8,128)(2,1)S(1)} %collective-permute-done.12.refs_0_.panel_ref, f32[4,256,1024]{2,1,0:T(8,128)S(1)} %shard_map.62.sum_ref, bf16[256,1792]{1,0:T(8,128)(2,1)S(1)} %get-tuple-element.251.refs_0_, ...), custom_call_target="tpu_custom_call" | custom-call | tf_op jit(solution)/shard_map/pallas_call | solution.py:314
  59.3 1.0 %shard_map.61.rho_ref = bf16[1792,1024]{1,0:T(8,128)(2,1)S(1)} custom-call(s32[128]{0:T(128)S(1)} %copy-done.3, bf16[256,1024]{1,0:T(8,128)(2,1)S(1)} %collective-permute-done.12.refs_0_.panel_ref, bf16[1792,1024]{1,0:T(8,128)(2,1)S(1)} %shard_map.60.refs_1_.rho_ref), custom_call_target="tpu_custom_call", output_to_operand_aliasing={{}: (2, {})} | custom-call | flops 5000000000 | tf_op jit(solution)/shard_map/pallas_call | solution.py:185
  60.3 5.2 %shard_map.64 = (bf16[4096,1024]{1,0:T(8,128)(2,1)}, s32[8,128]{1,0:T(8,128)S(1)}) custom-call(s32[8,128]{1,0:T(8,128)S(1)} %get-tuple-element.249.live_ref, bf16[1792,1024]{1,0:T(8,128)(2,1)S(1)} %shard_map.61.rho_ref, bf16[256,1792]{1,0:T(8,128)(2,1)S(1)} %collective-permute-done.10.refs_0_, ...), custom_call_target="tpu_custom_call", output_to_operand_aliasing={{0}: (6, {})} | custom-call | tf_op jit(solution)/shard_map/pallas_call | solution.py:231
  65.5 2.2 %collective-permute-done.19.refs_3_ = bf16[256,1792]{1,0:T(8,128)(2,1)S(1)} collective-permute-done((bf16[256,1792]{1,0:T(8,128)(2,1)S(1)}, bf16[256,1792]{1,0:T(8,128)(2,1)S(1)}, u32[]{:S(2)}, u32[]{:S(2)}) %collective-permute-start.19) | collective-permute-done | bytes 917536 | tf_op jit(solution)/shard_map/ppermute | solution.py:32
  67.7 0.9 %collective-permute-start.21 = (bf16[256,1792]{1,0:T(8,128)(2,1)S(1)}, bf16[256,1792]{1,0:T(8,128)(2,1)S(1)}, u32[]{:S(2)}, u32[]{:S(2)}) collective-permute-start(bf16[256,1792]{1,0:T(8,128)(2,1)S(1)} %collective-permute-done.19.refs_3_), channel_id=1, source_target_pairs={{0,1},{1,0},{2,3},{3,2},{4,5},{5,4},{6,7},{7,6},{8,9},{9,8},{10,11... | collective-permute-start | bytes 2752520 | tf_op jit(solution)/shard_map/ppermute | solution.py:32
  68.6 5.2 %shard_map.65 = (bf16[4096,1024]{1,0:T(8,128)(2,1)}, s32[8,128]{1,0:T(8,128)S(1)}) custom-call(s32[8,128]{1,0:T(8,128)S(1)} %get-tuple-element.268.live_ref, bf16[1792,1024]{1,0:T(8,128)(2,1)S(1)} %shard_map.61.rho_ref, bf16[256,1792]{1,0:T(8,128)(2,1)S(1)} %collective-permute-done.9.refs_0_, ...), custom_call_target="tpu_custom_call", output_to_operand_aliasing={{0}: (6, {})} | custom-call | flops 3758096384 | bytes 2097152 | tf_op jit(solution)/shard_map/pallas_call | solution.py:231
  73.8 0.8 collective-permute-start.23
  74.6 4.1 %shard_map.66 = (bf16[4096,1024]{1,0:T(8,128)(2,1)}, s32[8,128]{1,0:T(8,128)S(1)}) custom-call(s32[8,128]{1,0:T(8,128)S(1)} %get-tuple-element.273.live_ref, bf16[1792,1024]{1,0:T(8,128)(2,1)S(1)} %shard_map.61.rho_ref, bf16[256,1792]{1,0:T(8,128)(2,1)S(1)} %collective-permute-done.20.refs_0_, ...), custom_call_target="tpu_custom_call", output_to_operand_aliasing={{0}: (5, {})} | custom-call | flops 2818572288 | bytes 1572864 | tf_op jit(solution)/shard_map/pallas_call | solution.py:231
  78.7 2.0 %shard_map.67 = (bf16[4096,1024]{1,0:T(8,128)(2,1)}, s32[8,128]{1,0:T(8,128)S(1)}) custom-call(s32[8,128]{1,0:T(8,128)S(1)} %get-tuple-element.278.live_ref, bf16[1792,1024]{1,0:T(8,128)(2,1)S(1)} %shard_map.61.rho_ref, bf16[256,1792]{1,0:T(8,128)(2,1)S(1)} %collective-permute-done.23.refs_0_, ...), custom_call_target="tpu_custom_call", output_to_operand_aliasing={{0}: (3, {})} | custom-call | flops 939524096 | bytes 524288 | tf_op jit(solution)/shard_map/pallas_call | solution.py:231
  (36 shorter events, 3.0 us)
Async XLA Ops:
  0.0 0.7 copy-start
  0.7 12.9 %copy-start.3 = (s32[128]{0:T(128)S(1)}, s32[128]{0:T(128)}, u32[]{:S(2)}) copy-start(s32[128]{0:T(128)} %sizes_hbm.9) | copy-start | bytes 1540
  2.9 12.1 %collective-permute-start.3 = (bf16[256,1792]{1,0:T(8,128)(2,1)S(1)}, bf16[256,1792]{1,0:T(8,128)(2,1)S(1)}, u32[]{:S(2)}, u32[]{:S(2)}) collective-permute-start(bf16[256,1792]{1,0:T(8,128)(2,1)S(1)} %get-tuple-element.251.refs_0_), channel_id=1, source_target_pairs={{0,1},{1,0},{2,3},{3,2},{4,5},{5,4},{6,7},{7,6},{8,9},{9,8},{10,11... | collective-permute-start | bytes 2752520 | tf_op jit(solution)/shard_map/ppermute | solution.py:32
  4.4 10.6 %collective-permute-start.4 = (bf16[256,1024]{1,0:T(8,128)(2,1)S(1)}, bf16[256,1024]{1,0:T(8,128)(2,1)S(1)}, u32[]{:S(2)}, u32[]{:S(2)}) collective-permute-start(bf16[256,1024]{1,0:T(8,128)(2,1)S(1)} %get-tuple-element.250.refs_0_), channel_id=1, source_target_pairs={{0,16},{1,49},{16,32},{17,1},{32,48},{33,17},{48,0},{49,33},{2,18}... | collective-permute-start | bytes 1572872 | tf_op jit(solution)/shard_map/ppermute | solution.py:28
  8.3 13.0 %collective-permute-start.6 = (bf16[256,1792]{1,0:T(8,128)(2,1)S(1)}, bf16[256,1792]{1,0:T(8,128)(2,1)S(1)}, u32[]{:S(2)}, u32[]{:S(2)}) collective-permute-start(bf16[256,1792]{1,0:T(8,128)(2,1)S(1)} %get-tuple-element.251.refs_0_), channel_id=1, source_target_pairs={{0,2},{1,7},{2,4},{3,1},{4,6},{5,3},{6,0},{7,5},{8,10},{9,15},{10,... | collective-permute-start | bytes 2752520 | tf_op jit(solution)/shard_map/ppermute | solution.py:28
  10.7 15.2 %collective-permute-start.2 = (bf16[256,1024]{1,0:T(8,128)(2,1)S(1)}, bf16[256,1024]{1,0:T(8,128)(2,1)S(1)}, u32[]{:S(2)}, u32[]{:S(2)}) collective-permute-start(bf16[256,1024]{1,0:T(8,128)(2,1)S(1)} %get-tuple-element.250.refs_0_), channel_id=1, source_target_pairs={{0,64},{64,0},{1,65},{65,1},{2,66},{66,2},{3,67},{67,3},{4,68},{68... | collective-permute-start | bytes 1572872 | tf_op jit(solution)/shard_map/ppermute | solution.py:32
  14.5 29.4 %collective-permute-start.10 = (bf16[256,1792]{1,0:T(8,128)(2,1)S(1)}, bf16[256,1792]{1,0:T(8,128)(2,1)S(1)}, u32[]{:S(2)}, u32[]{:S(2)}) collective-permute-start(bf16[256,1792]{1,0:T(8,128)(2,1)S(1)} %get-tuple-element.251.refs_0_), channel_id=1, source_target_pairs={{0,8},{8,0},{1,9},{9,1},{2,10},{10,2},{3,11},{11,3},{4,12},{12,4},... | collective-permute-start | bytes 2752520 | tf_op jit(solution)/shard_map/ppermute | solution.py:32
  15.0 15.9 %collective-permute-start.8 = (bf16[256,1792]{1,0:T(8,128)(2,1)S(1)}, bf16[256,1792]{1,0:T(8,128)(2,1)S(1)}, u32[]{:S(2)}, u32[]{:S(2)}) collective-permute-start(bf16[256,1792]{1,0:T(8,128)(2,1)S(1)} %collective-permute-done.3.refs_1_), channel_id=1, source_target_pairs={{0,2},{1,7},{2,4},{3,1},{4,6},{5,3},{6,0},{7,5},{8,10},{9,15},{10,... | collective-permute-start | bytes 2752520 | tf_op jit(solution)/shard_map/ppermute | solution.py:28
  17.8 13.2 %collective-permute-start.11 = (bf16[256,1024]{1,0:T(8,128)(2,1)S(1)}, bf16[256,1024]{1,0:T(8,128)(2,1)S(1)}, u32[]{:S(2)}, u32[]{:S(2)}) collective-permute-start(bf16[256,1024]{1,0:T(8,128)(2,1)S(1)} %collective-permute-done.4.refs_0_), channel_id=1, source_target_pairs={{0,16},{1,49},{16,32},{17,1},{32,48},{33,17},{48,0},{49,33},{2,18}... | collective-permute-start | bytes 1572872 | tf_op jit(solution)/shard_map/ppermute | solution.py:28
  26.0 8.3 %collective-permute-start.5 = (bf16[256,1024]{1,0:T(8,128)(2,1)S(1)}, bf16[256,1024]{1,0:T(8,128)(2,1)S(1)}, u32[]{:S(2)}, u32[]{:S(2)}) collective-permute-start(bf16[256,1024]{1,0:T(8,128)(2,1)S(1)} %collective-permute-done.2.refs_0_), channel_id=1, source_target_pairs={{0,16},{1,49},{16,32},{17,1},{32,48},{33,17},{48,0},{49,33},{2,18}... | collective-permute-start | bytes 1572872 | tf_op jit(solution)/shard_map/ppermute | solution.py:28
  26.0 17.9 %collective-permute-start.9 = (bf16[256,1792]{1,0:T(8,128)(2,1)S(1)}, bf16[256,1792]{1,0:T(8,128)(2,1)S(1)}, u32[]{:S(2)}, u32[]{:S(2)}) collective-permute-start(bf16[256,1792]{1,0:T(8,128)(2,1)S(1)} %collective-permute-done.6.refs_2_), channel_id=1, source_target_pairs={{0,2},{1,7},{2,4},{3,1},{4,6},{5,3},{6,0},{7,5},{8,10},{9,15},{10,... | collective-permute-start | bytes 2752520 | tf_op jit(solution)/shard_map/ppermute | solution.py:28
  30.9 14.3 %collective-permute-start.13 = (bf16[256,1792]{1,0:T(8,128)(2,1)S(1)}, bf16[256,1792]{1,0:T(8,128)(2,1)S(1)}, u32[]{:S(2)}, u32[]{:S(2)}) collective-permute-start(bf16[256,1792]{1,0:T(8,128)(2,1)S(1)} %collective-permute-done.6.refs_2_), channel_id=1, source_target_pairs={{0,1},{1,0},{2,3},{3,2},{4,5},{5,4},{6,7},{7,6},{8,9},{9,8},{10,11... | collective-permute-start | bytes 2752520 | tf_op jit(solution)/shard_map/ppermute | solution.py:32
  30.9 14.3 %collective-permute-start.14 = (bf16[256,1024]{1,0:T(8,128)(2,1)S(1)}, bf16[256,1024]{1,0:T(8,128)(2,1)S(1)}, u32[]{:S(2)}, u32[]{:S(2)}) collective-permute-start(bf16[256,1024]{1,0:T(8,128)(2,1)S(1)} %collective-permute-done.11.refs_0_), channel_id=1, source_target_pairs={{0,16},{1,49},{16,32},{17,1},{32,48},{33,17},{48,0},{49,33},{2,18}... | collective-permute-start | bytes 1572872 | tf_op jit(solution)/shard_map/ppermute | solution.py:28
  34.3 12.6 %collective-permute-start.7 = (bf16[256,1024]{1,0:T(8,128)(2,1)S(1)}, bf16[256,1024]{1,0:T(8,128)(2,1)S(1)}, u32[]{:S(2)}, u32[]{:S(2)}) collective-permute-start(bf16[256,1024]{1,0:T(8,128)(2,1)S(1)} %collective-permute-done.5.refs_1_), channel_id=1, source_target_pairs={{0,16},{1,49},{16,32},{17,1},{32,48},{33,17},{48,0},{49,33},{2,18}... | collective-permute-start | bytes 1572872 | tf_op jit(solution)/shard_map/ppermute | solution.py:28
  45.2 6.0 %collective-permute-start.16 = (bf16[256,1792]{1,0:T(8,128)(2,1)S(1)}, bf16[256,1792]{1,0:T(8,128)(2,1)S(1)}, u32[]{:S(2)}, u32[]{:S(2)}) collective-permute-start(bf16[256,1792]{1,0:T(8,128)(2,1)S(1)} %collective-permute-done.8.refs_3_), channel_id=1, source_target_pairs={{0,1},{1,0},{2,3},{3,2},{4,5},{5,4},{6,7},{7,6},{8,9},{9,8},{10,11... | collective-permute-start | bytes 2752520 | tf_op jit(solution)/shard_map/ppermute | solution.py:32
  45.3 5.9 %collective-permute-start.15 = (bf16[256,1792]{1,0:T(8,128)(2,1)S(1)}, bf16[256,1792]{1,0:T(8,128)(2,1)S(1)}, u32[]{:S(2)}, u32[]{:S(2)}) collective-permute-start(bf16[256,1792]{1,0:T(8,128)(2,1)S(1)} %collective-permute-done.10.refs_0_), channel_id=1, source_target_pairs={{0,1},{1,0},{2,3},{3,2},{4,5},{5,4},{6,7},{7,6},{8,9},{9,8},{10,11... | collective-permute-start | bytes 2752520 | tf_op jit(solution)/shard_map/ppermute | solution.py:32
  45.8 21.9 %collective-permute-start.19 = (bf16[256,1792]{1,0:T(8,128)(2,1)S(1)}, bf16[256,1792]{1,0:T(8,128)(2,1)S(1)}, u32[]{:S(2)}, u32[]{:S(2)}) collective-permute-start(bf16[256,1792]{1,0:T(8,128)(2,1)S(1)} %collective-permute-done.9.refs_0_), channel_id=1, source_target_pairs={{0,8},{8,0},{1,9},{9,1},{2,10},{10,2},{3,11},{11,3},{4,12},{12,4},... | collective-permute-start | bytes 2752520 | tf_op jit(solution)/shard_map/ppermute | solution.py:32
  46.9 9.4 %collective-permute-start.12 = (bf16[256,1024]{1,0:T(8,128)(2,1)S(1)}, bf16[256,1024]{1,0:T(8,128)(2,1)S(1)}, u32[]{:S(2)}, u32[]{:S(2)}) collective-permute-start(bf16[256,1024]{1,0:T(8,128)(2,1)S(1)} %collective-permute-done.7.refs_1_), channel_id=1, source_target_pairs={{0,16},{1,49},{16,32},{17,1},{32,48},{33,17},{48,0},{49,33},{2,18}... | collective-permute-start | bytes 1572872 | tf_op jit(solution)/shard_map/ppermute | solution.py:28
  50.1 18.5 %collective-permute-start.18 = (bf16[256,1792]{1,0:T(8,128)(2,1)S(1)}, bf16[256,1792]{1,0:T(8,128)(2,1)S(1)}, u32[]{:S(2)}, u32[]{:S(2)}) collective-permute-start(bf16[256,1792]{1,0:T(8,128)(2,1)S(1)} %collective-permute-done.10.refs_0_), channel_id=1, source_target_pairs={{0,2},{1,7},{2,4},{3,1},{4,6},{5,3},{6,0},{7,5},{8,10},{9,15},{10,... | collective-permute-start | bytes 2752520 | tf_op jit(solution)/shard_map/ppermute | solution.py:28
  51.2 17.4 %collective-permute-start.17 = (bf16[256,1792]{1,0:T(8,128)(2,1)S(1)}, bf16[256,1792]{1,0:T(8,128)(2,1)S(1)}, u32[]{:S(2)}, u32[]{:S(2)}) collective-permute-start(bf16[256,1792]{1,0:T(8,128)(2,1)S(1)} %collective-permute-done.9.refs_0_), channel_id=1, source_target_pairs={{0,1},{1,0},{2,3},{3,2},{4,5},{5,4},{6,7},{7,6},{8,9},{9,8},{10,11... | collective-permute-start | bytes 2752520 | tf_op jit(solution)/shard_map/ppermute | solution.py:32
  51.2 22.6 %collective-permute-start.22 = (bf16[256,1792]{1,0:T(8,128)(2,1)S(1)}, bf16[256,1792]{1,0:T(8,128)(2,1)S(1)}, u32[]{:S(2)}, u32[]{:S(2)}) collective-permute-start(bf16[256,1792]{1,0:T(8,128)(2,1)S(1)} %collective-permute-done.15.refs_1_), channel_id=1, source_target_pairs={{0,2},{1,7},{2,4},{3,1},{4,6},{5,3},{6,0},{7,5},{8,10},{9,15},{10,... | collective-permute-start | bytes 2752520 | tf_op jit(solution)/shard_map/ppermute | solution.py:28
  67.7 6.9 %collective-permute-start.21 = (bf16[256,1792]{1,0:T(8,128)(2,1)S(1)}, bf16[256,1792]{1,0:T(8,128)(2,1)S(1)}, u32[]{:S(2)}, u32[]{:S(2)}) collective-permute-start(bf16[256,1792]{1,0:T(8,128)(2,1)S(1)} %collective-permute-done.19.refs_3_), channel_id=1, source_target_pairs={{0,1},{1,0},{2,3},{3,2},{4,5},{5,4},{6,7},{7,6},{8,9},{9,8},{10,11... | collective-permute-start | bytes 2752520 | tf_op jit(solution)/shard_map/ppermute | solution.py:32
  68.6 6.0 %collective-permute-start.20 = (bf16[256,1792]{1,0:T(8,128)(2,1)S(1)}, bf16[256,1792]{1,0:T(8,128)(2,1)S(1)}, u32[]{:S(2)}, u32[]{:S(2)}) collective-permute-start(bf16[256,1792]{1,0:T(8,128)(2,1)S(1)} %collective-permute-done.18.refs_2_), channel_id=1, source_target_pairs={{0,1},{1,0},{2,3},{3,2},{4,5},{5,4},{6,7},{7,6},{8,9},{9,8},{10,11... | collective-permute-start | bytes 2752520 | tf_op jit(solution)/shard_map/ppermute | solution.py:32
  73.8 4.9 %collective-permute-start.23 = (bf16[256,1792]{1,0:T(8,128)(2,1)S(1)}, bf16[256,1792]{1,0:T(8,128)(2,1)S(1)}, u32[]{:S(2)}, u32[]{:S(2)}) collective-permute-start(bf16[256,1792]{1,0:T(8,128)(2,1)S(1)} %collective-permute-done.22.refs_2_), channel_id=1, source_target_pairs={{0,1},{1,0},{2,3},{3,2},{4,5},{5,4},{6,7},{7,6},{8,9},{9,8},{10,11... | collective-permute-start | bytes 2752520 | tf_op jit(solution)/shard_map/ppermute | solution.py:32
  78.7 2.5 %copy-start.1 = (s32[32,16]{0,1:T(8,128)S(1)}, s32[32,16]{0,1:T(8,128)}, u32[]{:S(2)}) copy-start(s32[32,16]{0,1:T(8,128)} %param.13) | copy-start | bytes 6148
  78.7 3.1 %copy-start.2 = (bf16[1,256,2048]{2,1,0:T(8,128)(2,1)S(1)}, bf16[1,256,2048]{2,1,0:T(8,128)(2,1)}, u32[]{:S(2)}) copy-start(bf16[1,256,2048]{2,1,0:T(8,128)(2,1)} %tensor_hbm.1) | copy-start | bytes 3145732
